TPU v7x, 512 devices: a whole 4x4x16 slice. The times are simulated.
512 devices in a mesh: gx: 16 (over z), gy: 8 (over x, core), gz: 4 (over y).
Axes of the slice: x: 4, y: 4, z: 16, core: 2. Of those that a mesh axis runs over, the one named last changes fastest.
Arguments:
- state: float32 [4, 128, 64, 512], P(None, 'gx', 'gy', 'gz'), may hold values from -6 to 6
- sample_cell: int32 [524288], P(('gx', 'gy', 'gz')), may hold values from 0 to 8191
- sample_dest: int32 [524288, 1], P(('gx', 'gy', 'gz')), may hold values from 0 to 63; in each aligned block of 1024 rows (0 to 1023, 1024 to 2047, ...) at most 32 rows name the same one
- sample_weight: float32 [524288], P(('gx', 'gy', 'gz')), may hold values from 0.05 to 0.5
- sample_elem: int32 [524288], P(('gx', 'gy', 'gz')), may hold values from 0 to 127
- element_motion: float32 [3, 8192], P(None, ('gx', 'gz')), may hold values from -6 to 6
- element_coef: float32 [8192], P(('gx', 'gz')), may hold values from 0.01 to 0.1
Outputs:
- new_state: float32 [4, 128, 64, 512], P(None, 'gx', 'gy', 'gz')
- body_force: float32 [3, 128, 64, 512], P(None, 'gx', 'gy', 'gz')
Inputs may be any that keep to these rules, and one draw needn't show every extreme that they name: `sample_dest`: in the 1024 rows of one device no turbine-section device is named more than 32 times; some device names one exactly 32 times.
All inputs are finite; a program needn't handle non-finite values.
Results may differ from a plain program's by a relative error of at most 0.00012.
Values sent between devices are 32-bit elements; how exact they have to be, the bound alone decides.
No kernel may reach another device: no remote copies, remote signals or barrier semaphores. Data moves between devices by JAX's collectives and lax.ppermute only.
A program may use at most 64 MiB of HBM per device.

v0:
```python
import math

import jax
import jax.numpy as jnp
from jax import lax
from jax.sharding import PartitionSpec as P

DT_STEP = 0.4
BASE_COEF = 0.02
PRANDTL = 0.7
SMAG_COEF = 0.04


def with_halo(block, sides, width):
    for axis, dim in sides:
        count = lax.axis_size(axis)
        forward = [(i, i + 1) for i in range(count - 1)]
        forward.append((count - 1, 0))
        backward = [(target, source) for source, target in forward]
        low = lax.ppermute(
            lax.slice_in_dim(block, block.shape[dim] - width, None, axis=dim), axis, forward
        )
        high = lax.ppermute(lax.slice_in_dim(block, 0, width, axis=dim), axis, backward)
        block = jnp.concatenate([low, block, high], axis=dim)
    return block


def shifted(padded, axis, offset):
    lead = padded.ndim - 3
    parts = [slice(None)] * lead + [slice(1, -1)] * 3
    length = padded.shape[lead + axis]
    parts[lead + axis] = slice(1 + offset, length - 1 + offset)
    return padded[tuple(parts)]


def eddy(padded):
    grads = [
        [0.5 * (shifted(padded[c], j, 1) - shifted(padded[c], j, -1)) for j in range(3)]
        for c in range(3)
    ]
    strain = 0.0
    for c in range(3):
        for j in range(3):
            paired = 0.5 * (grads[c][j] + grads[j][c])
            strain = strain + paired * paired
    return SMAG_COEF * jnp.sqrt(2.0 * strain)


def advance(padded, viscous, force):
    centre_visc = shifted(viscous, 0, 0)
    result = []
    for c in range(4):
        values = padded[c]
        middle = shifted(values, 0, 0)
        ratio = 1.0 if c < 3 else 1.0 / PRANDTL
        change = jnp.zeros_like(middle)
        for j in range(3):
            upper = shifted(values, j, 1)
            lower = shifted(values, j, -1)
            upper_coef = BASE_COEF + ratio * 0.5 * (centre_visc + shifted(viscous, j, 1))
            lower_coef = BASE_COEF + ratio * 0.5 * (centre_visc + shifted(viscous, j, -1))
            change = change + upper_coef * (upper - middle) - lower_coef * (middle - lower)
            change = change - shifted(padded[j], 0, 0) * 0.5 * (upper - lower)
        if c < 3:
            change = change + force[c]
        result.append(middle + DT_STEP * change)
    return jnp.stack(result)


def routed_forces(
    sampled, sample_dest, sample_weight, sample_elem, element_motion, element_coef, peers
):
    count = sampled.shape[1]
    capacity = 2 * count // peers
    target = sample_dest[:, 0]
    onehot = (target[:, None] == jnp.arange(peers, dtype=jnp.int32)[None, :]).astype(jnp.int32)
    ranks = jnp.sum(jnp.cumsum(onehot, axis=0) * onehot, axis=1) - 1
    position = target * capacity + ranks
    send_rows = (
        jnp.zeros((3, peers * capacity), jnp.float32)
        .at[:, position]
        .set(sampled)
        .reshape(3, peers, capacity)
    )
    send_ids = (
        jnp.zeros((peers * capacity,), jnp.int32)
        .at[position]
        .set(sample_elem)
        .reshape(1, peers, capacity)
    )
    arrived_rows, arrived_ids = (
        lax.all_to_all(send_rows, ("gx", "gz"), split_axis=1, concat_axis=1, tiled=True),
        lax.all_to_all(send_ids, ("gx", "gz"), split_axis=1, concat_axis=1, tiled=True),
    )
    elements = element_coef.shape[0]
    flat_rows = arrived_rows.reshape(3, -1)
    flat_ids = arrived_ids.reshape(-1)
    total = flat_ids.shape[0]
    block = math.gcd(total, 2048)
    blocks = total // block
    columns = jnp.arange(elements, dtype=jnp.int32)

    def table():
        return (flat_ids[:, None] == columns[None, :]).astype(jnp.float32)

    def gather_sum(step, running):
        return running + jnp.dot(flat_rows, table(), precision=lax.Precision.HIGHEST)

    partial_sum = lax.fori_loop(0, blocks, gather_sum, jnp.zeros((3, elements), jnp.float32))
    point_velocity = lax.psum(partial_sum, "gy")
    relative = point_velocity + element_motion
    speed = jnp.sqrt(jnp.sum(relative * relative, axis=0))
    element_force = -element_coef * speed * relative

    def spread_back(step, filled):
        piece = jnp.dot(element_force, table().T, precision=lax.Precision.HIGHEST)
        return piece

    returned = lax.fori_loop(0, blocks, spread_back, jnp.zeros((3, total), jnp.float32)).reshape(
        3, peers, capacity
    )
    back_rows = lax.all_to_all(returned, ("gx", "gz"), split_axis=1, concat_axis=1, tiled=True)
    return back_rows.reshape(3, -1)[:, position] * sample_weight


def body(state, sample_cell, sample_dest, sample_weight, sample_elem, element_motion, element_coef):
    size_x = lax.axis_size("gx")
    size_z = lax.axis_size("gz")
    peers = size_x * size_z
    velocity = state[:3].reshape(3, -1)
    sampled = velocity[:, sample_cell] * sample_weight
    force_each = routed_forces(
        sampled, sample_dest, sample_weight, sample_elem, element_motion, element_coef, peers
    )
    cells = velocity.shape[1]
    body_force = (
        jnp.zeros((3, cells), jnp.float32)
        .at[:, sample_cell]
        .add(force_each)
        .reshape((3,) + state.shape[1:])
    )
    bottom = lax.axis_index("gz") == 0
    top = lax.axis_index("gz") == size_z - 1

    def walls(padded, width):
        depth = padded.shape[-1]
        level = jnp.arange(depth)
        outside = bottom & (level < width) | top & (level >= depth - width)
        return jnp.where(outside, 0.0, padded)

    padded = walls(with_halo(state, (("gx", 1), ("gy", 2), ("gz", 3)), 1), 1)
    viscous = eddy(padded)
    viscous = walls(with_halo(viscous, (("gx", 0), ("gy", 1), ("gz", 2)), 1), 1)
    new_state = advance(padded, viscous, body_force)
    return (new_state, body_force)


def solution(mesh):
    return jax.shard_map(
        body,
        mesh=mesh,
        in_specs=(
            P(None, "gx", "gy", "gz"),
            P(("gx", "gy", "gz")),
            P(("gx", "gy", "gz"), None),
            P(("gx", "gy", "gz")),
            P(("gx", "gy", "gz")),
            P(None, ("gx", "gz")),
            P(("gx", "gz")),
        ),
        out_specs=(P(None, "gx", "gy", "gz"), P(None, "gx", "gy", "gz")),
        check_vma=False,
    )
```

profile of v0, /device:TPU:1, one launch (start us, length us, event | category | flops | bytes accessed | tf_op | source)
XLA Modules:
  0.0 190.6 jit_solution(16754115630089105396)
XLA Ops:
  0.6 0.7 fusion.32
  1.4 4.5 %collective-permute-start = (f32[4,1,8,128]{3,2,1,0:T(8,128)S(1)}, f32[4,1,8,128]{3,2,1,0:T(8,128)S(1)}, u32[]{:S(2)}, u32[]{:S(2)}) collective-permute-start(f32[4,1,8,128]{3,2,1,0:T(8,128)S(1)} %get-tuple-element.60), channel_id=1, source_target_pairs={{0,32},{32,64},{64,96},{96,128},{128,160},{160,192},{192,224},{224... | collective-permute-start | bytes 49160 | tf_op jit(solution)/shard_map/ppermute | solution.py:20
  5.9 9.5 %collective-permute-start.1 = (f32[4,1,8,128]{3,2,1,0:T(8,128)S(1)}, f32[4,1,8,128]{3,2,1,0:T(8,128)S(1)}, u32[]{:S(2)}, u32[]{:S(2)}) collective-permute-start(f32[4,1,8,128]{3,2,1,0:T(8,128)S(1)} %get-tuple-element.59), channel_id=1, source_target_pairs={{32,0},{64,32},{96,64},{128,96},{160,128},{192,160},{224,192},{256... | collective-permute-start | bytes 49160 | tf_op jit(solution)/shard_map/ppermute | solution.py:23
  16.1 18.0 %reduce-window.6 = s32[64,8,128]{2,1,0:T(8,128)S(1)} reduce-window(s32[64,8,128]{2,1,0:T(8,128)S(1)} %fusion.14, s32[]{:T(128)} %constant.18.clone.1), window={size=1x1x128 pad=0_0x0_0x127_0}, to_apply=%region_0.0 | reduce-window | flops 8323072 | bytes 524292 | tf_op jit(solution)/shard_map/reduce-window
  34.7 0.8 fusion.11
  35.4 0.9 constant_dynamic-update-slice_fusion.1
  36.4 1.0 collective-permute-start.3
  37.4 1.1 collective-permute-start.2
  39.2 4.5 %scatter_custom_fusion.1 = s32[2048]{0:T(1024)S(1)} fusion(s32[1024]{0:T(1024)S(1)} %bitcast.73, s32[1024]{0:T(1024)} %param.11, s32[]{:T(128)} %constant.18.clone.1), kind=kCustom, calls=%fused_computation.83 | custom fusion | bytes 8704 | tf_op jit(solution)/shard_map/scatter | solution.py:88
  44.4 12.2 %all-to-all-start.1 = ((s32[1,64,32]{2,0,1:T(1,128)}), s32[1,64,32]{2,0,1:T(1,128)S(1)}, u32[]{:S(2)}, u32[]{:S(2)}) async-start(s32[1,64,32]{2,0,1:T(1,128)} %bitcast.11), calls=%async_computation.1 | async-start | bytes 65536 | tf_op jit(solution)/shard_map/all_to_all | solution.py:93
  56.8 4.1 %collective-permute-start.5 = (f32[4,10,10,1]{3,2,1,0:T(8,128)S(1)}, f32[4,10,10,1]{3,2,1,0:T(8,128)S(1)}, u32[]{:S(2)}, u32[]{:S(2)}) collective-permute-start(f32[4,10,10,1]{3,2,1,0:T(8,128)S(1)} %get-tuple-element.56), channel_id=1, source_target_pairs={{1,0},{2,1},{3,2},{0,3},{5,4},{6,5},{7,6},{4,7},{9,8},{10,9},{11,1... | collective-permute-start | bytes 4808 | tf_op jit(solution)/shard_map/ppermute | solution.py:23
  61.0 1.9 %collective-permute-start.4 = (f32[4,10,10,1]{3,2,1,0:T(8,128)S(1)}, f32[4,10,10,1]{3,2,1,0:T(8,128)S(1)}, u32[]{:S(2)}, u32[]{:S(2)}) collective-permute-start(f32[4,10,10,1]{3,2,1,0:T(8,128)S(1)} %get-tuple-element.55), channel_id=1, source_target_pairs={{0,1},{1,2},{2,3},{3,0},{4,5},{5,6},{6,7},{7,4},{8,9},{9,10},{10,1... | collective-permute-start | bytes 4808 | tf_op jit(solution)/shard_map/ppermute | solution.py:20
  62.9 4.5 %collective-permute-done.5 = f32[4,10,10,1]{3,2,1,0:T(8,128)S(1)} collective-permute-done((f32[4,10,10,1]{3,2,1,0:T(8,128)S(1)}, f32[4,10,10,1]{3,2,1,0:T(8,128)S(1)}, u32[]{:S(2)}, u32[]{:S(2)}) %collective-permute-start.5) | collective-permute-done | bytes 1632 | tf_op jit(solution)/shard_map/ppermute | solution.py:23
  67.4 4.7 %collective-permute-done.4 = f32[4,10,10,1]{3,2,1,0:T(8,128)S(1)} collective-permute-done((f32[4,10,10,1]{3,2,1,0:T(8,128)S(1)}, f32[4,10,10,1]{3,2,1,0:T(8,128)S(1)}, u32[]{:S(2)}, u32[]{:S(2)}) %collective-permute-start.4) | collective-permute-done | bytes 1632 | tf_op jit(solution)/shard_map/ppermute | solution.py:20
  72.9 4.6 %collective-permute-start.7 = (f32[1,8,128]{2,1,0:T(8,128)S(1)}, f32[1,8,128]{2,1,0:T(8,128)S(1)}, u32[]{:S(2)}, u32[]{:S(2)}) collective-permute-start(f32[1,8,128]{2,1,0:T(8,128)S(1)} %get-tuple-element.66), channel_id=1, source_target_pairs={{32,0},{64,32},{96,64},{128,96},{160,128},{192,160},{224,192},{256... | collective-permute-start | bytes 12296 | tf_op jit(solution)/shard_map/ppermute | solution.py:23
  77.5 1.9 %collective-permute-start.6 = (f32[1,8,128]{2,1,0:T(8,128)S(1)}, f32[1,8,128]{2,1,0:T(8,128)S(1)}, u32[]{:S(2)}, u32[]{:S(2)}) collective-permute-start(f32[1,8,128]{2,1,0:T(8,128)S(1)} %get-tuple-element.65), channel_id=1, source_target_pairs={{0,32},{32,64},{64,96},{96,128},{128,160},{160,192},{192,224},{224... | collective-permute-start | bytes 12296 | tf_op jit(solution)/shard_map/ppermute | solution.py:20
  79.4 3.6 %collective-permute-done.6 = f32[1,8,128]{2,1,0:T(8,128)S(1)} collective-permute-done((f32[1,8,128]{2,1,0:T(8,128)S(1)}, f32[1,8,128]{2,1,0:T(8,128)S(1)}, u32[]{:S(2)}, u32[]{:S(2)}) %collective-permute-start.6) | collective-permute-done | bytes 4128 | tf_op jit(solution)/shard_map/ppermute | solution.py:20
  83.1 3.7 %collective-permute-start.9 = (f32[10,1,128]{2,1,0:T(1,128)S(1)}, f32[10,1,128]{2,1,0:T(1,128)S(1)}, u32[]{:S(2)}, u32[]{:S(2)}) collective-permute-start(f32[10,1,128]{2,1,0:T(1,128)S(1)} %get-tuple-element.64), channel_id=1, source_target_pairs={{4,0},{8,4},{12,8},{16,12},{20,16},{24,20},{28,24},{0,28},{5,1},{9... | collective-permute-start | bytes 15368 | tf_op jit(solution)/shard_map/ppermute | solution.py:23
  86.7 1.1 collective-permute-start.8
  87.8 2.6 %copy.27 = f32[3,8,8,128]{0,3,2,1:T(8,128)} copy(f32[3,8,8,128]{3,2,1,0:T(8,128)S(1)} %slice-done) | data formatting | bytes 196608 | tf_op jit(solution)/shard_map/slice | solution.py:130
  90.4 9.6 %scatter_custom_fusion = f32[3,2048]{0,1:T(8,128)S(1)} fusion(s32[1024]{0:T(1024)S(1)} %bitcast.75, f32[]{:T(128)} %constant.22.clone.1, f32[1024]{0:T(1024)S(1)} %copy-done, f32[3,8192]{0,1:T(8,128)} %bitcast.66, s32[1024]{0:T(1024)S(1)} %get-tuple-element.67), kind=kCustom, calls=%fused_computation.15 | custom fusion | flops 3072 | bytes 131076 | tf_op jit(solution)/shard_map/scatter | solution.py:82
  100.0 1.1 copy.28
  101.1 9.8 %all-to-all-start = ((f32[3,64,32]{2,0,1:T(4,128)}), f32[3,64,32]{2,0,1:T(4,128)S(1)}, u32[]{:S(2)}, u32[]{:S(2)}) async-start(f32[3,64,32]{2,0,1:T(4,128)} %copy.28), calls=%async_computation | async-start | bytes 262144 | tf_op jit(solution)/shard_map/all_to_all | solution.py:92
  112.4 4.1 %collective-permute-start.11 = (f32[10,10,1]{2,1,0:T(8,128)S(1)}, f32[10,10,1]{2,1,0:T(8,128)S(1)}, u32[]{:S(2)}, u32[]{:S(2)}) collective-permute-start(f32[10,10,1]{2,1,0:T(8,128)S(1)} %get-tuple-element.62), channel_id=1, source_target_pairs={{1,0},{2,1},{3,2},{0,3},{5,4},{6,5},{7,6},{4,7},{9,8},{10,9},{11,1... | collective-permute-start | bytes 1208 | tf_op jit(solution)/shard_map/ppermute | solution.py:23
  116.6 1.9 %collective-permute-start.10 = (f32[10,10,1]{2,1,0:T(8,128)S(1)}, f32[10,10,1]{2,1,0:T(8,128)S(1)}, u32[]{:S(2)}, u32[]{:S(2)}) collective-permute-start(f32[10,10,1]{2,1,0:T(8,128)S(1)} %get-tuple-element.61), channel_id=1, source_target_pairs={{0,1},{1,2},{2,3},{3,0},{4,5},{5,6},{6,7},{7,4},{8,9},{9,10},{10,1... | collective-permute-start | bytes 1208 | tf_op jit(solution)/shard_map/ppermute | solution.py:20
  118.5 7.6 %all-to-all-done = f32[3,64,32]{2,0,1:T(4,128)S(1)} async-done(((f32[3,64,32]{2,0,1:T(4,128)}), f32[3,64,32]{2,0,1:T(4,128)S(1)}, u32[]{:S(2)}, u32[]{:S(2)}) %all-to-all-start) | async-done | bytes 24608 | tf_op jit(solution)/shard_map/all_to_all | solution.py:92
  126.8 15.7 %psum.7 = f32[3,128]{1,0:T(4,128)S(1)} all-reduce(f32[3,128]{1,0:T(4,128)S(1)} %fusion.3), channel_id=1, replica_groups=mesh['gx'=16,'gy'=8,'gz'=4] {'gy'}, use_global_device_ids=true, to_apply=%region_5.6 | all-reduce | flops 384 | bytes 3072 | tf_op jit(solution)/shard_map/psum | solution.py:110
  144.1 4.9 %all-to-all-start.2 = ((f32[3,64,32]{2,0,1:T(4,128)}), f32[3,64,32]{2,0,1:T(4,128)S(1)}, u32[]{:S(2)}, u32[]{:S(2)}) async-start(f32[3,64,32]{2,0,1:T(4,128)} %copy.31), calls=%async_computation.2 | async-start | bytes 262144 | tf_op jit(solution)/shard_map/all_to_all | solution.py:122
  149.2 14.6 %all-to-all-done.2 = f32[3,64,32]{2,0,1:T(4,128)S(1)} async-done(((f32[3,64,32]{2,0,1:T(4,128)}), f32[3,64,32]{2,0,1:T(4,128)S(1)}, u32[]{:S(2)}, u32[]{:S(2)}) %all-to-all-start.2) | async-done | bytes 24608 | tf_op jit(solution)/shard_map/all_to_all | solution.py:122
  164.3 11.4 %scatter_custom_fusion.2 = f32[3,8192]{0,1:T(8,128)} fusion(s32[1024]{0:T(1024)S(1)} %get-tuple-element.68, f32[]{:T(128)} %constant.22.clone.1, f32[1024]{0:T(1024)S(1)} %copy-done, f32[3,2048]{0,1:T(8,128)S(1)} %bitcast.67, s32[1024]{0:T(1024)S(1)} %broadcast_clamp_fusion), kind=kCustom, calls=%fused_computation.8 | custom fusion | flops 6144 | bytes 1155076 | tf_op jit(solution)/shard_map/scatter-add | solution.py:139
  175.7 10.1 %slice_reduce_fusion.2 = (f32[8192]{0:T(1024)S(1)}, f32[8192]{0:T(1024)S(1)}, f32[8192]{0:T(1024)S(1)}) fusion(f32[3,8192]{0,1:T(8,128)} %scatter_custom_fusion.2), kind=kLoop, calls=%fused_computation.7 | loop fusion | bytes 196608 | tf_op jit(solution)/shard_map/slice | solution.py:65
  186.5 3.5 %copy.33 = f32[3,8,8,128]{3,2,1,0:T(8,128)} copy(f32[3,8,8,128]{0,3,2,1:T(8,128)} %bitcast.65) | data formatting | bytes 196608
  (63 shorter events, 9.3 us)
Async XLA Ops:
  1.4 78.0 %copy-start.1 = (s32[1024]{0:T(1024)S(1)}, s32[1024]{0:T(1024)}, u32[]{:S(2)}) copy-start(s32[1024]{0:T(1024)} %param.8) | copy-start | bytes 12292
  1.4 34.1 %collective-permute-start = (f32[4,1,8,128]{3,2,1,0:T(8,128)S(1)}, f32[4,1,8,128]{3,2,1,0:T(8,128)S(1)}, u32[]{:S(2)}, u32[]{:S(2)}) collective-permute-start(f32[4,1,8,128]{3,2,1,0:T(8,128)S(1)} %get-tuple-element.60), channel_id=1, source_target_pairs={{0,32},{32,64},{64,96},{96,128},{128,160},{160,192},{192,224},{224... | collective-permute-start | bytes 49160 | tf_op jit(solution)/shard_map/ppermute | solution.py:20
  5.9 30.5 %collective-permute-start.1 = (f32[4,1,8,128]{3,2,1,0:T(8,128)S(1)}, f32[4,1,8,128]{3,2,1,0:T(8,128)S(1)}, u32[]{:S(2)}, u32[]{:S(2)}) collective-permute-start(f32[4,1,8,128]{3,2,1,0:T(8,128)S(1)} %get-tuple-element.59), channel_id=1, source_target_pairs={{32,0},{64,32},{96,64},{128,96},{160,128},{192,160},{224,192},{256... | collective-permute-start | bytes 49160 | tf_op jit(solution)/shard_map/ppermute | solution.py:23
  16.1 71.7 %slice-start = ((f32[4,8,8,128]{3,2,1,0:T(8,128)}), f32[3,8,8,128]{3,2,1,0:T(8,128)S(1)}, s32[]{:S(2)}) async-start(f32[4,8,8,128]{3,2,1,0:T(8,128)} %param.7), calls=%async_computation.3 | async-start | bytes 196608 | tf_op jit(solution)/shard_map/slice | solution.py:130
  36.4 20.2 %collective-permute-start.3 = (f32[4,10,1,128]{3,2,1,0:T(1,128)S(1)}, f32[4,10,1,128]{3,2,1,0:T(1,128)S(1)}, u32[]{:S(2)}, u32[]{:S(2)}) collective-permute-start(f32[4,10,1,128]{3,2,1,0:T(1,128)S(1)} %get-tuple-element.58), channel_id=1, source_target_pairs={{4,0},{8,4},{12,8},{16,12},{20,16},{24,20},{28,24},{0,28},{5,1},{9... | collective-permute-start | bytes 61448 | tf_op jit(solution)/shard_map/ppermute | solution.py:23
  37.4 19.2 %collective-permute-start.2 = (f32[4,10,1,128]{3,2,1,0:T(1,128)S(1)}, f32[4,10,1,128]{3,2,1,0:T(1,128)S(1)}, u32[]{:S(2)}, u32[]{:S(2)}) collective-permute-start(f32[4,10,1,128]{3,2,1,0:T(1,128)S(1)} %get-tuple-element.57), channel_id=1, source_target_pairs={{0,4},{4,8},{8,12},{12,16},{16,20},{20,24},{24,28},{28,0},{1,5},{5... | collective-permute-start | bytes 61448 | tf_op jit(solution)/shard_map/ppermute | solution.py:20
  44.4 56.8 %all-to-all-start.1 = ((s32[1,64,32]{2,0,1:T(1,128)}), s32[1,64,32]{2,0,1:T(1,128)S(1)}, u32[]{:S(2)}, u32[]{:S(2)}) async-start(s32[1,64,32]{2,0,1:T(1,128)} %bitcast.11), calls=%async_computation.1 | async-start | bytes 65536 | tf_op jit(solution)/shard_map/all_to_all | solution.py:93
  56.8 33.6 %copy-start = (f32[1024]{0:T(1024)S(1)}, f32[1024]{0:T(1024)}, u32[]{:S(2)}) copy-start(f32[1024]{0:T(1024)} %param.10) | copy-start | bytes 12292
  56.8 10.6 %collective-permute-start.5 = (f32[4,10,10,1]{3,2,1,0:T(8,128)S(1)}, f32[4,10,10,1]{3,2,1,0:T(8,128)S(1)}, u32[]{:S(2)}, u32[]{:S(2)}) collective-permute-start(f32[4,10,10,1]{3,2,1,0:T(8,128)S(1)} %get-tuple-element.56), channel_id=1, source_target_pairs={{1,0},{2,1},{3,2},{0,3},{5,4},{6,5},{7,6},{4,7},{9,8},{10,9},{11,1... | collective-permute-start | bytes 4808 | tf_op jit(solution)/shard_map/ppermute | solution.py:23
  61.0 11.2 %collective-permute-start.4 = (f32[4,10,10,1]{3,2,1,0:T(8,128)S(1)}, f32[4,10,10,1]{3,2,1,0:T(8,128)S(1)}, u32[]{:S(2)}, u32[]{:S(2)}) collective-permute-start(f32[4,10,10,1]{3,2,1,0:T(8,128)S(1)} %get-tuple-element.55), channel_id=1, source_target_pairs={{0,1},{1,2},{2,3},{3,0},{4,5},{5,6},{6,7},{7,4},{8,9},{9,10},{10,1... | collective-permute-start | bytes 4808 | tf_op jit(solution)/shard_map/ppermute | solution.py:20
  72.9 6.5 %collective-permute-start.7 = (f32[1,8,128]{2,1,0:T(8,128)S(1)}, f32[1,8,128]{2,1,0:T(8,128)S(1)}, u32[]{:S(2)}, u32[]{:S(2)}) collective-permute-start(f32[1,8,128]{2,1,0:T(8,128)S(1)} %get-tuple-element.66), channel_id=1, source_target_pairs={{32,0},{64,32},{96,64},{128,96},{160,128},{192,160},{224,192},{256... | collective-permute-start | bytes 12296 | tf_op jit(solution)/shard_map/ppermute | solution.py:23
  77.5 5.6 %collective-permute-start.6 = (f32[1,8,128]{2,1,0:T(8,128)S(1)}, f32[1,8,128]{2,1,0:T(8,128)S(1)}, u32[]{:S(2)}, u32[]{:S(2)}) collective-permute-start(f32[1,8,128]{2,1,0:T(8,128)S(1)} %get-tuple-element.65), channel_id=1, source_target_pairs={{0,32},{32,64},{64,96},{96,128},{128,160},{160,192},{192,224},{224... | collective-permute-start | bytes 12296 | tf_op jit(solution)/shard_map/ppermute | solution.py:20
  83.1 29.2 %collective-permute-start.9 = (f32[10,1,128]{2,1,0:T(1,128)S(1)}, f32[10,1,128]{2,1,0:T(1,128)S(1)}, u32[]{:S(2)}, u32[]{:S(2)}) collective-permute-start(f32[10,1,128]{2,1,0:T(1,128)S(1)} %get-tuple-element.64), channel_id=1, source_target_pairs={{4,0},{8,4},{12,8},{16,12},{20,16},{24,20},{28,24},{0,28},{5,1},{9... | collective-permute-start | bytes 15368 | tf_op jit(solution)/shard_map/ppermute | solution.py:23
  86.7 25.6 %collective-permute-start.8 = (f32[10,1,128]{2,1,0:T(1,128)S(1)}, f32[10,1,128]{2,1,0:T(1,128)S(1)}, u32[]{:S(2)}, u32[]{:S(2)}) collective-permute-start(f32[10,1,128]{2,1,0:T(1,128)S(1)} %get-tuple-element.63), channel_id=1, source_target_pairs={{0,4},{4,8},{8,12},{12,16},{16,20},{20,24},{24,28},{28,0},{1,5},{5... | collective-permute-start | bytes 15368 | tf_op jit(solution)/shard_map/ppermute | solution.py:20
  90.4 52.1 %copy-start.2 = (f32[3,128]{1,0:T(4,128)S(1)}, f32[3,128]{1,0:T(4,128)}, u32[]{:S(2)}) copy-start(f32[3,128]{1,0:T(4,128)} %param.12) | copy-start | bytes 4612
  90.4 52.1 %copy-start.3 = (f32[128]{0:T(128)S(1)}, f32[128]{0:T(128)}, u32[]{:S(2)}) copy-start(f32[128]{0:T(128)} %param.13) | copy-start | bytes 1540
  101.1 25.0 %all-to-all-start = ((f32[3,64,32]{2,0,1:T(4,128)}), f32[3,64,32]{2,0,1:T(4,128)S(1)}, u32[]{:S(2)}, u32[]{:S(2)}) async-start(f32[3,64,32]{2,0,1:T(4,128)} %copy.28), calls=%async_computation | async-start | bytes 262144 | tf_op jit(solution)/shard_map/all_to_all | solution.py:92
  112.4 36.6 %collective-permute-start.11 = (f32[10,10,1]{2,1,0:T(8,128)S(1)}, f32[10,10,1]{2,1,0:T(8,128)S(1)}, u32[]{:S(2)}, u32[]{:S(2)}) collective-permute-start(f32[10,10,1]{2,1,0:T(8,128)S(1)} %get-tuple-element.62), channel_id=1, source_target_pairs={{1,0},{2,1},{3,2},{0,3},{5,4},{6,5},{7,6},{4,7},{9,8},{10,9},{11,1... | collective-permute-start | bytes 1208 | tf_op jit(solution)/shard_map/ppermute | solution.py:23
  116.6 32.4 %collective-permute-start.10 = (f32[10,10,1]{2,1,0:T(8,128)S(1)}, f32[10,10,1]{2,1,0:T(8,128)S(1)}, u32[]{:S(2)}, u32[]{:S(2)}) collective-permute-start(f32[10,10,1]{2,1,0:T(8,128)S(1)} %get-tuple-element.61), channel_id=1, source_target_pairs={{0,1},{1,2},{2,3},{3,0},{4,5},{5,6},{6,7},{7,4},{8,9},{9,10},{10,1... | collective-permute-start | bytes 1208 | tf_op jit(solution)/shard_map/ppermute | solution.py:20
  144.1 19.7 %all-to-all-start.2 = ((f32[3,64,32]{2,0,1:T(4,128)}), f32[3,64,32]{2,0,1:T(4,128)S(1)}, u32[]{:S(2)}, u32[]{:S(2)}) async-start(f32[3,64,32]{2,0,1:T(4,128)} %copy.31), calls=%async_computation.2 | async-start | bytes 262144 | tf_op jit(solution)/shard_map/all_to_all | solution.py:122
where the time goes:
time: 193 us; the launch traced here: 191 us
  starting transfers between devices  66.3 us (34%)
  other arithmetic  44.4 us (23%)
  waiting for transfers between devices  35.1 us (18%)
  local copies, waits for them, and re-layouts  26.8 us (14%)
  blocking collectives  15.7 us (8%)
    ppermute x6, starting transfers between devices, with_halo(): lax.ppermute(lax.slice_in_dim(block, 0, width, axis=dim), axis, backward)  26.9 us
    another operation x3, other arithmetic  18.2 us
    psum x1, blocking collectives, routed_forces(): point_velocity = lax.psum(partial_sum, 'gy')  15.7 us
    all_to_all x1, waiting for transfers between devices, routed_forces(): lax.all_to_all(returned, ('gx', 'gz'), split_axis=1, concat_axis=1, tiled...  14.6 us
    ppermute x6, starting transfers between devices, with_halo(): lax.ppermute(lax.slice_in_dim(block, block.shape[dim] - width, None, axis...  12.5 us
    all_to_all x1, starting transfers between devices, routed_forces(): lax.all_to_all(send_ids, ('gx', 'gz'), split_axis=1, concat_axis=1, tiled...  12.2 us
    scatter-add x1, other arithmetic, body(): body_force = jnp.zeros((3, cells), jnp.float32).at[:, sample_cell].add(fo...  11.4 us
    slice x1, local copies, waits for them, and re-layouts, advance(): change = change + force[c]  10.1 us
  transfers between devices with their start and end apart: 15, of which 5 were waited for; matrix products, arithmetic and copies ran while one was open for 24% of the time, Pallas kernels for 0%

commit v1 on v0

v1 whole, which is shorter than its diff:
```python
import jax
import jax.numpy as jnp
from jax import lax
from jax.experimental import pallas as pl
from jax.experimental.pallas import tpu as pltpu
from jax.sharding import PartitionSpec as P

DT_STEP = 0.4
BASE_COEF = 0.02
PRANDTL = 0.7
SMAG_COEF = 0.04

ROWS = 1024
PLANE = ("gy", "gz")


def call(kernel, outs, scratch=(), smem=0, count=1, flops=2_000_000, nbytes=1_000_000):
    return pl.pallas_call(
        kernel,
        out_shape=outs,
        in_specs=[pl.BlockSpec(memory_space=pltpu.SMEM)] * smem
        + [pl.BlockSpec(memory_space=pltpu.VMEM)] * (count - smem),
        out_specs=jax.tree.map(lambda _: pl.BlockSpec(memory_space=pltpu.VMEM), outs),
        scratch_shapes=scratch,
        compiler_params=pltpu.CompilerParams(vmem_limit_bytes=24 * 1024 * 1024),
        cost_estimate=pl.CostEstimate(flops=flops, bytes_accessed=nbytes, transcendentals=0),
    )


def f32(*shape):
    return jax.ShapeDtypeStruct(shape, jnp.float32)


def halves(values):
    high = values.astype(jnp.bfloat16)
    return high, (values - high.astype(jnp.float32)).astype(jnp.bfloat16)


def onehot(index, size):
    wanted = lax.broadcasted_iota(jnp.int32, (size, ROWS), 0)
    return jnp.where(wanted == index, 1.0, 0.0).astype(jnp.bfloat16)


def pick(table, hot):
    both = jnp.concatenate(halves(table), axis=1)
    return jnp.dot(both, jnp.concatenate([hot, hot], axis=0), preferred_element_type=jnp.float32)


def put(values, hot):
    high, low = halves(values)
    dims = (((1,), (1,)), ((), ()))
    total = lax.dot_general(high, hot, dims, preferred_element_type=jnp.float32)
    return total + lax.dot_general(low, hot, dims, preferred_element_type=jnp.float32)


def cell_keys(cell):
    column = lax.broadcasted_iota(jnp.int32, (64, ROWS), 0) == (cell >> 7)
    return column, onehot(cell & 127, 128)


def element_keys(dest, elem):
    tile = (elem >> 4) * 4 + (dest & 3)
    along = dest >> 2
    number = tile * 2 + (along >> 3)
    shape = (32, 8, ROWS)
    row = lax.broadcasted_iota(jnp.int32, shape, 0) * 2 + (
        lax.broadcasted_iota(jnp.int32, shape, 1) & 1
    )
    return row == number[None], onehot((along & 7) * 16 + (elem & 15), 128)


def sample_kernel(state, cell, dest, elem, weight, out):
    column, hot_z = cell_keys(cell[...])
    found = pick(state[0:3].reshape(192, 128), hot_z).reshape(3, 64, ROWS)
    sampled = [
        jnp.sum(jnp.where(column, found[c], 0.0), axis=0, keepdims=True) * weight[...]
        for c in range(3)
    ]
    row = lax.broadcasted_iota(jnp.int32, (8, ROWS), 0) >> 1
    pattern = jnp.where(
        row == 0, sampled[0], jnp.where(row == 1, sampled[1], jnp.where(row == 2, sampled[2], 0.0))
    )
    match, hot_lane = element_keys(dest[...], elem[...])
    spread = jnp.where(match, pattern[None], 0.0).reshape(256, ROWS)
    out[...] = put(spread, hot_lane).reshape(32, 8, 128)


def own_kernel(place, parts, motion, coef, out):
    gx, gy = place[0], place[1]
    total = jnp.sum(parts[...], axis=0)
    row = lax.broadcasted_iota(jnp.int32, (8, 128), 0)
    lane = lax.broadcasted_iota(jnp.int32, (8, 128), 1)
    level = row >> 1
    held = jnp.where(
        level == 0,
        motion[0:1, :],
        jnp.where(level == 1, motion[1:2, :], jnp.where(level == 2, motion[2:3, :], coef[...])),
    )
    moved = pltpu.roll(held, ((gx & 7) * 16 - gy * 16 + 128) & 127, 1)
    mine = ((lane >> 4) == (gx & 7)) & ((row & 1) == (gx >> 3))
    total = total + jnp.where(mine, moved, 0.0)
    out[...] = jnp.broadcast_to(total[None], (16, 8, 128))


def force_kernel(parts, out):
    total = jnp.sum(parts[...], axis=0)
    row = lax.broadcasted_iota(jnp.int32, (8, 128), 0)

    def by_parity(values):
        values = values + pltpu.roll(values, 4, 0)
        return values + pltpu.roll(values, 2, 0)

    speed = jnp.sqrt(by_parity(jnp.where(row < 6, total * total, 0.0)))
    coef = by_parity(jnp.where(row < 6, 0.0, total))
    force = jnp.where(row < 6, -coef * speed * total, 0.0)
    out[...] = jnp.broadcast_to(force[None], (32, 8, 128))


def spread_kernel(forces, cell, dest, elem, weight, before, new_state, body_force):
    match, hot_lane = element_keys(dest[...], elem[...])
    found = pick(forces[...].reshape(256, 128), hot_lane).reshape(32, 8, ROWS)
    pairs = jnp.sum(jnp.where(match, found, 0.0), axis=0)
    column, hot_z = cell_keys(cell[...])
    each = [(pairs[2 * c : 2 * c + 1] + pairs[2 * c + 1 : 2 * c + 2]) * weight[...] for c in range(3)]
    spread = jnp.concatenate([jnp.where(column, each[c], 0.0) for c in range(3)], axis=0)
    body = put(spread, hot_z).reshape(3, 8, 8, 128)
    body_force[...] = body
    new_state[0:3] = before[0:3] + DT_STEP * body
    new_state[3] = before[3]


def fill(grid, state, xlo, xhi, ylo, yhi):
    grid[:, 2:10, 0:8, 0:128] = state[...]
    grid[:, 0:2, 0:8, 0:128] = xlo[...]
    grid[:, 10:12, 0:8, 0:128] = xhi[...]
    grid[:, 1:11, 8:10, 0:128] = yhi[...]
    grid[:, 1:11, 14:16, 0:128] = ylo[...]


def ends_kernel(state, xlo, xhi, ylo, yhi, zup, zdown, grid):
    grid[:, :, 8:16, 0:128] = jnp.zeros((4, 12, 8, 128), jnp.float32)
    fill(grid, state, xlo, xhi, ylo, yhi)
    rows = grid[:, 1:11, :, 0:128].reshape(640, 128)
    row = lax.broadcasted_iota(jnp.int32, (8, 128), 0)
    lane = lax.broadcasted_iota(jnp.int32, (8, 128), 1)
    wanted = jnp.where(row < 2, row, jnp.where(row < 4, row + 124, -1))
    ends = lax.dot_general(
        jnp.where(lane == wanted, 1.0, 0.0),
        rows,
        (((1,), (1,)), ((), ())),
        precision=lax.Precision.HIGHEST,
        preferred_element_type=jnp.float32,
    )
    zdown[...] = ends[0:2]
    zup[...] = ends[2:4]


def stencil_kernel(place, state, xlo, xhi, ylo, yhi, zlo, zhi, out, grid):
    gz = place[2]
    fill(grid, state, xlo, xhi, ylo, yhi)
    row = lax.broadcasted_iota(jnp.int32, (4, 128), 0)
    lane = lax.broadcasted_iota(jnp.int32, (4, 128), 1)
    wanted = jnp.where(row < 2, row, row + 124)
    ghosts = lax.dot_general(
        jnp.concatenate([zhi[...], zlo[...]], axis=0),
        jnp.where(lane == wanted, 1.0, 0.0),
        (((0,), (0,)), ((), ())),
        precision=lax.Precision.HIGHEST,
        preferred_element_type=jnp.float32,
    ).reshape(4, 10, 16, 128)
    level = lax.broadcasted_iota(jnp.int32, (1, 1, 256), 2)
    outside = ((level >= 128) & (level < 192) & (gz == 3)) | ((level >= 192) & (gz == 0))
    grid[:, 1:11, :, 128:256] = jnp.where(outside[None, :, :, 128:256], 0.0, ghosts)

    def around(values):
        return (
            (pltpu.roll(values, 15, 1), pltpu.roll(values, 1, 1)),
            (pltpu.roll(values, 255, 2), pltpu.roll(values, 1, 2)),
        )

    fields = [grid[c] for c in range(4)]
    sides = []
    diffs = []
    for c in range(4):
        middle = fields[c][1:11]
        near = ((fields[c][2:12], fields[c][0:10]),) + around(middle)
        sides.append(near)
        diffs.append([upper - lower for upper, lower in near])
    strain = 0.5 * (
        diffs[0][0] * diffs[0][0] + diffs[1][1] * diffs[1][1] + diffs[2][2] * diffs[2][2]
    )
    for i, j in ((0, 1), (0, 2), (1, 2)):
        paired = diffs[i][j] + diffs[j][i]
        strain = strain + 0.25 * paired * paired
    eddy = jnp.where(outside, 0.0, SMAG_COEF * jnp.sqrt(strain))

    def inner(values):
        return values[:, 0:8, 0:128]

    centre = inner(eddy[1:9])
    near = ((eddy[2:10], eddy[0:8]),) + around(eddy[1:9])
    faces = [[0.5 * (centre + inner(side)) for side in pair] for pair in near]
    wind = [0.5 * inner(fields[c][2:10]) for c in range(3)]
    for c in range(4):
        middle = inner(fields[c][2:10])
        ratio = 1.0 if c < 3 else 1.0 / PRANDTL
        change = 0.0
        for j in range(3):
            upper, lower = [inner(side[1:9]) for side in sides[c][j]]
            change = change + (BASE_COEF + ratio * faces[j][0]) * (upper - middle)
            change = change - (BASE_COEF + ratio * faces[j][1]) * (middle - lower)
            change = change - wind[j] * (upper - lower)
        out[c] = middle + DT_STEP * change


def swap(up, down, axis):
    count = lax.axis_size(axis)
    forward = [(i, (i + 1) % count) for i in range(count)]
    backward = [(target, source) for source, target in forward]
    return lax.ppermute(up, axis, forward), lax.ppermute(down, axis, backward)


def exchange(blocks, axes):
    return lax.all_to_all(blocks, axes, split_axis=0, concat_axis=0, tiled=True)


def body(state, sample_cell, sample_dest, sample_weight, sample_elem, element_motion, element_coef):
    place = jnp.stack([lax.axis_index(axis) for axis in ("gx", "gy", "gz")]).astype(jnp.int32)
    cell = sample_cell.reshape(1, ROWS)
    dest = sample_dest.reshape(1, ROWS)
    elem = sample_elem.reshape(1, ROWS)
    weight = sample_weight.reshape(1, ROWS)

    xlo, xhi = swap(state[:, 6:8], state[:, 0:2], "gx")
    partial = call(sample_kernel, f32(32, 8, 128), count=5)(state, cell, dest, elem, weight)
    partial = exchange(partial, PLANE)

    wide = jnp.concatenate([xlo[:, 1:2], state, xhi[:, 0:1]], axis=1)
    ylo, yhi = swap(wide[:, :, 6:8], wide[:, :, 0:2], "gy")

    totals = call(own_kernel, f32(16, 8, 128), smem=1, count=4)(
        place, partial, element_motion, element_coef.reshape(1, 128)
    )
    totals = exchange(totals, "gx")

    padded = pltpu.VMEM((4, 12, 16, 256), jnp.float32)
    zup, zdown = call(ends_kernel, (f32(2, 640), f32(2, 640)), (padded,), count=5)(
        state, xlo, xhi, ylo, yhi
    )
    zlo, zhi = swap(zup, zdown, "gz")

    forces = call(force_kernel, f32(32, 8, 128), count=1)(totals)
    forces = exchange(forces, PLANE)

    before = call(stencil_kernel, f32(4, 8, 8, 128), (padded,), smem=1, count=8)(
        place, state, xlo, xhi, ylo, yhi, zlo, zhi
    )
    return call(spread_kernel, (f32(4, 8, 8, 128), f32(3, 8, 8, 128)), count=6)(
        forces, cell, dest, elem, weight, before
    )


def solution(mesh):
    return jax.shard_map(
        body,
        mesh=mesh,
        in_specs=(
            P(None, "gx", "gy", "gz"),
            P(("gx", "gy", "gz")),
            P(("gx", "gy", "gz"), None),
            P(("gx", "gy", "gz")),
            P(("gx", "gy", "gz")),
            P(None, ("gx", "gz")),
            P(("gx", "gz")),
        ),
        out_specs=(P(None, "gx", "gy", "gz"), P(None, "gx", "gy", "gz")),
        check_vma=False,
    )
```

time: 193 us -> 75.6 us (0.39)
  the two profiles are of different devices: /device:TPU:1 before, /device:TPU:24 now
where the time goes in v1:
time: 75.6 us; the launch traced here: 75 us
  starting transfers between devices  43.8 us (58%)
  waiting for transfers between devices  18.7 us (25%)
  Pallas kernels  6.7 us (9%)
  local copies, waits for them, and re-layouts  4.9 us (6%)
  between operations  0.86 us (1%)
    all_to_all x3, starting transfers between devices, exchange(): return lax.all_to_all(blocks, axes, split_axis=0, concat_axis=0, tiled=True)  28.2 us
    ppermute x6, starting transfers between devices, swap(): return (lax.ppermute(up, axis, forward), lax.ppermute(down, axis, backward))  15.6 us
    ppermute x6, waiting for transfers between devices, swap(): return (lax.ppermute(up, axis, forward), lax.ppermute(down, axis, backward))  12.4 us
    all_to_all x3, waiting for transfers between devices, exchange(): return lax.all_to_all(blocks, axes, split_axis=0, concat_axis=0, tiled=True)  6.22 us
    unnamed x30, local copies, waits for them, and re-layouts  4.88 us
    pallas_call x1, Pallas kernels, body(): call(spread_kernel, (f32(4, 8, 8, 128), f32(3, 8, 8, 128)), count=6)  1.57 us
  transfers between devices with their start and end apart: 9, of which 5 were waited for; matrix products, arithmetic and copies ran while one was open for 0% of the time, Pallas kernels for 2%

profile of v1, /device:TPU:24, one launch (start us, length us, event | category | flops | bytes accessed | tf_op | source)
XLA Modules:
  0.0 75.0 jit_solution(4817509344785623331)
XLA Ops:
  0.6 0.7 copy-done.6
  1.3 0.9 %copy-done = f32[4,8,8,128]{3,2,1,0:T(8,128)S(1)} copy-done((f32[4,8,8,128]{3,2,1,0:T(8,128)S(1)}, f32[4,8,8,128]{3,2,1,0:T(8,128)}, u32[]{:S(2)}) %copy-start) | copy-done | bytes 131096
  2.2 0.7 copy-done.7
  2.9 0.7 copy-done.9
  3.6 0.7 copy-done.11
  4.3 1.4 %shard_map.86 = f32[32,8,128]{2,1,0:T(8,128)} custom-call(f32[4,8,8,128]{3,2,1,0:T(8,128)S(1)} %copy-done, s32[1,1024]{1,0:T(1,128)S(1)} %bitcast.8, s32[1,1024]{1,0:T(1,128)S(1)} %bitcast.10, s32[1,1024]{1,0:T(1,128)S(1)} %bitcast.12, f32[1,1024]{1,0:T(1,128)S(1)} %bitcast.14), custom_call_target="tpu_custom_call" | custom-call | flops 2000000 | bytes 1000000 | tf_op jit(solution)/shard_map/pallas_call | solution.py:235
  5.7 9.1 %all-to-all-start = ((f32[32,8,128]{2,1,0:T(8,128)}), f32[32,8,128]{2,1,0:T(8,128)S(1)}, u32[]{:S(2)}, u32[]{:S(2)}) async-start(f32[32,8,128]{2,1,0:T(8,128)} %shard_map.86), calls=%async_computation | async-start | bytes 262144 | tf_op jit(solution)/shard_map/all_to_all | solution.py:224
  14.8 0.0 copy-start.13
  14.8 0.1 pad_add_fusion.place
  14.9 6.2 %all-to-all-done.parts = f32[32,8,128]{2,1,0:T(8,128)S(1)} async-done(((f32[32,8,128]{2,1,0:T(8,128)}), f32[32,8,128]{2,1,0:T(8,128)S(1)}, u32[]{:S(2)}, u32[]{:S(2)}) %all-to-all-start) | async-done | bytes 131104 | tf_op jit(solution)/shard_map/all_to_all | solution.py:224
  21.1 1.2 %shard_map.87 = f32[16,8,128]{2,1,0:T(8,128)} custom-call(s32[3]{0:T(128)S(1)} %pad_add_fusion.place, f32[32,8,128]{2,1,0:T(8,128)S(1)} %all-to-all-done.parts, f32[3,128]{1,0:T(4,128)S(1)} %copy-done.13, f32[1,128]{1,0:T(1,128)S(1)} %bitcast.16), custom_call_target="tpu_custom_call" | custom-call | flops 2000000 | bytes 1000000 | tf_op jit(solution)/shard_map/pallas_call | solution.py:241
  22.3 13.3 %all-to-all-start.1 = ((f32[16,8,128]{2,1,0:T(8,128)}), f32[16,8,128]{2,1,0:T(8,128)S(1)}, u32[]{:S(2)}, u32[]{:S(2)}) async-start(f32[16,8,128]{2,1,0:T(8,128)} %shard_map.87), calls=%async_computation.1 | async-start | bytes 131072 | tf_op jit(solution)/shard_map/all_to_all | solution.py:224
  35.7 5.0 %collective-permute-start.1 = (f32[4,2,8,128]{3,2,1,0:T(8,128)S(1)}, f32[4,2,8,128]{3,2,1,0:T(8,128)S(1)}, u32[]{:S(2)}, u32[]{:S(2)}) collective-permute-start(f32[4,2,8,128]{3,2,1,0:T(8,128)S(1)} %get-tuple-element.8), channel_id=1, source_target_pairs={{32,0},{64,32},{96,64},{128,96},{160,128},{192,160},{224,192},{256... | collective-permute-start | bytes 98312 | tf_op jit(solution)/shard_map/ppermute | solution.py:220
  40.7 1.9 %collective-permute-start = (f32[4,2,8,128]{3,2,1,0:T(8,128)S(1)}, f32[4,2,8,128]{3,2,1,0:T(8,128)S(1)}, u32[]{:S(2)}, u32[]{:S(2)}) collective-permute-start(f32[4,2,8,128]{3,2,1,0:T(8,128)S(1)} %get-tuple-element.9), channel_id=1, source_target_pairs={{0,32},{32,64},{64,96},{96,128},{128,160},{160,192},{192,224},{224... | collective-permute-start | bytes 98312 | tf_op jit(solution)/shard_map/ppermute | solution.py:220
  42.7 0.6 copy-done.2
  43.3 4.5 %collective-permute-done.xlo = f32[4,2,8,128]{3,2,1,0:T(8,128)S(1)} collective-permute-done((f32[4,2,8,128]{3,2,1,0:T(8,128)S(1)}, f32[4,2,8,128]{3,2,1,0:T(8,128)S(1)}, u32[]{:S(2)}, u32[]{:S(2)}) %collective-permute-start) | collective-permute-done | bytes 32800 | tf_op jit(solution)/shard_map/ppermute | solution.py:220
  47.7 0.6 copy-done.4
  48.3 0.0 all-to-all-done.1.parts
  48.4 0.7 shard_map.88
  49.1 5.8 %all-to-all-start.2 = ((f32[32,8,128]{2,1,0:T(8,128)}), f32[32,8,128]{2,1,0:T(8,128)S(1)}, u32[]{:S(2)}, u32[]{:S(2)}) async-start(f32[32,8,128]{2,1,0:T(8,128)} %shard_map.88), calls=%async_computation.2 | async-start | bytes 262144 | tf_op jit(solution)/shard_map/all_to_all | solution.py:224
  55.0 2.6 %collective-permute-start.3 = (f32[4,10,2,128]{3,2,1,0:T(2,128)S(1)}, f32[4,10,2,128]{3,2,1,0:T(2,128)S(1)}, u32[]{:S(2)}, u32[]{:S(2)}) collective-permute-start(f32[4,10,2,128]{3,2,1,0:T(2,128)S(1)} %get-tuple-element.6), channel_id=1, source_target_pairs={{4,0},{8,4},{12,8},{16,12},{20,16},{24,20},{28,24},{0,28},{5,1},{9... | collective-permute-start | bytes 122888 | tf_op jit(solution)/shard_map/ppermute | solution.py:220
  57.6 1.7 %collective-permute-done.3.yhi = f32[4,10,2,128]{3,2,1,0:T(2,128)S(1)} collective-permute-done((f32[4,10,2,128]{3,2,1,0:T(2,128)S(1)}, f32[4,10,2,128]{3,2,1,0:T(2,128)S(1)}, u32[]{:S(2)}, u32[]{:S(2)}) %collective-permute-start.3) | collective-permute-done | bytes 40992 | tf_op jit(solution)/shard_map/ppermute | solution.py:220
  59.3 3.0 %collective-permute-done.2.ylo = f32[4,10,2,128]{3,2,1,0:T(2,128)S(1)} collective-permute-done((f32[4,10,2,128]{3,2,1,0:T(2,128)S(1)}, f32[4,10,2,128]{3,2,1,0:T(2,128)S(1)}, u32[]{:S(2)}, u32[]{:S(2)}) %collective-permute-start.2) | collective-permute-done | bytes 40992 | tf_op jit(solution)/shard_map/ppermute | solution.py:220
  62.2 0.4 shard_map.89
  62.7 2.5 %collective-permute-start.4 = (f32[2,640]{1,0:T(2,128)S(1)}, f32[2,640]{1,0:T(2,128)S(1)}, u32[]{:S(2)}, u32[]{:S(2)}) collective-permute-start(f32[2,640]{1,0:T(2,128)S(1)} %get-tuple-element.4), channel_id=1, source_target_pairs={{0,1},{1,2},{2,3},{3,0},{4,5},{5,6},{6,7},{7,4},{8,9},{9,10},{10,1... | collective-permute-start | bytes 15368 | tf_op jit(solution)/shard_map/ppermute | solution.py:220
  65.1 0.0 copy-start.8
  65.1 0.0 copy-start.10
  65.2 0.0 copy-start.12
  65.2 3.5 %collective-permute-start.5 = (f32[2,640]{1,0:T(2,128)S(1)}, f32[2,640]{1,0:T(2,128)S(1)}, u32[]{:S(2)}, u32[]{:S(2)}) collective-permute-start(f32[2,640]{1,0:T(2,128)S(1)} %get-tuple-element.5), channel_id=1, source_target_pairs={{1,0},{2,1},{3,2},{0,3},{5,4},{6,5},{7,6},{4,7},{9,8},{10,9},{11,1... | collective-permute-start | bytes 15368 | tf_op jit(solution)/shard_map/ppermute | solution.py:220
  68.7 3.3 %collective-permute-done.5.zhi = f32[2,640]{1,0:T(2,128)S(1)} collective-permute-done((f32[2,640]{1,0:T(2,128)S(1)}, f32[2,640]{1,0:T(2,128)S(1)}, u32[]{:S(2)}, u32[]{:S(2)}) %collective-permute-start.5) | collective-permute-done | bytes 5152 | tf_op jit(solution)/shard_map/ppermute | solution.py:220
  72.0 1.4 %shard_map.90.before = f32[4,8,8,128]{3,2,1,0:T(8,128)S(1)} custom-call(s32[3]{0:T(128)S(1)} %pad_add_fusion.place, f32[4,8,8,128]{3,2,1,0:T(8,128)S(1)} %copy-done.1, f32[4,2,8,128]{3,2,1,0:T(8,128)S(1)} %copy-done.5, f32[4,2,8,128]{3,2,1,0:T(8,128)S(1)} %copy-done.3, f32[4,10,2,128]{3,2,1,0:T(2,128)S(1)} %collective-permute-done.2.ylo, ...), custom_call_target="tpu_custom_call" | custom-call | flops 2000000 | bytes 1000000 | tf_op jit(solution)/shard_map/pallas_call | solution.py:255
  73.4 1.6 %shard_map.91 = (f32[4,8,8,128]{3,2,1,0:T(8,128)}, f32[3,8,8,128]{3,2,1,0:T(8,128)}) custom-call(f32[32,8,128]{2,1,0:T(8,128)S(1)} %all-to-all-done.2.forces, s32[1,1024]{1,0:T(1,128)S(1)} %bitcast.9, s32[1,1024]{1,0:T(1,128)S(1)} %bitcast.11, s32[1,1024]{1,0:T(1,128)S(1)} %bitcast.13, f32[1,1024]{1,0:T(1,128)S(1)} %bitcast.15, ...), custom_call_target="tpu_custom_call" | custom-call | flops 2000000 | bytes 1000000 | tf_op jit(solution)/shard_map/pallas_call | solution.py:258
  (29 shorter events, 0.1 us)
Async XLA Ops:
  0.6 0.7 copy-start.6
  1.3 0.9 %copy-start = (f32[4,8,8,128]{3,2,1,0:T(8,128)S(1)}, f32[4,8,8,128]{3,2,1,0:T(8,128)}, u32[]{:S(2)}) copy-start(f32[4,8,8,128]{3,2,1,0:T(8,128)} %state.5) | copy-start | bytes 393220
  2.2 0.7 copy-start.7
  2.9 0.7 copy-start.9
  3.6 0.7 copy-start.11
  5.7 15.4 %all-to-all-start = ((f32[32,8,128]{2,1,0:T(8,128)}), f32[32,8,128]{2,1,0:T(8,128)S(1)}, u32[]{:S(2)}, u32[]{:S(2)}) async-start(f32[32,8,128]{2,1,0:T(8,128)} %shard_map.86), calls=%async_computation | async-start | bytes 262144 | tf_op jit(solution)/shard_map/all_to_all | solution.py:224
  14.8 6.3 %copy-start.13 = (f32[3,128]{1,0:T(4,128)S(1)}, f32[3,128]{1,0:T(4,128)}, u32[]{:S(2)}) copy-start(f32[3,128]{1,0:T(4,128)} %motion.1) | copy-start | bytes 4612
  14.9 6.2 %copy-start.14 = (f32[128]{0:T(128)S(1)}, f32[128]{0:T(128)}, u32[]{:S(2)}) copy-start(f32[128]{0:T(128)} %param.13) | copy-start | bytes 1540
  21.1 14.5 %copy-start.1 = (f32[4,8,8,128]{3,2,1,0:T(8,128)S(1)}, f32[4,8,8,128]{3,2,1,0:T(8,128)}, u32[]{:S(2)}) copy-start(f32[4,8,8,128]{3,2,1,0:T(8,128)} %state.5) | copy-start | bytes 393220
  22.3 26.0 %all-to-all-start.1 = ((f32[16,8,128]{2,1,0:T(8,128)}), f32[16,8,128]{2,1,0:T(8,128)S(1)}, u32[]{:S(2)}, u32[]{:S(2)}) async-start(f32[16,8,128]{2,1,0:T(8,128)} %shard_map.87), calls=%async_computation.1 | async-start | bytes 131072 | tf_op jit(solution)/shard_map/all_to_all | solution.py:224
  35.7 7.0 %collective-permute-start.1 = (f32[4,2,8,128]{3,2,1,0:T(8,128)S(1)}, f32[4,2,8,128]{3,2,1,0:T(8,128)S(1)}, u32[]{:S(2)}, u32[]{:S(2)}) collective-permute-start(f32[4,2,8,128]{3,2,1,0:T(8,128)S(1)} %get-tuple-element.8), channel_id=1, source_target_pairs={{32,0},{64,32},{96,64},{128,96},{160,128},{192,160},{224,192},{256... | collective-permute-start | bytes 98312 | tf_op jit(solution)/shard_map/ppermute | solution.py:220
  40.7 7.0 %collective-permute-start = (f32[4,2,8,128]{3,2,1,0:T(8,128)S(1)}, f32[4,2,8,128]{3,2,1,0:T(8,128)S(1)}, u32[]{:S(2)}, u32[]{:S(2)}) collective-permute-start(f32[4,2,8,128]{3,2,1,0:T(8,128)S(1)} %get-tuple-element.9), channel_id=1, source_target_pairs={{0,32},{32,64},{64,96},{96,128},{128,160},{160,192},{192,224},{224... | collective-permute-start | bytes 98312 | tf_op jit(solution)/shard_map/ppermute | solution.py:220
  42.6 0.6 copy-start.2
  47.7 0.6 copy-start.4
  49.1 5.8 %slice-start = ((f32[4,2,8,128]{3,2,1,0:T(8,128)}), f32[4,1,8,128]{3,2,1,0:T(8,128)S(1)}, s32[]{:S(2)}) async-start(f32[4,2,8,128]{3,2,1,0:T(8,128)} %copy-done.2), calls=%async_computation.3 | async-start | bytes 32768 | tf_op jit(solution)/shard_map/slice | solution.py:238
  49.1 5.8 %slice-start.1 = ((f32[4,2,8,128]{3,2,1,0:T(8,128)}), f32[4,1,8,128]{3,2,1,0:T(8,128)S(1)}, s32[]{:S(2)}) async-start(f32[4,2,8,128]{3,2,1,0:T(8,128)} %copy-done.4), calls=%async_computation.4 | async-start | bytes 32768 | tf_op jit(solution)/shard_map/slice | solution.py:238
  49.1 24.3 %all-to-all-start.2 = ((f32[32,8,128]{2,1,0:T(8,128)}), f32[32,8,128]{2,1,0:T(8,128)S(1)}, u32[]{:S(2)}, u32[]{:S(2)}) async-start(f32[32,8,128]{2,1,0:T(8,128)} %shard_map.88), calls=%async_computation.2 | async-start | bytes 262144 | tf_op jit(solution)/shard_map/all_to_all | solution.py:224
  54.9 7.3 %copy-start.3 = (f32[4,2,8,128]{3,2,1,0:T(8,128)S(1)}, f32[4,2,8,128]{3,2,1,0:T(8,128)}, u32[]{:S(2)}) copy-start(f32[4,2,8,128]{3,2,1,0:T(8,128)} %copy-done.2) | copy-start | bytes 98308
  54.9 7.3 %copy-start.5 = (f32[4,2,8,128]{3,2,1,0:T(8,128)S(1)}, f32[4,2,8,128]{3,2,1,0:T(8,128)}, u32[]{:S(2)}) copy-start(f32[4,2,8,128]{3,2,1,0:T(8,128)} %copy-done.4) | copy-start | bytes 98308
  55.0 4.3 %collective-permute-start.3 = (f32[4,10,2,128]{3,2,1,0:T(2,128)S(1)}, f32[4,10,2,128]{3,2,1,0:T(2,128)S(1)}, u32[]{:S(2)}, u32[]{:S(2)}) collective-permute-start(f32[4,10,2,128]{3,2,1,0:T(2,128)S(1)} %get-tuple-element.6), channel_id=1, source_target_pairs={{4,0},{8,4},{12,8},{16,12},{20,16},{24,20},{28,24},{0,28},{5,1},{9... | collective-permute-start | bytes 122888 | tf_op jit(solution)/shard_map/ppermute | solution.py:220
  57.6 4.6 %collective-permute-start.2 = (f32[4,10,2,128]{3,2,1,0:T(2,128)S(1)}, f32[4,10,2,128]{3,2,1,0:T(2,128)S(1)}, u32[]{:S(2)}, u32[]{:S(2)}) collective-permute-start(f32[4,10,2,128]{3,2,1,0:T(2,128)S(1)} %get-tuple-element.7), channel_id=1, source_target_pairs={{0,4},{4,8},{8,12},{12,16},{16,20},{20,24},{24,28},{28,0},{1,5},{5... | collective-permute-start | bytes 122888 | tf_op jit(solution)/shard_map/ppermute | solution.py:220
  62.7 6.0 %collective-permute-start.4 = (f32[2,640]{1,0:T(2,128)S(1)}, f32[2,640]{1,0:T(2,128)S(1)}, u32[]{:S(2)}, u32[]{:S(2)}) collective-permute-start(f32[2,640]{1,0:T(2,128)S(1)} %get-tuple-element.4), channel_id=1, source_target_pairs={{0,1},{1,2},{2,3},{3,0},{4,5},{5,6},{6,7},{7,4},{8,9},{9,10},{10,1... | collective-permute-start | bytes 15368 | tf_op jit(solution)/shard_map/ppermute | solution.py:220
  65.1 8.3 %copy-start.8 = (s32[1024,1]{0,1:T(1,128)S(1)}, s32[1024,1]{0,1:T(1,128)}, u32[]{:S(2)}) copy-start(s32[1024,1]{0,1:T(1,128)} %param.9) | copy-start | bytes 12292
  65.1 8.3 %copy-start.10 = (s32[1024]{0:T(1024)S(1)}, s32[1024]{0:T(1024)}, u32[]{:S(2)}) copy-start(s32[1024]{0:T(1024)} %param.11) | copy-start | bytes 12292
  65.2 8.3 %copy-start.12 = (f32[1024]{0:T(1024)S(1)}, f32[1024]{0:T(1024)}, u32[]{:S(2)}) copy-start(f32[1024]{0:T(1024)} %param.10) | copy-start | bytes 12292
  65.2 6.9 %collective-permute-start.5 = (f32[2,640]{1,0:T(2,128)S(1)}, f32[2,640]{1,0:T(2,128)S(1)}, u32[]{:S(2)}, u32[]{:S(2)}) collective-permute-start(f32[2,640]{1,0:T(2,128)S(1)} %get-tuple-element.5), channel_id=1, source_target_pairs={{1,0},{2,1},{3,2},{0,3},{5,4},{6,5},{7,6},{4,7},{9,8},{10,9},{11,1... | collective-permute-start | bytes 15368 | tf_op jit(solution)/shard_map/ppermute | solution.py:220

commit v2 on v1

--- a/solution.py
+++ b/solution.py
@@ -14,12 +14,12 @@
 PLANE = ("gy", "gz")
 
 
-def call(kernel, outs, scratch=(), smem=0, count=1, flops=2_000_000, nbytes=1_000_000):
+def call(kernel, outs, scratch=(), smem=0, count=1, space=pltpu.VMEM, flops=2_000_000, nbytes=1_000_000):
     return pl.pallas_call(
         kernel,
         out_shape=outs,
         in_specs=[pl.BlockSpec(memory_space=pltpu.SMEM)] * smem
-        + [pl.BlockSpec(memory_space=pltpu.VMEM)] * (count - smem),
+        + [pl.BlockSpec(memory_space=space)] * (count - smem),
         out_specs=jax.tree.map(lambda _: pl.BlockSpec(memory_space=pltpu.VMEM), outs),
         scratch_shapes=scratch,
         compiler_params=pltpu.CompilerParams(vmem_limit_bytes=24 * 1024 * 1024),
@@ -69,9 +69,20 @@
     return row == number[None], onehot((along & 7) * 16 + (elem & 15), 128)
 
 
-def sample_kernel(state, cell, dest, elem, weight, out):
+def sample_kernel(state_in, cell_in, dest_in, elem_in, weight_in, out, *scratch):
+    held, sems = scratch[:5], scratch[5]
+    sources = (state_in.at[0:3], cell_in, dest_in, elem_in, weight_in)
+    copies = [
+        pltpu.make_async_copy(source, target, sems.at[i])
+        for i, (source, target) in enumerate(zip(sources, held))
+    ]
+    for copy in copies:
+        copy.start()
+    for copy in copies:
+        copy.wait()
+    state, cell, dest, elem, weight = held
     column, hot_z = cell_keys(cell[...])
-    found = pick(state[0:3].reshape(192, 128), hot_z).reshape(3, 64, ROWS)
+    found = pick(state[...].reshape(192, 128), hot_z).reshape(3, 64, ROWS)
     sampled = [
         jnp.sum(jnp.where(column, found[c], 0.0), axis=0, keepdims=True) * weight[...]
         for c in range(3)
@@ -85,9 +96,8 @@
     out[...] = put(spread, hot_lane).reshape(32, 8, 128)
 
 
-def own_kernel(place, parts, motion, coef, out):
+def own_kernel(place, motion, coef, out):
     gx, gy = place[0], place[1]
-    total = jnp.sum(parts[...], axis=0)
     row = lax.broadcasted_iota(jnp.int32, (8, 128), 0)
     lane = lax.broadcasted_iota(jnp.int32, (8, 128), 1)
     level = row >> 1
@@ -98,7 +108,11 @@
     )
     moved = pltpu.roll(held, ((gx & 7) * 16 - gy * 16 + 128) & 127, 1)
     mine = ((lane >> 4) == (gx & 7)) & ((row & 1) == (gx >> 3))
-    total = total + jnp.where(mine, moved, 0.0)
+    out[...] = jnp.where(mine, moved, 0.0)
+
+
+def total_kernel(parts, own, out):
+    total = jnp.sum(parts[...], axis=0) + own[...]
     out[...] = jnp.broadcast_to(total[None], (16, 8, 128))
 
 
@@ -232,25 +246,37 @@
     weight = sample_weight.reshape(1, ROWS)
 
     xlo, xhi = swap(state[:, 6:8], state[:, 0:2], "gx")
-    partial = call(sample_kernel, f32(32, 8, 128), count=5)(state, cell, dest, elem, weight)
+    rows = pltpu.VMEM((1, ROWS), jnp.int32)
+    held = (
+        pltpu.VMEM((3, 8, 8, 128), jnp.float32),
+        rows,
+        rows,
+        rows,
+        pltpu.VMEM((1, ROWS), jnp.float32),
+        pltpu.SemaphoreType.DMA((5,)),
+    )
+    partial = call(sample_kernel, f32(32, 8, 128), held, count=5, space=pltpu.HBM)(
+        state, cell, dest, elem, weight
+    )
     partial = exchange(partial, PLANE)
-
+    own = call(own_kernel, f32(8, 128), smem=1, count=3)(
+        place, element_motion, element_coef.reshape(1, 128)
+    )
+    partial, own, xlo, xhi = lax.optimization_barrier((partial, own, xlo, xhi))
+
+    totals = call(total_kernel, f32(16, 8, 128), count=2)(partial, own)
+    totals = exchange(totals, "gx")
     wide = jnp.concatenate([xlo[:, 1:2], state, xhi[:, 0:1]], axis=1)
     ylo, yhi = swap(wide[:, :, 6:8], wide[:, :, 0:2], "gy")
-
-    totals = call(own_kernel, f32(16, 8, 128), smem=1, count=4)(
-        place, partial, element_motion, element_coef.reshape(1, 128)
-    )
-    totals = exchange(totals, "gx")
-
+    totals, ylo, yhi = lax.optimization_barrier((totals, ylo, yhi))
+
+    forces = call(force_kernel, f32(32, 8, 128), count=1)(totals)
+    forces = exchange(forces, PLANE)
     padded = pltpu.VMEM((4, 12, 16, 256), jnp.float32)
     zup, zdown = call(ends_kernel, (f32(2, 640), f32(2, 640)), (padded,), count=5)(
         state, xlo, xhi, ylo, yhi
     )
     zlo, zhi = swap(zup, zdown, "gz")
-
-    forces = call(force_kernel, f32(32, 8, 128), count=1)(totals)
-    forces = exchange(forces, PLANE)
 
     before = call(stencil_kernel, f32(4, 8, 8, 128), (padded,), smem=1, count=8)(
         place, state, xlo, xhi, ylo, yhi, zlo, zhi

time: 75.6 us -> 72.8 us (0.963)
  the two profiles are of different devices: /device:TPU:24 before, /device:TPU:1 now
where the time goes in v2:
time: 72.8 us; the launch traced here: 71.8 us
  starting transfers between devices  47.6 us (65%)
  waiting for transfers between devices  11.3 us (16%)
  Pallas kernels  6.9 us (9%)
  local copies, waits for them, and re-layouts  5.05 us (7%)
  between operations  0.86 us (1%)
    all_to_all x3, starting transfers between devices, exchange(): return lax.all_to_all(blocks, axes, split_axis=0, concat_axis=0, tiled=True)  26.5 us
    ppermute x6, starting transfers between devices, swap(): return (lax.ppermute(up, axis, forward), lax.ppermute(down, axis, backward))  21.1 us
    ppermute x6, waiting for transfers between devices, swap(): return (lax.ppermute(up, axis, forward), lax.ppermute(down, axis, backward))  5.68 us
    all_to_all x3, waiting for transfers between devices, exchange(): return lax.all_to_all(blocks, axes, split_axis=0, concat_axis=0, tiled=True)  5.66 us
    unnamed x26, local copies, waits for them, and re-layouts  4.34 us
    pallas_call x1, Pallas kernels, body(): call(spread_kernel, (f32(4, 8, 8, 128), f32(3, 8, 8, 128)), count=6)  1.57 us
    pallas_call x1, Pallas kernels, body(): call(sample_kernel, f32(32, 8, 128), held, count=5, space=pltpu.HBM)  1.54 us
  transfers between devices with their start and end apart: 9, of which 4 were waited for; matrix products, arithmetic and copies ran while one was open for 0% of the time, Pallas kernels for 3%

profile of v2, /device:TPU:1, one launch (start us, length us, event | category | flops | bytes accessed | tf_op | source)
XLA Modules:
  0.0 71.8 jit_solution(15490586906580174160)
XLA Ops:
  0.6 0.7 copy-done.4
  1.3 0.9 %copy-done = f32[4,8,8,128]{3,2,1,0:T(8,128)S(1)} copy-done((f32[4,8,8,128]{3,2,1,0:T(8,128)S(1)}, f32[4,8,8,128]{3,2,1,0:T(8,128)}, u32[]{:S(2)}) %copy-start) | copy-done | bytes 131096
  2.2 0.7 copy-done.5
  2.9 0.7 copy-done.7
  3.6 0.7 copy-done.9
  4.3 1.5 %shard_map.86 = f32[32,8,128]{2,1,0:T(8,128)} custom-call(f32[4,8,8,128]{3,2,1,0:T(8,128)S(1)} %copy-done, s32[1,1024]{1,0:T(1,128)S(1)} %bitcast.8, s32[1,1024]{1,0:T(1,128)S(1)} %bitcast.10, s32[1,1024]{1,0:T(1,128)S(1)} %bitcast.12, f32[1,1024]{1,0:T(1,128)S(1)} %bitcast.14), custom_call_target="tpu_custom_call" | custom-call | flops 2000000 | bytes 1000000 | tf_op jit(solution)/shard_map/pallas_call | solution.py:258
  5.8 10.6 %all-to-all-start = ((f32[32,8,128]{2,1,0:T(8,128)}), f32[32,8,128]{2,1,0:T(8,128)S(1)}, u32[]{:S(2)}, u32[]{:S(2)}) async-start(f32[32,8,128]{2,1,0:T(8,128)} %shard_map.86), calls=%async_computation | async-start | bytes 262144 | tf_op jit(solution)/shard_map/all_to_all | solution.py:238
  16.4 9.3 %collective-permute-start.1 = (f32[4,2,8,128]{3,2,1,0:T(8,128)S(1)}, f32[4,2,8,128]{3,2,1,0:T(8,128)S(1)}, u32[]{:S(2)}, u32[]{:S(2)}) collective-permute-start(f32[4,2,8,128]{3,2,1,0:T(8,128)S(1)} %get-tuple-element.22), channel_id=1, source_target_pairs={{32,0},{64,32},{96,64},{128,96},{160,128},{192,160},{224,192},{256... | collective-permute-start | bytes 98312 | tf_op jit(solution)/shard_map/ppermute | solution.py:234
  25.7 1.9 %collective-permute-start = (f32[4,2,8,128]{3,2,1,0:T(8,128)S(1)}, f32[4,2,8,128]{3,2,1,0:T(8,128)S(1)}, u32[]{:S(2)}, u32[]{:S(2)}) collective-permute-start(f32[4,2,8,128]{3,2,1,0:T(8,128)S(1)} %get-tuple-element.23), channel_id=1, source_target_pairs={{0,32},{32,64},{64,96},{96,128},{128,160},{160,192},{192,224},{224... | collective-permute-start | bytes 98312 | tf_op jit(solution)/shard_map/ppermute | solution.py:234
  27.7 0.0 copy-start.11
  27.7 0.1 pad_add_fusion.place
  27.8 0.6 copy-done.11
  28.4 0.1 copy-done.12
  28.4 0.6 shard_map.87.own
  29.0 2.6 %collective-permute-done.xlo = f32[4,2,8,128]{3,2,1,0:T(8,128)S(1)} collective-permute-done((f32[4,2,8,128]{3,2,1,0:T(8,128)S(1)}, f32[4,2,8,128]{3,2,1,0:T(8,128)S(1)}, u32[]{:S(2)}, u32[]{:S(2)}) %collective-permute-start) | collective-permute-done | bytes 32800 | tf_op jit(solution)/shard_map/ppermute | solution.py:234
  31.6 0.7 shard_map.88
  32.3 5.7 %all-to-all-start.1 = ((f32[16,8,128]{2,1,0:T(8,128)}), f32[16,8,128]{2,1,0:T(8,128)S(1)}, u32[]{:S(2)}, u32[]{:S(2)}) async-start(f32[16,8,128]{2,1,0:T(8,128)} %shard_map.88), calls=%async_computation.1 | async-start | bytes 131072 | tf_op jit(solution)/shard_map/all_to_all | solution.py:238
  38.0 0.7 slice-done
  38.8 1.8 %collective-permute-start.3 = (f32[4,10,2,128]{3,2,1,0:T(2,128)S(1)}, f32[4,10,2,128]{3,2,1,0:T(2,128)S(1)}, u32[]{:S(2)}, u32[]{:S(2)}) collective-permute-start(f32[4,10,2,128]{3,2,1,0:T(2,128)S(1)} %get-tuple-element.20), channel_id=1, source_target_pairs={{4,0},{8,4},{12,8},{16,12},{20,16},{24,20},{28,24},{0,28},{5,1},{9... | collective-permute-start | bytes 122888 | tf_op jit(solution)/shard_map/ppermute | solution.py:234
  40.5 1.4 %collective-permute-start.2 = (f32[4,10,2,128]{3,2,1,0:T(2,128)S(1)}, f32[4,10,2,128]{3,2,1,0:T(2,128)S(1)}, u32[]{:S(2)}, u32[]{:S(2)}) collective-permute-start(f32[4,10,2,128]{3,2,1,0:T(2,128)S(1)} %get-tuple-element.21), channel_id=1, source_target_pairs={{0,4},{4,8},{8,12},{12,16},{16,20},{20,24},{24,28},{28,0},{1,5},{5... | collective-permute-start | bytes 122888 | tf_op jit(solution)/shard_map/ppermute | solution.py:234
  42.0 2.0 %collective-permute-done.3.yhi = f32[4,10,2,128]{3,2,1,0:T(2,128)S(1)} collective-permute-done((f32[4,10,2,128]{3,2,1,0:T(2,128)S(1)}, f32[4,10,2,128]{3,2,1,0:T(2,128)S(1)}, u32[]{:S(2)}, u32[]{:S(2)}) %collective-permute-start.3) | collective-permute-done | bytes 40992 | tf_op jit(solution)/shard_map/ppermute | solution.py:234
  43.9 5.7 %all-to-all-done.1.parts = f32[16,8,128]{2,1,0:T(8,128)S(1)} async-done(((f32[16,8,128]{2,1,0:T(8,128)}), f32[16,8,128]{2,1,0:T(8,128)S(1)}, u32[]{:S(2)}, u32[]{:S(2)}) %all-to-all-start.1) | async-done | bytes 65568 | tf_op jit(solution)/shard_map/all_to_all | solution.py:238
  49.6 0.7 shard_map.89
  50.3 10.3 %all-to-all-start.2 = ((f32[32,8,128]{2,1,0:T(8,128)}), f32[32,8,128]{2,1,0:T(8,128)S(1)}, u32[]{:S(2)}, u32[]{:S(2)}) async-start(f32[32,8,128]{2,1,0:T(8,128)} %shard_map.89), calls=%async_computation.2 | async-start | bytes 262144 | tf_op jit(solution)/shard_map/all_to_all | solution.py:238
  60.6 0.4 shard_map.90
  61.0 3.3 %collective-permute-start.4 = (f32[2,640]{1,0:T(2,128)S(1)}, f32[2,640]{1,0:T(2,128)S(1)}, u32[]{:S(2)}, u32[]{:S(2)}) collective-permute-start(f32[2,640]{1,0:T(2,128)S(1)} %get-tuple-element.18), channel_id=1, source_target_pairs={{0,1},{1,2},{2,3},{3,0},{4,5},{5,6},{6,7},{7,4},{8,9},{9,10},{10,1... | collective-permute-start | bytes 15368 | tf_op jit(solution)/shard_map/ppermute | solution.py:234
  64.3 0.0 copy-start.8
  64.3 0.0 copy-start.10
  64.4 3.3 %collective-permute-start.5 = (f32[2,640]{1,0:T(2,128)S(1)}, f32[2,640]{1,0:T(2,128)S(1)}, u32[]{:S(2)}, u32[]{:S(2)}) collective-permute-start(f32[2,640]{1,0:T(2,128)S(1)} %get-tuple-element.19), channel_id=1, source_target_pairs={{1,0},{2,1},{3,2},{0,3},{5,4},{6,5},{7,6},{4,7},{9,8},{10,9},{11,1... | collective-permute-start | bytes 15368 | tf_op jit(solution)/shard_map/ppermute | solution.py:234
  67.7 1.1 %collective-permute-done.5.zhi = f32[2,640]{1,0:T(2,128)S(1)} collective-permute-done((f32[2,640]{1,0:T(2,128)S(1)}, f32[2,640]{1,0:T(2,128)S(1)}, u32[]{:S(2)}, u32[]{:S(2)}) %collective-permute-start.5) | collective-permute-done | bytes 5152 | tf_op jit(solution)/shard_map/ppermute | solution.py:234
  68.8 1.4 %shard_map.91.before = f32[4,8,8,128]{3,2,1,0:T(8,128)S(1)} custom-call(s32[3]{0:T(128)S(1)} %pad_add_fusion.place, f32[4,8,8,128]{3,2,1,0:T(8,128)S(1)} %copy-done.1, f32[4,2,8,128]{3,2,1,0:T(8,128)S(1)} %copy-done.3, f32[4,2,8,128]{3,2,1,0:T(8,128)S(1)} %collective-permute-done.1.xhi, f32[4,10,2,128]{3,2,1,0:T(2,128)S(1)} %collective-permute-done.2.ylo, ...), custom_call_target="tpu_custom_call" | custom-call | flops 2000000 | bytes 1000000 | tf_op jit(solution)/shard_map/pallas_call | solution.py:281
  70.3 1.6 %shard_map.92 = (f32[4,8,8,128]{3,2,1,0:T(8,128)}, f32[3,8,8,128]{3,2,1,0:T(8,128)}) custom-call(f32[32,8,128]{2,1,0:T(8,128)S(1)} %all-to-all-done.2.forces, s32[1,1024]{1,0:T(1,128)S(1)} %bitcast.9, s32[1,1024]{1,0:T(1,128)S(1)} %bitcast.11, s32[1,1024]{1,0:T(1,128)S(1)} %bitcast.13, f32[1,1024]{1,0:T(1,128)S(1)} %bitcast.15, ...), custom_call_target="tpu_custom_call" | custom-call | flops 2000000 | bytes 1000000 | tf_op jit(solution)/shard_map/pallas_call | solution.py:284
  (25 shorter events, 0.1 us)
Async XLA Ops:
  0.6 0.7 copy-start.4
  1.3 0.9 %copy-start = (f32[4,8,8,128]{3,2,1,0:T(8,128)S(1)}, f32[4,8,8,128]{3,2,1,0:T(8,128)}, u32[]{:S(2)}) copy-start(f32[4,8,8,128]{3,2,1,0:T(8,128)} %state.3) | copy-start | bytes 393220
  2.2 0.7 copy-start.5
  2.9 0.7 copy-start.7
  3.6 0.7 copy-start.9
  5.8 10.6 %copy-start.1 = (f32[4,8,8,128]{3,2,1,0:T(8,128)S(1)}, f32[4,8,8,128]{3,2,1,0:T(8,128)}, u32[]{:S(2)}) copy-start(f32[4,8,8,128]{3,2,1,0:T(8,128)} %state.3) | copy-start | bytes 393220
  5.8 25.8 %all-to-all-start = ((f32[32,8,128]{2,1,0:T(8,128)}), f32[32,8,128]{2,1,0:T(8,128)S(1)}, u32[]{:S(2)}, u32[]{:S(2)}) async-start(f32[32,8,128]{2,1,0:T(8,128)} %shard_map.86), calls=%async_computation | async-start | bytes 262144 | tf_op jit(solution)/shard_map/all_to_all | solution.py:238
  16.4 12.6 %collective-permute-start.1 = (f32[4,2,8,128]{3,2,1,0:T(8,128)S(1)}, f32[4,2,8,128]{3,2,1,0:T(8,128)S(1)}, u32[]{:S(2)}, u32[]{:S(2)}) collective-permute-start(f32[4,2,8,128]{3,2,1,0:T(8,128)S(1)} %get-tuple-element.22), channel_id=1, source_target_pairs={{32,0},{64,32},{96,64},{128,96},{160,128},{192,160},{224,192},{256... | collective-permute-start | bytes 98312 | tf_op jit(solution)/shard_map/ppermute | solution.py:234
  25.7 5.9 %collective-permute-start = (f32[4,2,8,128]{3,2,1,0:T(8,128)S(1)}, f32[4,2,8,128]{3,2,1,0:T(8,128)S(1)}, u32[]{:S(2)}, u32[]{:S(2)}) collective-permute-start(f32[4,2,8,128]{3,2,1,0:T(8,128)S(1)} %get-tuple-element.23), channel_id=1, source_target_pairs={{0,32},{32,64},{64,96},{96,128},{128,160},{160,192},{192,224},{224... | collective-permute-start | bytes 98312 | tf_op jit(solution)/shard_map/ppermute | solution.py:234
  27.7 0.7 copy-start.11
  27.8 0.7 copy-start.12
  31.6 6.4 %copy-start.2 = (f32[4,2,8,128]{3,2,1,0:T(8,128)}, f32[4,2,8,128]{3,2,1,0:T(8,128)S(1)}, u32[]{:S(2)}) copy-start(f32[4,2,8,128]{3,2,1,0:T(8,128)S(1)} %collective-permute-done.xlo) | copy-start | bytes 98308
  32.3 17.3 %all-to-all-start.1 = ((f32[16,8,128]{2,1,0:T(8,128)}), f32[16,8,128]{2,1,0:T(8,128)S(1)}, u32[]{:S(2)}, u32[]{:S(2)}) async-start(f32[16,8,128]{2,1,0:T(8,128)} %shard_map.88), calls=%async_computation.1 | async-start | bytes 131072 | tf_op jit(solution)/shard_map/all_to_all | solution.py:238
  38.0 0.7 %slice-start = ((f32[4,2,8,128]{3,2,1,0:T(8,128)}), f32[4,1,8,128]{3,2,1,0:T(8,128)S(1)}, s32[]{:S(2)}) async-start(f32[4,2,8,128]{3,2,1,0:T(8,128)} %copy-done.2), calls=%async_computation.3 | async-start | bytes 32768 | tf_op jit(solution)/shard_map/slice | solution.py:269
  38.8 5.2 %collective-permute-start.3 = (f32[4,10,2,128]{3,2,1,0:T(2,128)S(1)}, f32[4,10,2,128]{3,2,1,0:T(2,128)S(1)}, u32[]{:S(2)}, u32[]{:S(2)}) collective-permute-start(f32[4,10,2,128]{3,2,1,0:T(2,128)S(1)} %get-tuple-element.20), channel_id=1, source_target_pairs={{4,0},{8,4},{12,8},{16,12},{20,16},{24,20},{28,24},{0,28},{5,1},{9... | collective-permute-start | bytes 122888 | tf_op jit(solution)/shard_map/ppermute | solution.py:234
  40.5 3.4 %collective-permute-start.2 = (f32[4,10,2,128]{3,2,1,0:T(2,128)S(1)}, f32[4,10,2,128]{3,2,1,0:T(2,128)S(1)}, u32[]{:S(2)}, u32[]{:S(2)}) collective-permute-start(f32[4,10,2,128]{3,2,1,0:T(2,128)S(1)} %get-tuple-element.21), channel_id=1, source_target_pairs={{0,4},{4,8},{8,12},{12,16},{16,20},{20,24},{24,28},{28,0},{1,5},{5... | collective-permute-start | bytes 122888 | tf_op jit(solution)/shard_map/ppermute | solution.py:234
  50.3 10.3 %copy-start.3 = (f32[4,2,8,128]{3,2,1,0:T(8,128)S(1)}, f32[4,2,8,128]{3,2,1,0:T(8,128)}, u32[]{:S(2)}) copy-start(f32[4,2,8,128]{3,2,1,0:T(8,128)} %copy-done.2) | copy-start | bytes 98308
  50.3 20.0 %all-to-all-start.2 = ((f32[32,8,128]{2,1,0:T(8,128)}), f32[32,8,128]{2,1,0:T(8,128)S(1)}, u32[]{:S(2)}, u32[]{:S(2)}) async-start(f32[32,8,128]{2,1,0:T(8,128)} %shard_map.89), calls=%async_computation.2 | async-start | bytes 262144 | tf_op jit(solution)/shard_map/all_to_all | solution.py:238
  61.0 6.7 %collective-permute-start.4 = (f32[2,640]{1,0:T(2,128)S(1)}, f32[2,640]{1,0:T(2,128)S(1)}, u32[]{:S(2)}, u32[]{:S(2)}) collective-permute-start(f32[2,640]{1,0:T(2,128)S(1)} %get-tuple-element.18), channel_id=1, source_target_pairs={{0,1},{1,2},{2,3},{3,0},{4,5},{5,6},{6,7},{7,4},{8,9},{9,10},{10,1... | collective-permute-start | bytes 15368 | tf_op jit(solution)/shard_map/ppermute | solution.py:234
  64.3 5.9 %copy-start.6 = (s32[1024,1]{0,1:T(1,128)S(1)}, s32[1024,1]{0,1:T(1,128)}, u32[]{:S(2)}) copy-start(s32[1024,1]{0,1:T(1,128)} %param.9) | copy-start | bytes 12292
  64.3 5.9 %copy-start.8 = (s32[1024]{0:T(1024)S(1)}, s32[1024]{0:T(1024)}, u32[]{:S(2)}) copy-start(s32[1024]{0:T(1024)} %param.11) | copy-start | bytes 12292
  64.3 5.9 %copy-start.10 = (f32[1024]{0:T(1024)S(1)}, f32[1024]{0:T(1024)}, u32[]{:S(2)}) copy-start(f32[1024]{0:T(1024)} %param.10) | copy-start | bytes 12292
  64.4 4.5 %collective-permute-start.5 = (f32[2,640]{1,0:T(2,128)S(1)}, f32[2,640]{1,0:T(2,128)S(1)}, u32[]{:S(2)}, u32[]{:S(2)}) collective-permute-start(f32[2,640]{1,0:T(2,128)S(1)} %get-tuple-element.19), channel_id=1, source_target_pairs={{1,0},{2,1},{3,2},{0,3},{5,4},{6,5},{7,6},{4,7},{9,8},{10,9},{11,1... | collective-permute-start | bytes 15368 | tf_op jit(solution)/shard_map/ppermute | solution.py:234

commit v3 on v2

v3 whole, which is shorter than its diff:
```python
import jax
import jax.numpy as jnp
from jax import lax
from jax.experimental import pallas as pl
from jax.experimental.pallas import tpu as pltpu
from jax.sharding import PartitionSpec as P

DT_STEP = 0.4
BASE_COEF = 0.02
PRANDTL = 0.7
SMAG_COEF = 0.04

ROWS = 1024
PLANE = ("gy", "gz")


def call(kernel, outs, scratch=(), count=1, space=pltpu.VMEM, limit=24 * 1024 * 1024):
    return pl.pallas_call(
        kernel,
        out_shape=outs,
        in_specs=[pl.BlockSpec(memory_space=space)] * count,
        out_specs=jax.tree.map(lambda _: pl.BlockSpec(memory_space=pltpu.VMEM), outs),
        scratch_shapes=scratch,
        compiler_params=pltpu.CompilerParams(vmem_limit_bytes=limit),
        cost_estimate=pl.CostEstimate(
            flops=2_000_000, bytes_accessed=1_000_000, transcendentals=0
        ),
    )


def f32(*shape):
    return jax.ShapeDtypeStruct(shape, jnp.float32)


def halves(values):
    high = values.astype(jnp.bfloat16)
    return high, (values - high.astype(jnp.float32)).astype(jnp.bfloat16)


def onehot(index, size):
    wanted = lax.broadcasted_iota(jnp.int32, (size, ROWS), 0)
    return jnp.where(wanted == index, 1.0, 0.0).astype(jnp.bfloat16)


def pick(table, hot):
    both = jnp.concatenate(halves(table), axis=1)
    return jnp.dot(both, jnp.concatenate([hot, hot], axis=0), preferred_element_type=jnp.float32)


def put(values, hot):
    high, low = halves(values)
    dims = (((1,), (1,)), ((), ()))
    total = lax.dot_general(high, hot, dims, preferred_element_type=jnp.float32)
    return total + lax.dot_general(low, hot, dims, preferred_element_type=jnp.float32)


def cell_keys(cell):
    column = lax.broadcasted_iota(jnp.int32, (64, ROWS), 0) == (cell >> 7)
    return column, onehot(cell & 127, 128)


def element_keys(dest, elem):
    tile = (elem >> 4) * 4 + (dest & 3)
    along = dest >> 2
    number = tile * 2 + (along >> 3)
    shape = (32, 8, ROWS)
    row = lax.broadcasted_iota(jnp.int32, shape, 0) * 2 + (
        lax.broadcasted_iota(jnp.int32, shape, 1) & 1
    )
    return row == number[None], onehot((along & 7) * 16 + (elem & 15), 128)


def own_part(motion, coef):
    gx, gy = lax.axis_index("gx"), lax.axis_index("gy")
    row = lax.broadcasted_iota(jnp.int32, (8, 128), 0)
    lane = lax.broadcasted_iota(jnp.int32, (8, 128), 1)
    level = row >> 1
    held = jnp.where(
        level == 0,
        motion[0:1, :],
        jnp.where(level == 1, motion[1:2, :], jnp.where(level == 2, motion[2:3, :], coef[...])),
    )
    moved = pltpu.roll(held, ((gx & 7) * 16 - gy * 16 + 128) & 127, 1)
    mine = ((lane >> 4) == (gx & 7)) & ((row & 1) == (gx >> 3))
    return jnp.where(mine, moved, 0.0)


def sample_kernel(
    state_in, cell_in, dest_in, elem_in, weight_in, motion_in, coef_in, out, own, *scratch
):
    held, sems = scratch[:7], scratch[7]
    sources = (state_in.at[0:3], cell_in, dest_in, elem_in, weight_in, motion_in, coef_in)
    copies = [
        pltpu.make_async_copy(source, target, sems.at[i])
        for i, (source, target) in enumerate(zip(sources, held))
    ]
    for copy in copies:
        copy.start()
    for copy in copies:
        copy.wait()
    state, cell, dest, elem, weight, motion, coef = held
    own[...] = own_part(motion, coef)
    column, hot_z = cell_keys(cell[...])
    found = pick(state[...].reshape(192, 128), hot_z).reshape(3, 64, ROWS)
    sampled = [
        jnp.sum(jnp.where(column, found[c], 0.0), axis=0, keepdims=True) * weight[...]
        for c in range(3)
    ]
    row = lax.broadcasted_iota(jnp.int32, (8, ROWS), 0) >> 1
    pattern = jnp.where(
        row == 0, sampled[0], jnp.where(row == 1, sampled[1], jnp.where(row == 2, sampled[2], 0.0))
    )
    match, hot_lane = element_keys(dest[...], elem[...])
    spread = jnp.where(match, pattern[None], 0.0).reshape(256, ROWS)
    out[...] = put(spread, hot_lane).reshape(32, 8, 128)


def total_kernel(parts, own, out):
    total = jnp.sum(parts[...], axis=0) + own[...]
    out[...] = jnp.broadcast_to(total[None], (16, 8, 128))


def force_kernel(parts, packs, out):
    total = jnp.sum(parts[...], axis=0)
    row = lax.broadcasted_iota(jnp.int32, (8, 128), 0)

    def by_parity(values):
        values = values + pltpu.roll(values, 4, 0)
        return values + pltpu.roll(values, 2, 0)

    speed = jnp.sqrt(by_parity(jnp.where(row < 6, total * total, 0.0)))
    coef = by_parity(jnp.where(row < 6, 0.0, total))
    force = jnp.where(row < 6, -coef * speed * total, 0.0)
    out[:, 0:8] = jnp.broadcast_to(force[None], (32, 8, 128))
    above = (lax.axis_index("gz") + 1) & 3
    for level in range(4):
        pack = jnp.where(above == level, packs[1], packs[0])
        for across in range(8):
            out[4 * across + level, 8:16] = pack


def fill(grid, state, xlo, xhi, ylo, yhi):
    grid[:, 2:10, 0:8, 0:128] = state[...]
    grid[:, 0:2, 0:8, 0:128] = xlo[...]
    grid[:, 10:12, 0:8, 0:128] = xhi[...]
    grid[:, 1:11, 8:10, 0:128] = yhi[...]
    grid[:, 1:11, 14:16, 0:128] = ylo[...]


def lanes(count, places):
    row = lax.broadcasted_iota(jnp.int32, (count, 128), 0)
    lane = lax.broadcasted_iota(jnp.int32, (count, 128), 1)
    hot = (row == 0) & (lane == places[0])
    for i, place in enumerate(places[1:]):
        hot = hot | ((row == i + 1) & (lane == place))
    return jnp.where(hot, 1.0, 0.0)


def exact(left, right, dims):
    return lax.dot_general(
        left,
        right,
        ((dims, dims), ((), ())),
        precision=lax.Precision.HIGHEST,
        preferred_element_type=jnp.float32,
    )


def ends_kernel(state, xlo, xhi, ylo, yhi, packs, grid):
    grid[:, :, 8:16] = jnp.zeros((4, 12, 8, 128), jnp.float32)
    fill(grid, state, xlo, xhi, ylo, yhi)
    near = exact(lanes(8, (0, 127)), grid[:, 1:11].reshape(640, 128), (1,))
    far = exact(lanes(8, (1, 126)), state[...].reshape(256, 128), (1,))
    for side in range(2):
        pieces = [near[side : side + 1, 128 * i : 128 * i + 128] for i in range(5)]
        pieces += [far[side : side + 1, 128 * i : 128 * i + 128] for i in range(2)]
        packs[side] = jnp.concatenate(pieces + [jnp.zeros((1, 128), jnp.float32)], axis=0)


def unpack(high, low):
    def rows(pack, first, count):
        return jnp.concatenate([pack[i : i + 1] for i in range(first, first + count)], axis=1)

    near = jnp.concatenate([rows(high, 0, 5), rows(low, 0, 5)], axis=0)
    far = jnp.concatenate([rows(high, 5, 2), rows(low, 5, 2)], axis=0)
    near = exact(near, lanes(2, (0, 127)), (0,)).reshape(4, 10, 16, 128)
    return near, exact(far, lanes(2, (1, 126)), (0,)).reshape(4, 8, 8, 128)


def final_kernel(
    parts, cell, dest, elem, weight, state, xlo, xhi, ylo, yhi, new_state, body_force, grid
):
    match, hot_lane = element_keys(dest[...], elem[...])
    found = pick(parts[:, 0:8].reshape(256, 128), hot_lane).reshape(32, 8, ROWS)
    pairs = jnp.sum(jnp.where(match, found, 0.0), axis=0)
    column, hot_z = cell_keys(cell[...])
    each = [(pairs[2 * c : 2 * c + 1] + pairs[2 * c + 1 : 2 * c + 2]) * weight[...] for c in range(3)]
    spread = jnp.concatenate([jnp.where(column, each[c], 0.0) for c in range(3)], axis=0)
    body = put(spread, hot_z).reshape(3, 8, 8, 128)
    body_force[...] = body

    gy, gz = lax.axis_index("gy"), lax.axis_index("gz")
    fill(grid, state, xlo, xhi, ylo, yhi)
    near, far = unpack(parts[gy * 4 + ((gz + 1) & 3), 8:16], parts[gy * 4 + ((gz + 3) & 3), 8:16])
    level = lax.broadcasted_iota(jnp.int32, (1, 1, 256), 2)
    outside = ((level >= 128) & (level < 192) & (gz == 3)) | ((level >= 192) & (gz == 0))
    beyond = outside[:, :, 128:256][None]
    grid[:, 1:11, :, 128:256] = jnp.where(beyond, 0.0, near)
    grid[:, 2:10, 0:8, 128:256] += jnp.where(beyond, 0.0, far)

    def around(values):
        return (
            (pltpu.roll(values, 15, 1), pltpu.roll(values, 1, 1)),
            (pltpu.roll(values, 255, 2), pltpu.roll(values, 1, 2)),
        )

    fields = [grid[c] for c in range(4)]
    sides = []
    diffs = []
    for c in range(4):
        middle = fields[c][1:11]
        near = ((fields[c][2:12], fields[c][0:10]),) + around(middle)
        sides.append(near)
        diffs.append([upper - lower for upper, lower in near])
    strain = 0.5 * (
        diffs[0][0] * diffs[0][0] + diffs[1][1] * diffs[1][1] + diffs[2][2] * diffs[2][2]
    )
    for i, j in ((0, 1), (0, 2), (1, 2)):
        paired = diffs[i][j] + diffs[j][i]
        strain = strain + 0.25 * paired * paired
    eddy = jnp.where(outside, 0.0, SMAG_COEF * jnp.sqrt(strain))

    def inner(values):
        return values[:, 0:8, 0:128]

    centre = inner(eddy[1:9])
    near = ((eddy[2:10], eddy[0:8]),) + around(eddy[1:9])
    faces = [[0.5 * (centre + inner(side)) for side in pair] for pair in near]
    wind = [0.5 * inner(fields[c][2:10]) for c in range(3)]
    for c in range(4):
        middle = inner(fields[c][2:10])
        ratio = 1.0 if c < 3 else 1.0 / PRANDTL
        change = 0.0
        for j in range(3):
            upper, lower = [inner(side[1:9]) for side in sides[c][j]]
            change = change + (BASE_COEF + ratio * faces[j][0]) * (upper - middle)
            change = change - (BASE_COEF + ratio * faces[j][1]) * (middle - lower)
            change = change - wind[j] * (upper - lower)
        if c < 3:
            change = change + body[c]
        new_state[c] = middle + DT_STEP * change


def swap(up, down, axis):
    count = lax.axis_size(axis)
    forward = [(i, (i + 1) % count) for i in range(count)]
    backward = [(target, source) for source, target in forward]
    return lax.ppermute(up, axis, forward), lax.ppermute(down, axis, backward)


def exchange(blocks, axes):
    return lax.all_to_all(blocks, axes, split_axis=0, concat_axis=0, tiled=True)


def body(state, sample_cell, sample_dest, sample_weight, sample_elem, element_motion, element_coef):
    cell = sample_cell.reshape(1, ROWS)
    dest = sample_dest.reshape(1, ROWS)
    elem = sample_elem.reshape(1, ROWS)
    weight = sample_weight.reshape(1, ROWS)

    xlo, xhi = swap(state[:, 6:8], state[:, 0:2], "gx")
    coef = element_coef.reshape(1, 128)
    rows = pltpu.VMEM((1, ROWS), jnp.int32)
    held = (
        pltpu.VMEM((3, 8, 8, 128), jnp.float32),
        rows,
        rows,
        rows,
        pltpu.VMEM((1, ROWS), jnp.float32),
        pltpu.VMEM((3, 128), jnp.float32),
        pltpu.VMEM((1, 128), jnp.float32),
        pltpu.SemaphoreType.DMA((7,)),
    )
    partial, own = call(
        sample_kernel, (f32(32, 8, 128), f32(8, 128)), held, 7, pltpu.HBM, 60 * 1024 * 1024
    )(state, cell, dest, elem, weight, element_motion, coef)
    partial = exchange(partial, PLANE)
    partial, own, xlo, xhi = lax.optimization_barrier((partial, own, xlo, xhi))

    totals = call(total_kernel, f32(16, 8, 128), count=2)(partial, own)
    totals = exchange(totals, "gx")
    wide = jnp.concatenate([xlo[:, 1:2], state, xhi[:, 0:1]], axis=1)
    ylo, yhi = swap(wide[:, :, 6:8], wide[:, :, 0:2], "gy")
    ghosts = (xlo, xhi, ylo, yhi)
    packs = call(ends_kernel, f32(2, 8, 128), (pltpu.VMEM((4, 12, 16, 128), jnp.float32),), 5)(
        state, *ghosts
    )

    forces = call(force_kernel, f32(32, 16, 128), count=2)(totals, packs)
    forces = exchange(forces, PLANE)
    grid = pltpu.VMEM((4, 12, 16, 256), jnp.float32)
    return call(final_kernel, (f32(4, 8, 8, 128), f32(3, 8, 8, 128)), (grid,), 10)(
        forces, cell, dest, elem, weight, state, *ghosts
    )


def solution(mesh):
    return jax.shard_map(
        body,
        mesh=mesh,
        in_specs=(
            P(None, "gx", "gy", "gz"),
            P(("gx", "gy", "gz")),
            P(("gx", "gy", "gz"), None),
            P(("gx", "gy", "gz")),
            P(("gx", "gy", "gz")),
            P(None, ("gx", "gz")),
            P(("gx", "gz")),
        ),
        out_specs=(P(None, "gx", "gy", "gz"), P(None, "gx", "gy", "gz")),
        check_vma=False,
    )
```

time: 72.8 us -> 68.4 us (0.940)
  blocking collectives: 0 us -> 18.9 us
  starting transfers between devices: 47.6 us -> 30.7 us
  local copies, waits for them, and re-layouts: 5.05 us -> 0.76 us
  Pallas kernels: 6.9 us -> 5.76 us
    all_to_all x0 -> x1, blocking collectives: none -> 18.9 us  [exchange(): return lax.all_to_all(blocks, axes, split_axis=0, concat_axis=0, tiled=True)]
    all_to_all x3 -> x2, starting transfers between devices: 26.5 us -> 16.3 us  [exchange(): return lax.all_to_all(blocks, axes, split_axis=0, concat_axis=0, tiled=True)]
    ppermute x6 -> x4, starting transfers between devices: 21.1 us -> 14.4 us  [swap(): return (lax.ppermute(up, axis, forward), lax.ppermute(down, axis, backward))]
    unnamed x26 -> x16, local copies, waits for them, and re-layouts: 4.34 us -> 0.05 us
    pallas_call x6 -> x4, Pallas kernels: 6.23 us -> 5.09 us  [the longest x1 2.35 us: body(): call(sample_kernel, (f32(32, 8, 128), f32(8, 128)), held, 7, pltpu.HBM, 6...]
    all_to_all x3 -> x2, waiting for transfers between devices: 5.66 us -> 5.11 us  [exchange(): return lax.all_to_all(blocks, axes, split_axis=0, concat_axis=0, tiled=True)]
    ppermute x6 -> x4, waiting for transfers between devices: 5.68 us -> 5.89 us  [swap(): return (lax.ppermute(up, axis, forward), lax.ppermute(down, axis, backward))]
  transfers between devices with their start and end apart: 9 -> 6, of which waited for: 4 -> 3; matrix products, arithmetic and copies ran while one was open for 0% -> 0% of each run, Pallas kernels for 3% -> 1%
where the time goes in v3:
time: 68.4 us; the launch traced here: 67.9 us
  starting transfers between devices  30.7 us (45%)
  blocking collectives  18.9 us (28%)
  waiting for transfers between devices  11 us (16%)
  Pallas kernels  5.76 us (8%)
  between operations  0.8 us (1%)
  local copies, waits for them, and re-layouts  0.76 us (1%)
    all_to_all x1, blocking collectives, exchange(): return lax.all_to_all(blocks, axes, split_axis=0, concat_axis=0, tiled=True)  18.9 us
    all_to_all x2, starting transfers between devices, exchange(): return lax.all_to_all(blocks, axes, split_axis=0, concat_axis=0, tiled=True)  16.3 us
    ppermute x4, starting transfers between devices, swap(): return (lax.ppermute(up, axis, forward), lax.ppermute(down, axis, backward))  14.4 us
    ppermute x4, waiting for transfers between devices, swap(): return (lax.ppermute(up, axis, forward), lax.ppermute(down, axis, backward))  5.89 us
    all_to_all x2, waiting for transfers between devices, exchange(): return lax.all_to_all(blocks, axes, split_axis=0, concat_axis=0, tiled=True)  5.11 us
    pallas_call x1, Pallas kernels, body(): call(sample_kernel, (f32(32, 8, 128), f32(8, 128)), held, 7, pltpu.HBM, 6...  2.35 us
    pallas_call x1, Pallas kernels, body(): call(final_kernel, (f32(4, 8, 8, 128), f32(3, 8, 8, 128)), (grid,), 10)  2.17 us
  transfers between devices with their start and end apart: 6, of which 3 were waited for; matrix products, arithmetic and copies ran while one was open for 0% of the time, Pallas kernels for 1%

profile of v3, /device:TPU:1, one launch (start us, length us, event | category | flops | bytes accessed | tf_op | source)
XLA Modules:
  0.0 67.9 jit_solution(10419338343871514653)
XLA Ops:
  0.6 2.3 %shard_map.86 = (f32[32,8,128]{2,1,0:T(8,128)}, f32[8,128]{1,0:T(8,128)}) custom-call(f32[4,8,8,128]{3,2,1,0:T(8,128)} %state.3, s32[1,1024]{1,0:T(1,128)} %bitcast.5, s32[1,1024]{1,0:T(1,128)} %bitcast.7, s32[1,1024]{1,0:T(1,128)} %bitcast.9, f32[1,1024]{1,0:T(1,128)} %bitcast.11, f32[3,128]{1,0:T(4,128)} %motion_in.1, f32[1,128]{1,0:T(1,128)} %bitcast.13), custom_call_target="tpu_custom_call" | custom-call | flops 2000000 | bytes 1000000 | tf_op jit(solution)/shard_map/pallas_call | solution.py:284
  3.0 0.0 copy-start
  3.0 10.6 %all-to-all-start = ((f32[32,8,128]{2,1,0:T(8,128)}), f32[32,8,128]{2,1,0:T(8,128)S(1)}, u32[]{:S(2)}, u32[]{:S(2)}) async-start(f32[32,8,128]{2,1,0:T(8,128)} %get-tuple-element.8), calls=%async_computation | async-start | bytes 262144 | tf_op jit(solution)/shard_map/all_to_all | solution.py:262
  13.6 0.0 copy-done
  13.6 0.0 copy-start.7
  13.6 9.3 %collective-permute-start.1 = (f32[4,2,8,128]{3,2,1,0:T(8,128)S(1)}, f32[4,2,8,128]{3,2,1,0:T(8,128)S(1)}, u32[]{:S(2)}, u32[]{:S(2)}) collective-permute-start(f32[4,2,8,128]{3,2,1,0:T(8,128)S(1)} %get-tuple-element.16), channel_id=1, source_target_pairs={{32,0},{64,32},{96,64},{128,96},{160,128},{192,160},{224,192},{256... | collective-permute-start | bytes 98312 | tf_op jit(solution)/shard_map/ppermute | solution.py:258
  22.9 1.9 %collective-permute-start = (f32[4,2,8,128]{3,2,1,0:T(8,128)S(1)}, f32[4,2,8,128]{3,2,1,0:T(8,128)S(1)}, u32[]{:S(2)}, u32[]{:S(2)}) collective-permute-start(f32[4,2,8,128]{3,2,1,0:T(8,128)S(1)} %get-tuple-element.17), channel_id=1, source_target_pairs={{0,32},{32,64},{64,96},{96,128},{128,160},{160,192},{192,224},{224... | collective-permute-start | bytes 98312 | tf_op jit(solution)/shard_map/ppermute | solution.py:258
  24.8 0.0 collective-permute-done.1.xhi
  24.8 3.9 %collective-permute-done.xlo = f32[4,2,8,128]{3,2,1,0:T(8,128)S(1)} collective-permute-done((f32[4,2,8,128]{3,2,1,0:T(8,128)S(1)}, f32[4,2,8,128]{3,2,1,0:T(8,128)S(1)}, u32[]{:S(2)}, u32[]{:S(2)}) %collective-permute-start) | collective-permute-done | bytes 32800 | tf_op jit(solution)/shard_map/ppermute | solution.py:258
  28.8 0.0 all-to-all-done.parts
  28.8 0.0 copy-done.7
  28.8 0.7 shard_map.87
  29.5 5.7 %all-to-all-start.1 = ((f32[16,8,128]{2,1,0:T(8,128)}), f32[16,8,128]{2,1,0:T(8,128)S(1)}, u32[]{:S(2)}, u32[]{:S(2)}) async-start(f32[16,8,128]{2,1,0:T(8,128)} %shard_map.87), calls=%async_computation.1 | async-start | bytes 131072 | tf_op jit(solution)/shard_map/all_to_all | solution.py:262
  35.2 0.0 copy-done.1
  35.2 0.0 slice-start
  35.2 0.7 %slice-done = f32[4,1,8,128]{3,2,1,0:T(8,128)S(1)} async-done(((f32[4,2,8,128]{3,2,1,0:T(8,128)}), f32[4,1,8,128]{3,2,1,0:T(8,128)S(1)}, s32[]{:S(2)}) %slice-start) | async-done | bytes 16408 | tf_op jit(solution)/shard_map/slice | solution.py:292
  35.9 1.8 %collective-permute-start.3 = (f32[4,10,2,128]{3,2,1,0:T(2,128)S(1)}, f32[4,10,2,128]{3,2,1,0:T(2,128)S(1)}, u32[]{:S(2)}, u32[]{:S(2)}) collective-permute-start(f32[4,10,2,128]{3,2,1,0:T(2,128)S(1)} %get-tuple-element.14), channel_id=1, source_target_pairs={{4,0},{8,4},{12,8},{16,12},{20,16},{24,20},{28,24},{0,28},{5,1},{9... | collective-permute-start | bytes 122888 | tf_op jit(solution)/shard_map/ppermute | solution.py:258
  37.7 1.4 %collective-permute-start.2 = (f32[4,10,2,128]{3,2,1,0:T(2,128)S(1)}, f32[4,10,2,128]{3,2,1,0:T(2,128)S(1)}, u32[]{:S(2)}, u32[]{:S(2)}) collective-permute-start(f32[4,10,2,128]{3,2,1,0:T(2,128)S(1)} %get-tuple-element.15), channel_id=1, source_target_pairs={{0,4},{4,8},{8,12},{12,16},{16,20},{20,24},{24,28},{28,0},{1,5},{5... | collective-permute-start | bytes 122888 | tf_op jit(solution)/shard_map/ppermute | solution.py:258
  39.1 2.0 %collective-permute-done.3.yhi = f32[4,10,2,128]{3,2,1,0:T(2,128)S(1)} collective-permute-done((f32[4,10,2,128]{3,2,1,0:T(2,128)S(1)}, f32[4,10,2,128]{3,2,1,0:T(2,128)S(1)}, u32[]{:S(2)}, u32[]{:S(2)}) %collective-permute-start.3) | collective-permute-done | bytes 40992 | tf_op jit(solution)/shard_map/ppermute | solution.py:258
  41.1 0.0 collective-permute-done.2.ylo
  41.1 0.0 copy-done.2
  41.1 0.5 shard_map.88.packs
  41.6 5.1 %all-to-all-done.1.parts = f32[16,8,128]{2,1,0:T(8,128)S(1)} async-done(((f32[16,8,128]{2,1,0:T(8,128)}), f32[16,8,128]{2,1,0:T(8,128)S(1)}, u32[]{:S(2)}, u32[]{:S(2)}) %all-to-all-start.1) | async-done | bytes 65568 | tf_op jit(solution)/shard_map/all_to_all | solution.py:262
  46.8 0.0 copy-start.3
  46.8 0.0 copy-start.4
  46.8 0.0 copy-start.5
  46.8 0.0 copy-start.6
  46.8 18.9 %all_to_all.15.parts = f32[32,16,128]{2,1,0:T(8,128)S(1)} all-to-all(f32[32,16,128]{2,1,0:T(8,128)S(1)} %shard_map.89), channel_id=1, replica_groups=mesh['gx'=16,'gy'=8,'gz'=4] {'gy','gz'}, dimensions={0} | all-to-all | bytes 524288 | tf_op jit(solution)/shard_map/all_to_all | solution.py:262
  65.7 0.0 copy-done.3
  65.7 0.0 copy-done.4
  65.7 0.0 copy-done.5
  65.7 2.2 %shard_map.90 = (f32[4,8,8,128]{3,2,1,0:T(8,128)}, f32[3,8,8,128]{3,2,1,0:T(8,128)}) custom-call(f32[32,16,128]{2,1,0:T(8,128)S(1)} %all_to_all.15.parts, s32[1,1024]{1,0:T(1,128)S(1)} %bitcast.6, s32[1,1024]{1,0:T(1,128)S(1)} %bitcast.8, s32[1,1024]{1,0:T(1,128)S(1)} %bitcast.10, f32[1,1024]{1,0:T(1,128)S(1)} %bitcast.12, f32[4,8,8,128]{3,2,1,0:T(8,128)S(1)} %copy-done, ...), custom_call_target="tpu_custom_call" | custom-call | flops 2000000 | bytes 1000000 | tf_op jit(solution)/shard_map/pallas_call | solution.py:302
  (7 shorter events, 0.1 us)
Async XLA Ops:
  3.0 10.6 %copy-start = (f32[4,8,8,128]{3,2,1,0:T(8,128)S(1)}, f32[4,8,8,128]{3,2,1,0:T(8,128)}, u32[]{:S(2)}) copy-start(f32[4,8,8,128]{3,2,1,0:T(8,128)} %state.3) | copy-start | bytes 393220
  3.0 25.8 %all-to-all-start = ((f32[32,8,128]{2,1,0:T(8,128)}), f32[32,8,128]{2,1,0:T(8,128)S(1)}, u32[]{:S(2)}, u32[]{:S(2)}) async-start(f32[32,8,128]{2,1,0:T(8,128)} %get-tuple-element.8), calls=%async_computation | async-start | bytes 262144 | tf_op jit(solution)/shard_map/all_to_all | solution.py:262
  13.6 15.2 %copy-start.7 = (f32[8,128]{1,0:T(8,128)S(1)}, f32[8,128]{1,0:T(8,128)}, u32[]{:S(2)}) copy-start(f32[8,128]{1,0:T(8,128)} %get-tuple-element.11.own) | copy-start | bytes 12292
  13.6 11.2 %collective-permute-start.1 = (f32[4,2,8,128]{3,2,1,0:T(8,128)S(1)}, f32[4,2,8,128]{3,2,1,0:T(8,128)S(1)}, u32[]{:S(2)}, u32[]{:S(2)}) collective-permute-start(f32[4,2,8,128]{3,2,1,0:T(8,128)S(1)} %get-tuple-element.16), channel_id=1, source_target_pairs={{32,0},{64,32},{96,64},{128,96},{160,128},{192,160},{224,192},{256... | collective-permute-start | bytes 98312 | tf_op jit(solution)/shard_map/ppermute | solution.py:258
  22.9 5.9 %collective-permute-start = (f32[4,2,8,128]{3,2,1,0:T(8,128)S(1)}, f32[4,2,8,128]{3,2,1,0:T(8,128)S(1)}, u32[]{:S(2)}, u32[]{:S(2)}) collective-permute-start(f32[4,2,8,128]{3,2,1,0:T(8,128)S(1)} %get-tuple-element.17), channel_id=1, source_target_pairs={{0,32},{32,64},{64,96},{96,128},{128,160},{160,192},{192,224},{224... | collective-permute-start | bytes 98312 | tf_op jit(solution)/shard_map/ppermute | solution.py:258
  28.8 6.4 %copy-start.1 = (f32[4,2,8,128]{3,2,1,0:T(8,128)}, f32[4,2,8,128]{3,2,1,0:T(8,128)S(1)}, u32[]{:S(2)}) copy-start(f32[4,2,8,128]{3,2,1,0:T(8,128)S(1)} %collective-permute-done.xlo) | copy-start | bytes 98308
  29.5 17.3 %all-to-all-start.1 = ((f32[16,8,128]{2,1,0:T(8,128)}), f32[16,8,128]{2,1,0:T(8,128)S(1)}, u32[]{:S(2)}, u32[]{:S(2)}) async-start(f32[16,8,128]{2,1,0:T(8,128)} %shard_map.87), calls=%async_computation.1 | async-start | bytes 131072 | tf_op jit(solution)/shard_map/all_to_all | solution.py:262
  35.2 0.7 %slice-start = ((f32[4,2,8,128]{3,2,1,0:T(8,128)}), f32[4,1,8,128]{3,2,1,0:T(8,128)S(1)}, s32[]{:S(2)}) async-start(f32[4,2,8,128]{3,2,1,0:T(8,128)} %copy-done.1), calls=%async_computation.3 | async-start | bytes 32768 | tf_op jit(solution)/shard_map/slice | solution.py:292
  35.9 5.2 %copy-start.2 = (f32[4,2,8,128]{3,2,1,0:T(8,128)S(1)}, f32[4,2,8,128]{3,2,1,0:T(8,128)}, u32[]{:S(2)}) copy-start(f32[4,2,8,128]{3,2,1,0:T(8,128)} %copy-done.1) | copy-start | bytes 98308
  35.9 5.2 %collective-permute-start.3 = (f32[4,10,2,128]{3,2,1,0:T(2,128)S(1)}, f32[4,10,2,128]{3,2,1,0:T(2,128)S(1)}, u32[]{:S(2)}, u32[]{:S(2)}) collective-permute-start(f32[4,10,2,128]{3,2,1,0:T(2,128)S(1)} %get-tuple-element.14), channel_id=1, source_target_pairs={{4,0},{8,4},{12,8},{16,12},{20,16},{24,20},{28,24},{0,28},{5,1},{9... | collective-permute-start | bytes 122888 | tf_op jit(solution)/shard_map/ppermute | solution.py:258
  37.7 3.4 %collective-permute-start.2 = (f32[4,10,2,128]{3,2,1,0:T(2,128)S(1)}, f32[4,10,2,128]{3,2,1,0:T(2,128)S(1)}, u32[]{:S(2)}, u32[]{:S(2)}) collective-permute-start(f32[4,10,2,128]{3,2,1,0:T(2,128)S(1)} %get-tuple-element.15), channel_id=1, source_target_pairs={{0,4},{4,8},{8,12},{12,16},{16,20},{20,24},{24,28},{28,0},{1,5},{5... | collective-permute-start | bytes 122888 | tf_op jit(solution)/shard_map/ppermute | solution.py:258
  46.8 18.9 %copy-start.3 = (s32[1024]{0:T(1024)S(1)}, s32[1024]{0:T(1024)}, u32[]{:S(2)}) copy-start(s32[1024]{0:T(1024)} %param.8) | copy-start | bytes 12292
  46.8 18.9 %copy-start.4 = (s32[1024,1]{0,1:T(1,128)S(1)}, s32[1024,1]{0,1:T(1,128)}, u32[]{:S(2)}) copy-start(s32[1024,1]{0,1:T(1,128)} %param.9) | copy-start | bytes 12292
  46.8 18.9 %copy-start.5 = (s32[1024]{0:T(1024)S(1)}, s32[1024]{0:T(1024)}, u32[]{:S(2)}) copy-start(s32[1024]{0:T(1024)} %param.11) | copy-start | bytes 12292
  46.8 18.9 %copy-start.6 = (f32[1024]{0:T(1024)S(1)}, f32[1024]{0:T(1024)}, u32[]{:S(2)}) copy-start(f32[1024]{0:T(1024)} %param.10) | copy-start | bytes 12292

commit v4 on v3

--- a/solution.py
+++ b/solution.py
@@ -85,11 +85,41 @@
     return jnp.where(mine, moved, 0.0)
 
 
+def lanes(count, places):
+    row = lax.broadcasted_iota(jnp.int32, (count, 128), 0)
+    lane = lax.broadcasted_iota(jnp.int32, (count, 128), 1)
+    hot = (row == 0) & (lane == places[0])
+    for i, place in enumerate(places[1:]):
+        hot = hot | ((row == i + 1) & (lane == place))
+    return jnp.where(hot, 1.0, 0.0)
+
+
+def exact(left, right, dims):
+    return lax.dot_general(
+        left,
+        right,
+        ((dims, dims), ((), ())),
+        precision=lax.Precision.HIGHEST,
+        preferred_element_type=jnp.float32,
+    )
+
+
 def sample_kernel(
-    state_in, cell_in, dest_in, elem_in, weight_in, motion_in, coef_in, out, own, *scratch
+    state_in,
+    cell_in,
+    dest_in,
+    elem_in,
+    weight_in,
+    motion_in,
+    coef_in,
+    out,
+    own,
+    yup,
+    ydown,
+    *scratch,
 ):
     held, sems = scratch[:7], scratch[7]
-    sources = (state_in.at[0:3], cell_in, dest_in, elem_in, weight_in, motion_in, coef_in)
+    sources = (state_in, cell_in, dest_in, elem_in, weight_in, motion_in, coef_in)
     copies = [
         pltpu.make_async_copy(source, target, sems.at[i])
         for i, (source, target) in enumerate(zip(sources, held))
@@ -100,8 +130,13 @@
         copy.wait()
     state, cell, dest, elem, weight, motion, coef = held
     own[...] = own_part(motion, coef)
+    yup[...] = state[:, :, 6:8]
+    ydown[...] = state[:, :, 0:2]
+    ends = exact(lanes(8, (0, 127, 1, 126)), state[...].reshape(256, 128), (1,))
+    pack = [ends[i : i + 1, 128 * j : 128 * j + 128] for i in range(4) for j in range(2)]
+    out[:, 8:16] = jnp.broadcast_to(jnp.concatenate(pack, axis=0)[None], (32, 8, 128))
     column, hot_z = cell_keys(cell[...])
-    found = pick(state[...].reshape(192, 128), hot_z).reshape(3, 64, ROWS)
+    found = pick(state[0:3].reshape(192, 128), hot_z).reshape(3, 64, ROWS)
     sampled = [
         jnp.sum(jnp.where(column, found[c], 0.0), axis=0, keepdims=True) * weight[...]
         for c in range(3)
@@ -112,15 +147,15 @@
     )
     match, hot_lane = element_keys(dest[...], elem[...])
     spread = jnp.where(match, pattern[None], 0.0).reshape(256, ROWS)
-    out[...] = put(spread, hot_lane).reshape(32, 8, 128)
+    out[:, 0:8] = put(spread, hot_lane).reshape(32, 8, 128)
 
 
 def total_kernel(parts, own, out):
-    total = jnp.sum(parts[...], axis=0) + own[...]
+    total = jnp.sum(parts[:, 0:8], axis=0) + own[...]
     out[...] = jnp.broadcast_to(total[None], (16, 8, 128))
 
 
-def force_kernel(parts, packs, out):
+def force_kernel(parts, out):
     total = jnp.sum(parts[...], axis=0)
     row = lax.broadcasted_iota(jnp.int32, (8, 128), 0)
 
@@ -131,67 +166,66 @@
     speed = jnp.sqrt(by_parity(jnp.where(row < 6, total * total, 0.0)))
     coef = by_parity(jnp.where(row < 6, 0.0, total))
     force = jnp.where(row < 6, -coef * speed * total, 0.0)
-    out[:, 0:8] = jnp.broadcast_to(force[None], (32, 8, 128))
-    above = (lax.axis_index("gz") + 1) & 3
-    for level in range(4):
-        pack = jnp.where(above == level, packs[1], packs[0])
-        for across in range(8):
-            out[4 * across + level, 8:16] = pack
-
-
-def fill(grid, state, xlo, xhi, ylo, yhi):
+    out[...] = jnp.broadcast_to(force[None], (32, 8, 128))
+
+
+def fill(grid, state, ylo, yhi, ghosts, first, second):
     grid[:, 2:10, 0:8, 0:128] = state[...]
-    grid[:, 0:2, 0:8, 0:128] = xlo[...]
-    grid[:, 10:12, 0:8, 0:128] = xhi[...]
-    grid[:, 1:11, 8:10, 0:128] = yhi[...]
-    grid[:, 1:11, 14:16, 0:128] = ylo[...]
-
-
-def lanes(count, places):
-    row = lax.broadcasted_iota(jnp.int32, (count, 128), 0)
-    lane = lax.broadcasted_iota(jnp.int32, (count, 128), 1)
-    hot = (row == 0) & (lane == places[0])
-    for i, place in enumerate(places[1:]):
-        hot = hot | ((row == i + 1) & (lane == place))
-    return jnp.where(hot, 1.0, 0.0)
-
-
-def exact(left, right, dims):
-    return lax.dot_general(
-        left,
-        right,
-        ((dims, dims), ((), ())),
-        precision=lax.Precision.HIGHEST,
-        preferred_element_type=jnp.float32,
-    )
-
-
-def ends_kernel(state, xlo, xhi, ylo, yhi, packs, grid):
-    grid[:, :, 8:16] = jnp.zeros((4, 12, 8, 128), jnp.float32)
-    fill(grid, state, xlo, xhi, ylo, yhi)
-    near = exact(lanes(8, (0, 127)), grid[:, 1:11].reshape(640, 128), (1,))
-    far = exact(lanes(8, (1, 126)), state[...].reshape(256, 128), (1,))
-    for side in range(2):
-        pieces = [near[side : side + 1, 128 * i : 128 * i + 128] for i in range(5)]
-        pieces += [far[side : side + 1, 128 * i : 128 * i + 128] for i in range(2)]
-        packs[side] = jnp.concatenate(pieces + [jnp.zeros((1, 128), jnp.float32)], axis=0)
-
-
-def unpack(high, low):
-    def rows(pack, first, count):
-        return jnp.concatenate([pack[i : i + 1] for i in range(first, first + count)], axis=1)
-
-    near = jnp.concatenate([rows(high, 0, 5), rows(low, 0, 5)], axis=0)
-    far = jnp.concatenate([rows(high, 5, 2), rows(low, 5, 2)], axis=0)
-    near = exact(near, lanes(2, (0, 127)), (0,)).reshape(4, 10, 16, 128)
-    return near, exact(far, lanes(2, (1, 126)), (0,)).reshape(4, 8, 8, 128)
+    grid[:, 2:10, 8:10, 0:128] = yhi[...]
+    grid[:, 2:10, 14:16, 0:128] = ylo[...]
+    grid[:, 2:10, :, 128:256] = ghosts[...]
+    even = (lax.axis_index("gx") & 1) == 0
+    for plane, near, slab in (
+        (0, 1, jnp.where(even, second[...], first[...])),
+        (10, 10, jnp.where(even, first[...], second[...])),
+    ):
+        grid[:, plane : plane + 2, 0:8, 0:128] = slab[:, 0:2]
+        grid[:, near, 8:16, 0:128] = slab[:, 2]
+        grid[:, near, 0:8, 128:256] = slab[:, 3]
+
+
+def faces_kernel(parts, state, ylo, yhi, first, second, ghosts):
+    gx, gy, gz = [lax.axis_index(axis) for axis in ("gx", "gy", "gz")]
+    lane = lax.broadcasted_iota(jnp.int32, (1, 256), 1)
+
+    def rows(across, up, top):
+        pack = parts[((gy + across) & 7) * 4 + ((gz + (1 if up else 3)) & 3), 8:16]
+        found = jnp.concatenate([pack[top : top + 1], pack[top + 1 : top + 2]], axis=1)
+        return jnp.where(gz == (3 if up else 0), 0.0, found)
+
+    def edge(up, top):
+        y = lane & 7
+        beside = jnp.where(y == 0, rows(1, up, top), 0.0)
+        return jnp.where(y == 7, rows(7, up, top), beside)
+
+    inner = jnp.concatenate(
+        [rows(0, True, 0), rows(0, False, 2), rows(0, True, 4), rows(0, False, 6)], axis=0
+    )
+    inner = exact(inner, lanes(4, (0, 127, 1, 126)), (0,)).reshape(4, 8, 8, 128)
+    edges = jnp.concatenate([edge(True, 0), edge(False, 2)], axis=0)
+    ghosts[:, :, 0:8] = inner
+    ghosts[:, :, 8:16] = exact(edges, lanes(2, (0, 127)), (0,)).reshape(4, 8, 8, 128)
+
+    even = (gx & 1) == 0
+    row = lax.broadcasted_iota(jnp.int32, (1, 8, 128), 1)
+
+    def slab(x, near):
+        beside = jnp.where(
+            row == 0, yhi[:, near, 0:1], jnp.where(row == 7, ylo[:, near, 1:2], 0.0)
+        )
+        return [state[:, x], state[:, x + 1], beside, inner[:, near]]
+
+    for i, (high, low) in enumerate(zip(slab(6, 7), slab(0, 0))):
+        first[:, i] = jnp.where(even, high, low)
+        second[:, i] = jnp.where(even, low, high)
 
 
 def final_kernel(
-    parts, cell, dest, elem, weight, state, xlo, xhi, ylo, yhi, new_state, body_force, grid
+    parts, cell, dest, elem, weight, state, ylo, yhi, ghosts, first, second, *results
 ):
+    new_state, body_force, grid = results
     match, hot_lane = element_keys(dest[...], elem[...])
-    found = pick(parts[:, 0:8].reshape(256, 128), hot_lane).reshape(32, 8, ROWS)
+    found = pick(parts[...].reshape(256, 128), hot_lane).reshape(32, 8, ROWS)
     pairs = jnp.sum(jnp.where(match, found, 0.0), axis=0)
     column, hot_z = cell_keys(cell[...])
     each = [(pairs[2 * c : 2 * c + 1] + pairs[2 * c + 1 : 2 * c + 2]) * weight[...] for c in range(3)]
@@ -199,14 +233,10 @@
     body = put(spread, hot_z).reshape(3, 8, 8, 128)
     body_force[...] = body
 
-    gy, gz = lax.axis_index("gy"), lax.axis_index("gz")
-    fill(grid, state, xlo, xhi, ylo, yhi)
-    near, far = unpack(parts[gy * 4 + ((gz + 1) & 3), 8:16], parts[gy * 4 + ((gz + 3) & 3), 8:16])
+    gz = lax.axis_index("gz")
+    fill(grid, state, ylo, yhi, ghosts, first, second)
     level = lax.broadcasted_iota(jnp.int32, (1, 1, 256), 2)
     outside = ((level >= 128) & (level < 192) & (gz == 3)) | ((level >= 192) & (gz == 0))
-    beyond = outside[:, :, 128:256][None]
-    grid[:, 1:11, :, 128:256] = jnp.where(beyond, 0.0, near)
-    grid[:, 2:10, 0:8, 128:256] += jnp.where(beyond, 0.0, far)
 
     def around(values):
         return (
@@ -251,11 +281,18 @@
         new_state[c] = middle + DT_STEP * change
 
 
-def swap(up, down, axis):
+def shift(up, down, axis):
     count = lax.axis_size(axis)
     forward = [(i, (i + 1) % count) for i in range(count)]
     backward = [(target, source) for source, target in forward]
     return lax.ppermute(up, axis, forward), lax.ppermute(down, axis, backward)
+
+
+def swap(slab, axis, odd):
+    count = lax.axis_size(axis)
+    return lax.ppermute(
+        slab, axis, [(i, (i + 1 if i % 2 == odd else i - 1) % count) for i in range(count)]
+    )
 
 
 def exchange(blocks, axes):
@@ -268,11 +305,10 @@
     elem = sample_elem.reshape(1, ROWS)
     weight = sample_weight.reshape(1, ROWS)
 
-    xlo, xhi = swap(state[:, 6:8], state[:, 0:2], "gx")
     coef = element_coef.reshape(1, 128)
     rows = pltpu.VMEM((1, ROWS), jnp.int32)
     held = (
-        pltpu.VMEM((3, 8, 8, 128), jnp.float32),
+        pltpu.VMEM((4, 8, 8, 128), jnp.float32),
         rows,
         rows,
         rows,
@@ -281,26 +317,35 @@
         pltpu.VMEM((1, 128), jnp.float32),
         pltpu.SemaphoreType.DMA((7,)),
     )
-    partial, own = call(
-        sample_kernel, (f32(32, 8, 128), f32(8, 128)), held, 7, pltpu.HBM, 60 * 1024 * 1024
+    side = f32(4, 8, 2, 128)
+    partial, own, yup, ydown = call(
+        sample_kernel,
+        (f32(32, 16, 128), f32(8, 128), side, side),
+        held,
+        7,
+        pltpu.HBM,
+        60 * 1024 * 1024,
     )(state, cell, dest, elem, weight, element_motion, coef)
-    partial = exchange(partial, PLANE)
-    partial, own, xlo, xhi = lax.optimization_barrier((partial, own, xlo, xhi))
-
-    totals = call(total_kernel, f32(16, 8, 128), count=2)(partial, own)
+    parts = exchange(partial, PLANE)
+    ylo, yhi = shift(yup, ydown, "gy")
+    parts, ylo, yhi = lax.optimization_barrier((parts, ylo, yhi))
+
+    totals = call(total_kernel, f32(16, 8, 128), count=2)(parts, own)
     totals = exchange(totals, "gx")
-    wide = jnp.concatenate([xlo[:, 1:2], state, xhi[:, 0:1]], axis=1)
-    ylo, yhi = swap(wide[:, :, 6:8], wide[:, :, 0:2], "gy")
-    ghosts = (xlo, xhi, ylo, yhi)
-    packs = call(ends_kernel, f32(2, 8, 128), (pltpu.VMEM((4, 12, 16, 128), jnp.float32),), 5)(
-        state, *ghosts
-    )
-
-    forces = call(force_kernel, f32(32, 16, 128), count=2)(totals, packs)
+    slab = f32(4, 4, 8, 128)
+    first, second, ghosts = call(faces_kernel, (slab, slab, f32(4, 8, 16, 128)), count=4)(
+        parts, state, ylo, yhi
+    )
+    first = swap(first, "gx", 0)
+    totals, first = lax.optimization_barrier((totals, first))
+
+    forces = call(force_kernel, f32(32, 8, 128), count=1)(totals)
+    forces, second = lax.optimization_barrier((forces, second))
     forces = exchange(forces, PLANE)
+    second = swap(second, "gx", 1)
     grid = pltpu.VMEM((4, 12, 16, 256), jnp.float32)
-    return call(final_kernel, (f32(4, 8, 8, 128), f32(3, 8, 8, 128)), (grid,), 10)(
-        forces, cell, dest, elem, weight, state, *ghosts
+    return call(final_kernel, (f32(4, 8, 8, 128), f32(3, 8, 8, 128)), (grid,), 11)(
+        forces, cell, dest, elem, weight, state, ylo, yhi, ghosts, first, second
     )
 
 

time: 68.4 us -> 64.6 us (0.944)
  blocking collectives: 18.9 us -> 0 us
  waiting for transfers between devices: 11 us -> 19.6 us
  starting transfers between devices: 30.7 us -> 37.6 us
  local copies, waits for them, and re-layouts: 0.76 us -> 0.04 us
    all_to_all x1 -> x0, blocking collectives: 18.9 us -> none  [exchange(): return lax.all_to_all(blocks, axes, split_axis=0, concat_axis=0, tiled=True)]
    all_to_all x2 -> x3, starting transfers between devices: 16.3 us -> 29.4 us  [exchange(): return lax.all_to_all(blocks, axes, split_axis=0, concat_axis=0, tiled=True)]
    ppermute x4, starting transfers between devices: 14.4 us -> 8.16 us  [the longest x2 6.49 us: swap(): lax.ppermute(slab, axis, [(i, (i + 1 if i % 2 == odd else i - 1) % count)...]
    all_to_all x2 -> x3, waiting for transfers between devices: 5.11 us -> 9.78 us  [exchange(): return lax.all_to_all(blocks, axes, split_axis=0, concat_axis=0, tiled=True)]
    ppermute x4, waiting for transfers between devices: 5.89 us -> 9.8 us  [the longest x2 5.58 us: swap(): lax.ppermute(slab, axis, [(i, (i + 1 if i % 2 == odd else i - 1) % count)...]
    slice x4 -> x0, local copies, waits for them, and re-layouts: 0.71 us -> none  [the longest x3 0.7 us: body(): wide = jnp.concatenate([xlo[:, 1:2], state, xhi[:, 0:1]], axis=1)]
  transfers between devices with their start and end apart: 6 -> 7, of which waited for: 3 -> 7; matrix products, arithmetic and copies ran while one was open for 0% -> 0% of each run, Pallas kernels for 1% -> 1%
where the time goes in v4:
time: 64.6 us; the launch traced here: 64.1 us
  starting transfers between devices  37.6 us (58%)
  waiting for transfers between devices  19.6 us (30%)
  Pallas kernels  6.12 us (9%)
  between operations  0.75 us (1%)
    all_to_all x3, starting transfers between devices, exchange(): return lax.all_to_all(blocks, axes, split_axis=0, concat_axis=0, tiled=True)  29.4 us
    all_to_all x3, waiting for transfers between devices, exchange(): return lax.all_to_all(blocks, axes, split_axis=0, concat_axis=0, tiled=True)  9.78 us
    ppermute x2, starting transfers between devices, swap(): lax.ppermute(slab, axis, [(i, (i + 1 if i % 2 == odd else i - 1) % count)...  6.49 us
    ppermute x2, waiting for transfers between devices, swap(): lax.ppermute(slab, axis, [(i, (i + 1 if i % 2 == odd else i - 1) % count)...  5.58 us
    ppermute x2, waiting for transfers between devices, shift(): return (lax.ppermute(up, axis, forward), lax.ppermute(down, axis, backward))  4.22 us
    pallas_call x1, Pallas kernels, body(): call(sample_kernel, (f32(32, 16, 128), f32(8, 128), side, side), held, 7,...  2.42 us
    pallas_call x1, Pallas kernels, body(): call(final_kernel, (f32(4, 8, 8, 128), f32(3, 8, 8, 128)), (grid,), 11)  1.88 us
    ppermute x2, starting transfers between devices, shift(): return (lax.ppermute(up, axis, forward), lax.ppermute(down, axis, backward))  1.67 us
  transfers between devices with their start and end apart: 7, of which 7 were waited for; matrix products, arithmetic and copies ran while one was open for 0% of the time, Pallas kernels for 1%

profile of v4, /device:TPU:1, one launch (start us, length us, event | category | flops | bytes accessed | tf_op | source)
XLA Modules:
  0.0 64.1 jit_solution(10805976417383356645)
XLA Ops:
  0.6 2.4 %shard_map.86 = (f32[32,16,128]{2,1,0:T(8,128)}, f32[8,128]{1,0:T(8,128)}, f32[4,8,2,128]{3,2,1,0:T(2,128)}, f32[4,8,2,128]{3,2,1,0:T(2,128)}) custom-call(f32[4,8,8,128]{3,2,1,0:T(8,128)} %state.3, s32[1,1024]{1,0:T(1,128)} %bitcast.5, s32[1,1024]{1,0:T(1,128)} %bitcast.7, s32[1,1024]{1,0:T(1,128)} %bitcast.9, f32[1,1024]{1,0:T(1,128)} %bitcast.11, ...), custom_call_target="tpu_custom_call" | custom-call | flops 2000000 | bytes 1000000 | tf_op jit(solution)/shard_map/pallas_call | solution.py:321
  3.1 0.0 copy-start.7
  3.1 0.0 copy-start.6
  3.1 10.4 %all-to-all-start = ((f32[32,16,128]{2,1,0:T(8,128)}), f32[32,16,128]{2,1,0:T(8,128)S(1)}, u32[]{:S(2)}, u32[]{:S(2)}) async-start(f32[32,16,128]{2,1,0:T(8,128)} %get-tuple-element.16), calls=%async_computation | async-start | bytes 524288 | tf_op jit(solution)/shard_map/all_to_all | solution.py:299
  13.5 0.0 copy-start.5
  13.5 0.0 copy-done.7
  13.5 1.7 %collective-permute-start = (f32[4,8,2,128]{3,2,1,0:T(2,128)S(1)}, f32[4,8,2,128]{3,2,1,0:T(2,128)S(1)}, u32[]{:S(2)}, u32[]{:S(2)}) collective-permute-start(f32[4,8,2,128]{3,2,1,0:T(2,128)S(1)} %copy-done.7), channel_id=1, source_target_pairs={{0,4},{4,8},{8,12},{12,16},{16,20},{20,24},{24,28},{28,0},{1,5},{5... | collective-permute-start | bytes 98312 | tf_op jit(solution)/shard_map/ppermute | solution.py:288
  15.2 0.0 copy-done.6
  15.2 0.0 collective-permute-start.1
  15.2 2.1 %collective-permute-done.ylo = f32[4,8,2,128]{3,2,1,0:T(2,128)S(1)} collective-permute-done((f32[4,8,2,128]{3,2,1,0:T(2,128)S(1)}, f32[4,8,2,128]{3,2,1,0:T(2,128)S(1)}, u32[]{:S(2)}, u32[]{:S(2)}) %collective-permute-start) | collective-permute-done | bytes 32800 | tf_op jit(solution)/shard_map/ppermute | solution.py:288
  17.3 2.1 %collective-permute-done.1.yhi = f32[4,8,2,128]{3,2,1,0:T(2,128)S(1)} collective-permute-done((f32[4,8,2,128]{3,2,1,0:T(2,128)S(1)}, f32[4,8,2,128]{3,2,1,0:T(2,128)S(1)}, u32[]{:S(2)}, u32[]{:S(2)}) %collective-permute-start.1) | collective-permute-done | bytes 32800 | tf_op jit(solution)/shard_map/ppermute | solution.py:288
  19.4 3.1 %all-to-all-done.parts = f32[32,16,128]{2,1,0:T(8,128)S(1)} async-done(((f32[32,16,128]{2,1,0:T(8,128)}), f32[32,16,128]{2,1,0:T(8,128)S(1)}, u32[]{:S(2)}, u32[]{:S(2)}) %all-to-all-start) | async-done | bytes 262176 | tf_op jit(solution)/shard_map/all_to_all | solution.py:299
  22.5 0.0 copy-done.5
  22.5 0.7 %shard_map.87 = f32[16,8,128]{2,1,0:T(8,128)} custom-call(f32[32,16,128]{2,1,0:T(8,128)S(1)} %all-to-all-done.parts, f32[8,128]{1,0:T(8,128)S(1)} %copy-done.5), custom_call_target="tpu_custom_call" | custom-call | flops 2000000 | bytes 1000000 | tf_op jit(solution)/shard_map/pallas_call | solution.py:333
  23.2 0.0 copy-start
  23.2 13.1 %all-to-all-start.1 = ((f32[16,8,128]{2,1,0:T(8,128)}), f32[16,8,128]{2,1,0:T(8,128)S(1)}, u32[]{:S(2)}, u32[]{:S(2)}) async-start(f32[16,8,128]{2,1,0:T(8,128)} %shard_map.87), calls=%async_computation.1 | async-start | bytes 131072 | tf_op jit(solution)/shard_map/all_to_all | solution.py:299
  36.3 0.0 copy-done
  36.4 0.5 shard_map.88
  36.8 3.3 %collective-permute-start.2 = (f32[4,4,8,128]{3,2,1,0:T(8,128)S(1)}, f32[4,4,8,128]{3,2,1,0:T(8,128)S(1)}, u32[]{:S(2)}, u32[]{:S(2)}) collective-permute-start(f32[4,4,8,128]{3,2,1,0:T(8,128)S(1)} %get-tuple-element.23), channel_id=1, source_target_pairs={{0,32},{32,0},{64,96},{96,64},{128,160},{160,128},{192,224},{224,1... | collective-permute-start | bytes 196616 | tf_op jit(solution)/shard_map/ppermute | solution.py:293
  40.1 2.3 %collective-permute-done.2.first = f32[4,4,8,128]{3,2,1,0:T(8,128)S(1)} collective-permute-done((f32[4,4,8,128]{3,2,1,0:T(8,128)S(1)}, f32[4,4,8,128]{3,2,1,0:T(8,128)S(1)}, u32[]{:S(2)}, u32[]{:S(2)}) %collective-permute-start.2) | collective-permute-done | bytes 65568 | tf_op jit(solution)/shard_map/ppermute | solution.py:293
  42.4 5.5 %all-to-all-done.1.parts = f32[16,8,128]{2,1,0:T(8,128)S(1)} async-done(((f32[16,8,128]{2,1,0:T(8,128)}), f32[16,8,128]{2,1,0:T(8,128)S(1)}, u32[]{:S(2)}, u32[]{:S(2)}) %all-to-all-start.1) | async-done | bytes 65568 | tf_op jit(solution)/shard_map/all_to_all | solution.py:299
  47.9 0.7 %shard_map.89 = f32[32,8,128]{2,1,0:T(8,128)} custom-call(f32[16,8,128]{2,1,0:T(8,128)S(1)} %all-to-all-done.1.parts), custom_call_target="tpu_custom_call" | custom-call | flops 2000000 | bytes 1000000 | tf_op jit(solution)/shard_map/pallas_call | solution.py:342
  48.6 0.0 copy-start.1
  48.6 5.9 %all-to-all-start.2 = ((f32[32,8,128]{2,1,0:T(8,128)}), f32[32,8,128]{2,1,0:T(8,128)S(1)}, u32[]{:S(2)}, u32[]{:S(2)}) async-start(f32[32,8,128]{2,1,0:T(8,128)} %shard_map.89), calls=%async_computation.2 | async-start | bytes 262144 | tf_op jit(solution)/shard_map/all_to_all | solution.py:299
  54.5 3.2 %collective-permute-start.3 = (f32[4,4,8,128]{3,2,1,0:T(8,128)S(1)}, f32[4,4,8,128]{3,2,1,0:T(8,128)S(1)}, u32[]{:S(2)}, u32[]{:S(2)}) collective-permute-start(f32[4,4,8,128]{3,2,1,0:T(8,128)S(1)} %get-tuple-element.29), channel_id=1, source_target_pairs={{0,480},{32,64},{64,32},{96,128},{128,96},{160,192},{192,160},{224... | collective-permute-start | bytes 196616 | tf_op jit(solution)/shard_map/ppermute | solution.py:293
  57.8 3.3 %collective-permute-done.3.second = f32[4,4,8,128]{3,2,1,0:T(8,128)S(1)} collective-permute-done((f32[4,4,8,128]{3,2,1,0:T(8,128)S(1)}, f32[4,4,8,128]{3,2,1,0:T(8,128)S(1)}, u32[]{:S(2)}, u32[]{:S(2)}) %collective-permute-start.3) | collective-permute-done | bytes 65568 | tf_op jit(solution)/shard_map/ppermute | solution.py:293
  61.0 1.2 %all-to-all-done.2.parts = f32[32,8,128]{2,1,0:T(8,128)S(1)} async-done(((f32[32,8,128]{2,1,0:T(8,128)}), f32[32,8,128]{2,1,0:T(8,128)S(1)}, u32[]{:S(2)}, u32[]{:S(2)}) %all-to-all-start.2) | async-done | bytes 131104 | tf_op jit(solution)/shard_map/all_to_all | solution.py:299
  62.2 0.0 copy-done.1
  62.2 0.0 copy-done.2
  62.2 0.0 copy-done.3
  62.2 0.0 copy-done.4
  62.2 1.9 %shard_map.90 = (f32[4,8,8,128]{3,2,1,0:T(8,128)}, f32[3,8,8,128]{3,2,1,0:T(8,128)}) custom-call(f32[32,8,128]{2,1,0:T(8,128)S(1)} %all-to-all-done.2.parts, s32[1,1024]{1,0:T(1,128)S(1)} %bitcast.6, s32[1,1024]{1,0:T(1,128)S(1)} %bitcast.8, s32[1,1024]{1,0:T(1,128)S(1)} %bitcast.10, f32[1,1024]{1,0:T(1,128)S(1)} %bitcast.12, f32[4,8,8,128]{3,2,1,0:T(8,128)S(1)} %copy-done, ...), custom_call_target="tpu_custom_call" | custom-call | flops 2000000 | bytes 1000000 | tf_op jit(solution)/shard_map/pallas_call | solution.py:347
  (3 shorter events, 0.0 us)
Async XLA Ops:
  3.1 10.5 %copy-start.7 = (f32[4,8,2,128]{3,2,1,0:T(2,128)S(1)}, f32[4,8,2,128]{3,2,1,0:T(2,128)}, u32[]{:S(2)}) copy-start(f32[4,8,2,128]{3,2,1,0:T(2,128)} %get-tuple-element.17) | copy-start | bytes 98308
  3.1 12.1 %copy-start.6 = (f32[4,8,2,128]{3,2,1,0:T(2,128)S(1)}, f32[4,8,2,128]{3,2,1,0:T(2,128)}, u32[]{:S(2)}) copy-start(f32[4,8,2,128]{3,2,1,0:T(2,128)} %get-tuple-element.18) | copy-start | bytes 98308
  3.1 19.5 %all-to-all-start = ((f32[32,16,128]{2,1,0:T(8,128)}), f32[32,16,128]{2,1,0:T(8,128)S(1)}, u32[]{:S(2)}, u32[]{:S(2)}) async-start(f32[32,16,128]{2,1,0:T(8,128)} %get-tuple-element.16), calls=%async_computation | async-start | bytes 524288 | tf_op jit(solution)/shard_map/all_to_all | solution.py:299
  13.5 9.0 %copy-start.5 = (f32[8,128]{1,0:T(8,128)S(1)}, f32[8,128]{1,0:T(8,128)}, u32[]{:S(2)}) copy-start(f32[8,128]{1,0:T(8,128)} %get-tuple-element.20.own) | copy-start | bytes 12292
  13.5 3.8 %collective-permute-start = (f32[4,8,2,128]{3,2,1,0:T(2,128)S(1)}, f32[4,8,2,128]{3,2,1,0:T(2,128)S(1)}, u32[]{:S(2)}, u32[]{:S(2)}) collective-permute-start(f32[4,8,2,128]{3,2,1,0:T(2,128)S(1)} %copy-done.7), channel_id=1, source_target_pairs={{0,4},{4,8},{8,12},{12,16},{16,20},{20,24},{24,28},{28,0},{1,5},{5... | collective-permute-start | bytes 98312 | tf_op jit(solution)/shard_map/ppermute | solution.py:288
  15.2 4.2 %collective-permute-start.1 = (f32[4,8,2,128]{3,2,1,0:T(2,128)S(1)}, f32[4,8,2,128]{3,2,1,0:T(2,128)S(1)}, u32[]{:S(2)}, u32[]{:S(2)}) collective-permute-start(f32[4,8,2,128]{3,2,1,0:T(2,128)S(1)} %copy-done.6), channel_id=1, source_target_pairs={{4,0},{8,4},{12,8},{16,12},{20,16},{24,20},{28,24},{0,28},{5,1},{9... | collective-permute-start | bytes 98312 | tf_op jit(solution)/shard_map/ppermute | solution.py:288
  23.2 13.1 %copy-start = (f32[4,8,8,128]{3,2,1,0:T(8,128)S(1)}, f32[4,8,8,128]{3,2,1,0:T(8,128)}, u32[]{:S(2)}) copy-start(f32[4,8,8,128]{3,2,1,0:T(8,128)} %state.3) | copy-start | bytes 393220
  23.2 24.7 %all-to-all-start.1 = ((f32[16,8,128]{2,1,0:T(8,128)}), f32[16,8,128]{2,1,0:T(8,128)S(1)}, u32[]{:S(2)}, u32[]{:S(2)}) async-start(f32[16,8,128]{2,1,0:T(8,128)} %shard_map.87), calls=%async_computation.1 | async-start | bytes 131072 | tf_op jit(solution)/shard_map/all_to_all | solution.py:299
  36.8 5.6 %collective-permute-start.2 = (f32[4,4,8,128]{3,2,1,0:T(8,128)S(1)}, f32[4,4,8,128]{3,2,1,0:T(8,128)S(1)}, u32[]{:S(2)}, u32[]{:S(2)}) collective-permute-start(f32[4,4,8,128]{3,2,1,0:T(8,128)S(1)} %get-tuple-element.23), channel_id=1, source_target_pairs={{0,32},{32,0},{64,96},{96,64},{128,160},{160,128},{192,224},{224,1... | collective-permute-start | bytes 196616 | tf_op jit(solution)/shard_map/ppermute | solution.py:293
  48.6 13.6 %copy-start.1 = (s32[1024]{0:T(1024)S(1)}, s32[1024]{0:T(1024)}, u32[]{:S(2)}) copy-start(s32[1024]{0:T(1024)} %param.8) | copy-start | bytes 12292
  48.6 13.6 %copy-start.2 = (s32[1024,1]{0,1:T(1,128)S(1)}, s32[1024,1]{0,1:T(1,128)}, u32[]{:S(2)}) copy-start(s32[1024,1]{0,1:T(1,128)} %param.9) | copy-start | bytes 12292
  48.6 13.6 %copy-start.3 = (s32[1024]{0:T(1024)S(1)}, s32[1024]{0:T(1024)}, u32[]{:S(2)}) copy-start(s32[1024]{0:T(1024)} %param.11) | copy-start | bytes 12292
  48.6 13.6 %copy-start.4 = (f32[1024]{0:T(1024)S(1)}, f32[1024]{0:T(1024)}, u32[]{:S(2)}) copy-start(f32[1024]{0:T(1024)} %param.10) | copy-start | bytes 12292
  48.6 13.6 %all-to-all-start.2 = ((f32[32,8,128]{2,1,0:T(8,128)}), f32[32,8,128]{2,1,0:T(8,128)S(1)}, u32[]{:S(2)}, u32[]{:S(2)}) async-start(f32[32,8,128]{2,1,0:T(8,128)} %shard_map.89), calls=%async_computation.2 | async-start | bytes 262144 | tf_op jit(solution)/shard_map/all_to_all | solution.py:299
  54.5 6.5 %collective-permute-start.3 = (f32[4,4,8,128]{3,2,1,0:T(8,128)S(1)}, f32[4,4,8,128]{3,2,1,0:T(8,128)S(1)}, u32[]{:S(2)}, u32[]{:S(2)}) collective-permute-start(f32[4,4,8,128]{3,2,1,0:T(8,128)S(1)} %get-tuple-element.29), channel_id=1, source_target_pairs={{0,480},{32,64},{64,32},{96,128},{128,96},{160,192},{192,160},{224... | collective-permute-start | bytes 196616 | tf_op jit(solution)/shard_map/ppermute | solution.py:293

commit v5 on v4

--- a/solution.py
+++ b/solution.py
@@ -220,10 +220,7 @@
         second[:, i] = jnp.where(even, low, high)
 
 
-def final_kernel(
-    parts, cell, dest, elem, weight, state, ylo, yhi, ghosts, first, second, *results
-):
-    new_state, body_force, grid = results
+def spread_kernel(parts, cell, dest, elem, weight, before, new_state, body_force):
     match, hot_lane = element_keys(dest[...], elem[...])
     found = pick(parts[...].reshape(256, 128), hot_lane).reshape(32, 8, ROWS)
     pairs = jnp.sum(jnp.where(match, found, 0.0), axis=0)
@@ -232,7 +229,11 @@
     spread = jnp.concatenate([jnp.where(column, each[c], 0.0) for c in range(3)], axis=0)
     body = put(spread, hot_z).reshape(3, 8, 8, 128)
     body_force[...] = body
-
+    new_state[0:3] = before[0:3] + DT_STEP * body
+    new_state[3] = before[3]
+
+
+def stencil_kernel(state, ylo, yhi, ghosts, first, second, before, grid):
     gz = lax.axis_index("gz")
     fill(grid, state, ylo, yhi, ghosts, first, second)
     level = lax.broadcasted_iota(jnp.int32, (1, 1, 256), 2)
@@ -276,9 +277,7 @@
             change = change + (BASE_COEF + ratio * faces[j][0]) * (upper - middle)
             change = change - (BASE_COEF + ratio * faces[j][1]) * (middle - lower)
             change = change - wind[j] * (upper - lower)
-        if c < 3:
-            change = change + body[c]
-        new_state[c] = middle + DT_STEP * change
+        before[c] = middle + DT_STEP * change
 
 
 def shift(up, down, axis):
@@ -336,16 +335,17 @@
     first, second, ghosts = call(faces_kernel, (slab, slab, f32(4, 8, 16, 128)), count=4)(
         parts, state, ylo, yhi
     )
-    first = swap(first, "gx", 0)
-    totals, first = lax.optimization_barrier((totals, first))
+    first, second = swap(first, "gx", 0), swap(second, "gx", 1)
+    totals, first, second = lax.optimization_barrier((totals, first, second))
 
     forces = call(force_kernel, f32(32, 8, 128), count=1)(totals)
-    forces, second = lax.optimization_barrier((forces, second))
     forces = exchange(forces, PLANE)
-    second = swap(second, "gx", 1)
     grid = pltpu.VMEM((4, 12, 16, 256), jnp.float32)
-    return call(final_kernel, (f32(4, 8, 8, 128), f32(3, 8, 8, 128)), (grid,), 11)(
-        forces, cell, dest, elem, weight, state, ylo, yhi, ghosts, first, second
+    before = call(stencil_kernel, f32(4, 8, 8, 128), (grid,), 6)(
+        state, ylo, yhi, ghosts, first, second
+    )
+    return call(spread_kernel, (f32(4, 8, 8, 128), f32(3, 8, 8, 128)), count=6)(
+        forces, cell, dest, elem, weight, before
     )
 
 

time: 64.6 us -> 64.1 us (level)
  waiting for transfers between devices: 19.6 us -> 17.9 us
  starting transfers between devices: 37.6 us -> 38.6 us
    ppermute x2, waiting for transfers between devices: 5.58 us -> 2.37 us  [swap(): lax.ppermute(slab, axis, [(i, (i + 1 if i % 2 == odd else i - 1) % count)...]
    all_to_all x3, waiting for transfers between devices: 9.78 us -> 11.3 us  [exchange(): return lax.all_to_all(blocks, axes, split_axis=0, concat_axis=0, tiled=True)]
    ppermute x2, starting transfers between devices: 6.49 us -> 7.58 us  [swap(): lax.ppermute(slab, axis, [(i, (i + 1 if i % 2 == odd else i - 1) % count)...]
    pallas_call x1 -> x2, Pallas kernels: 1.88 us -> 2.13 us  [the longest x1 1.57 us: body(): call(spread_kernel, (f32(4, 8, 8, 128), f32(3, 8, 8, 128)), count=6)]
  transfers between devices with their start and end apart: 7 -> 7, of which waited for: 7 -> 6; matrix products, arithmetic and copies ran while one was open for 0% -> 0% of each run, Pallas kernels for 1% -> 2%
where the time goes in v5:
time: 64.1 us; the launch traced here: 63.6 us
  starting transfers between devices  38.6 us (60%)
  waiting for transfers between devices  17.9 us (28%)
  Pallas kernels  6.37 us (10%)
  between operations  0.79 us (1%)
    all_to_all x3, starting transfers between devices, exchange(): return lax.all_to_all(blocks, axes, split_axis=0, concat_axis=0, tiled=True)  29.3 us
    all_to_all x3, waiting for transfers between devices, exchange(): return lax.all_to_all(blocks, axes, split_axis=0, concat_axis=0, tiled=True)  11.3 us
    ppermute x2, starting transfers between devices, swap(): lax.ppermute(slab, axis, [(i, (i + 1 if i % 2 == odd else i - 1) % count)...  7.58 us
    ppermute x2, waiting for transfers between devices, shift(): return (lax.ppermute(up, axis, forward), lax.ppermute(down, axis, backward))  4.22 us
    pallas_call x1, Pallas kernels, body(): call(sample_kernel, (f32(32, 16, 128), f32(8, 128), side, side), held, 7,...  2.42 us
    ppermute x2, waiting for transfers between devices, swap(): lax.ppermute(slab, axis, [(i, (i + 1 if i % 2 == odd else i - 1) % count)...  2.37 us
    ppermute x2, starting transfers between devices, shift(): return (lax.ppermute(up, axis, forward), lax.ppermute(down, axis, backward))  1.67 us
    pallas_call x1, Pallas kernels, body(): call(spread_kernel, (f32(4, 8, 8, 128), f32(3, 8, 8, 128)), count=6)  1.57 us
  transfers between devices with their start and end apart: 7, of which 6 were waited for; matrix products, arithmetic and copies ran while one was open for 0% of the time, Pallas kernels for 2%

profile of v5, /device:TPU:1, one launch (start us, length us, event | category | flops | bytes accessed | tf_op | source)
XLA Modules:
  0.0 63.6 jit_solution(15257781828976742782)
XLA Ops:
  0.6 2.4 %shard_map.86 = (f32[32,16,128]{2,1,0:T(8,128)}, f32[8,128]{1,0:T(8,128)}, f32[4,8,2,128]{3,2,1,0:T(2,128)}, f32[4,8,2,128]{3,2,1,0:T(2,128)}) custom-call(f32[4,8,8,128]{3,2,1,0:T(8,128)} %state.3, s32[1,1024]{1,0:T(1,128)} %bitcast.5, s32[1,1024]{1,0:T(1,128)} %bitcast.7, s32[1,1024]{1,0:T(1,128)} %bitcast.9, f32[1,1024]{1,0:T(1,128)} %bitcast.11, ...), custom_call_target="tpu_custom_call" | custom-call | flops 2000000 | bytes 1000000 | tf_op jit(solution)/shard_map/pallas_call | solution.py:320
  3.1 0.0 copy-start.7
  3.1 0.0 copy-start.6
  3.1 10.4 %all-to-all-start = ((f32[32,16,128]{2,1,0:T(8,128)}), f32[32,16,128]{2,1,0:T(8,128)S(1)}, u32[]{:S(2)}, u32[]{:S(2)}) async-start(f32[32,16,128]{2,1,0:T(8,128)} %get-tuple-element.15), calls=%async_computation | async-start | bytes 524288 | tf_op jit(solution)/shard_map/all_to_all | solution.py:298
  13.5 0.0 copy-start.5
  13.5 1.7 %collective-permute-start = (f32[4,8,2,128]{3,2,1,0:T(2,128)S(1)}, f32[4,8,2,128]{3,2,1,0:T(2,128)S(1)}, u32[]{:S(2)}, u32[]{:S(2)}) collective-permute-start(f32[4,8,2,128]{3,2,1,0:T(2,128)S(1)} %copy-done.7), channel_id=1, source_target_pairs={{0,4},{4,8},{8,12},{12,16},{16,20},{20,24},{24,28},{28,0},{1,5},{5... | collective-permute-start | bytes 98312 | tf_op jit(solution)/shard_map/ppermute | solution.py:287
  15.2 0.0 copy-done.6
  15.2 0.0 collective-permute-start.1
  15.2 2.1 %collective-permute-done.ylo = f32[4,8,2,128]{3,2,1,0:T(2,128)S(1)} collective-permute-done((f32[4,8,2,128]{3,2,1,0:T(2,128)S(1)}, f32[4,8,2,128]{3,2,1,0:T(2,128)S(1)}, u32[]{:S(2)}, u32[]{:S(2)}) %collective-permute-start) | collective-permute-done | bytes 32800 | tf_op jit(solution)/shard_map/ppermute | solution.py:287
  17.3 2.1 %collective-permute-done.1.yhi = f32[4,8,2,128]{3,2,1,0:T(2,128)S(1)} collective-permute-done((f32[4,8,2,128]{3,2,1,0:T(2,128)S(1)}, f32[4,8,2,128]{3,2,1,0:T(2,128)S(1)}, u32[]{:S(2)}, u32[]{:S(2)}) %collective-permute-start.1) | collective-permute-done | bytes 32800 | tf_op jit(solution)/shard_map/ppermute | solution.py:287
  19.4 3.1 %all-to-all-done.parts = f32[32,16,128]{2,1,0:T(8,128)S(1)} async-done(((f32[32,16,128]{2,1,0:T(8,128)}), f32[32,16,128]{2,1,0:T(8,128)S(1)}, u32[]{:S(2)}, u32[]{:S(2)}) %all-to-all-start) | async-done | bytes 262176 | tf_op jit(solution)/shard_map/all_to_all | solution.py:298
  22.5 0.0 copy-done.5
  22.5 0.7 %shard_map.87 = f32[16,8,128]{2,1,0:T(8,128)} custom-call(f32[32,16,128]{2,1,0:T(8,128)S(1)} %all-to-all-done.parts, f32[8,128]{1,0:T(8,128)S(1)} %copy-done.5), custom_call_target="tpu_custom_call" | custom-call | flops 2000000 | bytes 1000000 | tf_op jit(solution)/shard_map/pallas_call | solution.py:332
  23.2 13.1 %all-to-all-start.1 = ((f32[16,8,128]{2,1,0:T(8,128)}), f32[16,8,128]{2,1,0:T(8,128)S(1)}, u32[]{:S(2)}, u32[]{:S(2)}) async-start(f32[16,8,128]{2,1,0:T(8,128)} %shard_map.87), calls=%async_computation.1 | async-start | bytes 131072 | tf_op jit(solution)/shard_map/all_to_all | solution.py:298
  36.3 0.0 copy-done
  36.4 0.5 shard_map.88
  36.8 3.3 %collective-permute-start.2 = (f32[4,4,8,128]{3,2,1,0:T(8,128)S(1)}, f32[4,4,8,128]{3,2,1,0:T(8,128)S(1)}, u32[]{:S(2)}, u32[]{:S(2)}) collective-permute-start(f32[4,4,8,128]{3,2,1,0:T(8,128)S(1)} %get-tuple-element.22), channel_id=1, source_target_pairs={{0,32},{32,0},{64,96},{96,64},{128,160},{160,128},{192,224},{224,1... | collective-permute-start | bytes 196616 | tf_op jit(solution)/shard_map/ppermute | solution.py:292
  40.1 4.3 %collective-permute-start.3 = (f32[4,4,8,128]{3,2,1,0:T(8,128)S(1)}, f32[4,4,8,128]{3,2,1,0:T(8,128)S(1)}, u32[]{:S(2)}, u32[]{:S(2)}) collective-permute-start(f32[4,4,8,128]{3,2,1,0:T(8,128)S(1)} %get-tuple-element.23), channel_id=1, source_target_pairs={{0,480},{32,64},{64,32},{96,128},{128,96},{160,192},{192,160},{224... | collective-permute-start | bytes 196616 | tf_op jit(solution)/shard_map/ppermute | solution.py:292
  44.4 0.0 collective-permute-done.2.first
  44.4 2.4 %collective-permute-done.3.second = f32[4,4,8,128]{3,2,1,0:T(8,128)S(1)} collective-permute-done((f32[4,4,8,128]{3,2,1,0:T(8,128)S(1)}, f32[4,4,8,128]{3,2,1,0:T(8,128)S(1)}, u32[]{:S(2)}, u32[]{:S(2)}) %collective-permute-start.3) | collective-permute-done | bytes 65568 | tf_op jit(solution)/shard_map/ppermute | solution.py:292
  46.8 1.1 %all-to-all-done.1.parts = f32[16,8,128]{2,1,0:T(8,128)S(1)} async-done(((f32[16,8,128]{2,1,0:T(8,128)}), f32[16,8,128]{2,1,0:T(8,128)S(1)}, u32[]{:S(2)}, u32[]{:S(2)}) %all-to-all-start.1) | async-done | bytes 65568 | tf_op jit(solution)/shard_map/all_to_all | solution.py:298
  47.9 0.7 %shard_map.89 = f32[32,8,128]{2,1,0:T(8,128)} custom-call(f32[16,8,128]{2,1,0:T(8,128)S(1)} %all-to-all-done.1.parts), custom_call_target="tpu_custom_call" | custom-call | flops 2000000 | bytes 1000000 | tf_op jit(solution)/shard_map/pallas_call | solution.py:341
  48.6 5.7 %all-to-all-start.2 = ((f32[32,8,128]{2,1,0:T(8,128)}), f32[32,8,128]{2,1,0:T(8,128)S(1)}, u32[]{:S(2)}, u32[]{:S(2)}) async-start(f32[32,8,128]{2,1,0:T(8,128)} %shard_map.89), calls=%async_computation.2 | async-start | bytes 262144 | tf_op jit(solution)/shard_map/all_to_all | solution.py:298
  54.4 0.0 copy-start.1
  54.4 0.0 copy-start.2
  54.4 0.0 copy-start.3
  54.4 0.0 copy-start.4
  54.4 0.6 shard_map.90.before
  55.0 7.1 %all-to-all-done.2.parts = f32[32,8,128]{2,1,0:T(8,128)S(1)} async-done(((f32[32,8,128]{2,1,0:T(8,128)}), f32[32,8,128]{2,1,0:T(8,128)S(1)}, u32[]{:S(2)}, u32[]{:S(2)}) %all-to-all-start.2) | async-done | bytes 131104 | tf_op jit(solution)/shard_map/all_to_all | solution.py:298
  62.0 0.0 copy-done.1
  62.0 0.0 copy-done.3
  62.1 1.6 %shard_map.91 = (f32[4,8,8,128]{3,2,1,0:T(8,128)}, f32[3,8,8,128]{3,2,1,0:T(8,128)}) custom-call(f32[32,8,128]{2,1,0:T(8,128)S(1)} %all-to-all-done.2.parts, s32[1,1024]{1,0:T(1,128)S(1)} %bitcast.6, s32[1,1024]{1,0:T(1,128)S(1)} %bitcast.8, s32[1,1024]{1,0:T(1,128)S(1)} %bitcast.10, f32[1,1024]{1,0:T(1,128)S(1)} %bitcast.12, ...), custom_call_target="tpu_custom_call" | custom-call | flops 2000000 | bytes 1000000 | tf_op jit(solution)/shard_map/pallas_call | solution.py:347
  (4 shorter events, 0.0 us)
Async XLA Ops:
  3.1 10.5 %copy-start.7 = (f32[4,8,2,128]{3,2,1,0:T(2,128)S(1)}, f32[4,8,2,128]{3,2,1,0:T(2,128)}, u32[]{:S(2)}) copy-start(f32[4,8,2,128]{3,2,1,0:T(2,128)} %get-tuple-element.16) | copy-start | bytes 98308
  3.1 12.1 %copy-start.6 = (f32[4,8,2,128]{3,2,1,0:T(2,128)S(1)}, f32[4,8,2,128]{3,2,1,0:T(2,128)}, u32[]{:S(2)}) copy-start(f32[4,8,2,128]{3,2,1,0:T(2,128)} %get-tuple-element.17) | copy-start | bytes 98308
  3.1 19.5 %all-to-all-start = ((f32[32,16,128]{2,1,0:T(8,128)}), f32[32,16,128]{2,1,0:T(8,128)S(1)}, u32[]{:S(2)}, u32[]{:S(2)}) async-start(f32[32,16,128]{2,1,0:T(8,128)} %get-tuple-element.15), calls=%async_computation | async-start | bytes 524288 | tf_op jit(solution)/shard_map/all_to_all | solution.py:298
  13.5 9.0 %copy-start.5 = (f32[8,128]{1,0:T(8,128)S(1)}, f32[8,128]{1,0:T(8,128)}, u32[]{:S(2)}) copy-start(f32[8,128]{1,0:T(8,128)} %get-tuple-element.19.own) | copy-start | bytes 12292
  13.5 3.8 %collective-permute-start = (f32[4,8,2,128]{3,2,1,0:T(2,128)S(1)}, f32[4,8,2,128]{3,2,1,0:T(2,128)S(1)}, u32[]{:S(2)}, u32[]{:S(2)}) collective-permute-start(f32[4,8,2,128]{3,2,1,0:T(2,128)S(1)} %copy-done.7), channel_id=1, source_target_pairs={{0,4},{4,8},{8,12},{12,16},{16,20},{20,24},{24,28},{28,0},{1,5},{5... | collective-permute-start | bytes 98312 | tf_op jit(solution)/shard_map/ppermute | solution.py:287
  15.2 4.2 %collective-permute-start.1 = (f32[4,8,2,128]{3,2,1,0:T(2,128)S(1)}, f32[4,8,2,128]{3,2,1,0:T(2,128)S(1)}, u32[]{:S(2)}, u32[]{:S(2)}) collective-permute-start(f32[4,8,2,128]{3,2,1,0:T(2,128)S(1)} %copy-done.6), channel_id=1, source_target_pairs={{4,0},{8,4},{12,8},{16,12},{20,16},{24,20},{28,24},{0,28},{5,1},{9... | collective-permute-start | bytes 98312 | tf_op jit(solution)/shard_map/ppermute | solution.py:287
  23.2 13.1 %copy-start = (f32[4,8,8,128]{3,2,1,0:T(8,128)S(1)}, f32[4,8,8,128]{3,2,1,0:T(8,128)}, u32[]{:S(2)}) copy-start(f32[4,8,8,128]{3,2,1,0:T(8,128)} %state.3) | copy-start | bytes 393220
  23.2 24.7 %all-to-all-start.1 = ((f32[16,8,128]{2,1,0:T(8,128)}), f32[16,8,128]{2,1,0:T(8,128)S(1)}, u32[]{:S(2)}, u32[]{:S(2)}) async-start(f32[16,8,128]{2,1,0:T(8,128)} %shard_map.87), calls=%async_computation.1 | async-start | bytes 131072 | tf_op jit(solution)/shard_map/all_to_all | solution.py:298
  36.8 7.6 %collective-permute-start.2 = (f32[4,4,8,128]{3,2,1,0:T(8,128)S(1)}, f32[4,4,8,128]{3,2,1,0:T(8,128)S(1)}, u32[]{:S(2)}, u32[]{:S(2)}) collective-permute-start(f32[4,4,8,128]{3,2,1,0:T(8,128)S(1)} %get-tuple-element.22), channel_id=1, source_target_pairs={{0,32},{32,0},{64,96},{96,64},{128,160},{160,128},{192,224},{224,1... | collective-permute-start | bytes 196616 | tf_op jit(solution)/shard_map/ppermute | solution.py:292
  40.1 6.7 %collective-permute-start.3 = (f32[4,4,8,128]{3,2,1,0:T(8,128)S(1)}, f32[4,4,8,128]{3,2,1,0:T(8,128)S(1)}, u32[]{:S(2)}, u32[]{:S(2)}) collective-permute-start(f32[4,4,8,128]{3,2,1,0:T(8,128)S(1)} %get-tuple-element.23), channel_id=1, source_target_pairs={{0,480},{32,64},{64,32},{96,128},{128,96},{160,192},{192,160},{224... | collective-permute-start | bytes 196616 | tf_op jit(solution)/shard_map/ppermute | solution.py:292
  48.6 13.4 %all-to-all-start.2 = ((f32[32,8,128]{2,1,0:T(8,128)}), f32[32,8,128]{2,1,0:T(8,128)S(1)}, u32[]{:S(2)}, u32[]{:S(2)}) async-start(f32[32,8,128]{2,1,0:T(8,128)} %shard_map.89), calls=%async_computation.2 | async-start | bytes 262144 | tf_op jit(solution)/shard_map/all_to_all | solution.py:298
  54.4 7.7 %copy-start.1 = (s32[1024]{0:T(1024)S(1)}, s32[1024]{0:T(1024)}, u32[]{:S(2)}) copy-start(s32[1024]{0:T(1024)} %param.8) | copy-start | bytes 12292
  54.4 7.7 %copy-start.2 = (s32[1024,1]{0,1:T(1,128)S(1)}, s32[1024,1]{0,1:T(1,128)}, u32[]{:S(2)}) copy-start(s32[1024,1]{0,1:T(1,128)} %param.9) | copy-start | bytes 12292
  54.4 7.7 %copy-start.3 = (s32[1024]{0:T(1024)S(1)}, s32[1024]{0:T(1024)}, u32[]{:S(2)}) copy-start(s32[1024]{0:T(1024)} %param.11) | copy-start | bytes 12292
  54.4 7.6 %copy-start.4 = (f32[1024]{0:T(1024)S(1)}, f32[1024]{0:T(1024)}, u32[]{:S(2)}) copy-start(f32[1024]{0:T(1024)} %param.10) | copy-start | bytes 12292

commit v6 on v4

--- a/solution.py
+++ b/solution.py
@@ -94,12 +94,28 @@
     return jnp.where(hot, 1.0, 0.0)
 
 
-def exact(left, right, dims):
+def thirds(values):
+    high, rest = halves(values)
+    low = values - high.astype(jnp.float32) - rest.astype(jnp.float32)
+    return high, rest, low.astype(jnp.bfloat16)
+
+
+def take_lanes(places, rows):
+    hot = lanes(8, places).astype(jnp.bfloat16)
+    dims = (((1,), (1,)), ((), ()))
+    parts = [
+        lax.dot_general(hot, part, dims, preferred_element_type=jnp.float32)
+        for part in thirds(rows)
+    ]
+    return parts[0] + parts[1] + parts[2]
+
+
+def give_lanes(rows, places):
+    hot = lanes(len(places), places)
     return lax.dot_general(
-        left,
-        right,
-        ((dims, dims), ((), ())),
-        precision=lax.Precision.HIGHEST,
+        jnp.concatenate(thirds(rows), axis=0),
+        jnp.concatenate([hot, hot, hot], axis=0).astype(jnp.bfloat16),
+        (((0,), (0,)), ((), ())),
         preferred_element_type=jnp.float32,
     )
 
@@ -114,8 +130,8 @@
     coef_in,
     out,
     own,
-    yup,
-    ydown,
+    first,
+    second,
     *scratch,
 ):
     held, sems = scratch[:7], scratch[7]
@@ -130,11 +146,9 @@
         copy.wait()
     state, cell, dest, elem, weight, motion, coef = held
     own[...] = own_part(motion, coef)
-    yup[...] = state[:, :, 6:8]
-    ydown[...] = state[:, :, 0:2]
-    ends = exact(lanes(8, (0, 127, 1, 126)), state[...].reshape(256, 128), (1,))
-    pack = [ends[i : i + 1, 128 * j : 128 * j + 128] for i in range(4) for j in range(2)]
-    out[:, 8:16] = jnp.broadcast_to(jnp.concatenate(pack, axis=0)[None], (32, 8, 128))
+    even = (lax.axis_index("gx") & 1) == 0
+    first[...] = jnp.where(even, state[:, 6:8], state[:, 0:2])
+    second[...] = jnp.where(even, state[:, 0:2], state[:, 6:8])
     column, hot_z = cell_keys(cell[...])
     found = pick(state[0:3].reshape(192, 128), hot_z).reshape(3, 64, ROWS)
     sampled = [
@@ -147,15 +161,15 @@
     )
     match, hot_lane = element_keys(dest[...], elem[...])
     spread = jnp.where(match, pattern[None], 0.0).reshape(256, ROWS)
-    out[:, 0:8] = put(spread, hot_lane).reshape(32, 8, 128)
+    out[...] = put(spread, hot_lane).reshape(32, 8, 128)
 
 
 def total_kernel(parts, own, out):
-    total = jnp.sum(parts[:, 0:8], axis=0) + own[...]
+    total = jnp.sum(parts[...], axis=0) + own[...]
     out[...] = jnp.broadcast_to(total[None], (16, 8, 128))
 
 
-def force_kernel(parts, out):
+def force_kernel(parts, packs, out):
     total = jnp.sum(parts[...], axis=0)
     row = lax.broadcasted_iota(jnp.int32, (8, 128), 0)
 
@@ -166,66 +180,69 @@
     speed = jnp.sqrt(by_parity(jnp.where(row < 6, total * total, 0.0)))
     coef = by_parity(jnp.where(row < 6, 0.0, total))
     force = jnp.where(row < 6, -coef * speed * total, 0.0)
-    out[...] = jnp.broadcast_to(force[None], (32, 8, 128))
-
-
-def fill(grid, state, ylo, yhi, ghosts, first, second):
+    out[:, 0:8] = jnp.broadcast_to(force[None], (32, 8, 128))
+    above = (lax.axis_index("gz") + 1) & 3
+    for level in range(4):
+        pack = jnp.where(above == level, packs[1], packs[0])
+        for across in range(8):
+            out[4 * across + level, 8:16] = pack
+
+
+def beside(first, second):
+    even = (lax.axis_index("gx") & 1) == 0
+    first, second = first[...], second[...]
+    return jnp.where(even, second, first), jnp.where(even, first, second)
+
+
+def faces_kernel(state, first, second, yup, ydown, packs):
+    xlo, xhi = beside(first, second)
+    wide = jnp.concatenate([xlo, state[...], xhi], axis=1)
+    yup[...] = wide[:, 1:11, 6:8]
+    ydown[...] = wide[:, 1:11, 0:2]
+    ends = take_lanes((0, 1, 127, 126), wide.reshape(384, 128))
+    blank = jnp.zeros((2, 128), jnp.float32)
+    for side in range(2):
+        pieces = [
+            ends[2 * side + i : 2 * side + i + 1, 128 * j : 128 * j + 128]
+            for i in range(2)
+            for j in range(3)
+        ]
+        packs[side] = jnp.concatenate(pieces + [blank], axis=0)
+
+
+def fill(grid, parts, state, ylo, yhi, first, second):
+    gy, gz = lax.axis_index("gy"), lax.axis_index("gz")
+    xlo, xhi = beside(first, second)
+    grid[:, 0:2, 0:8, 0:128] = xlo
     grid[:, 2:10, 0:8, 0:128] = state[...]
-    grid[:, 2:10, 8:10, 0:128] = yhi[...]
-    grid[:, 2:10, 14:16, 0:128] = ylo[...]
-    grid[:, 2:10, :, 128:256] = ghosts[...]
-    even = (lax.axis_index("gx") & 1) == 0
-    for plane, near, slab in (
-        (0, 1, jnp.where(even, second[...], first[...])),
-        (10, 10, jnp.where(even, first[...], second[...])),
-    ):
-        grid[:, plane : plane + 2, 0:8, 0:128] = slab[:, 0:2]
-        grid[:, near, 8:16, 0:128] = slab[:, 2]
-        grid[:, near, 0:8, 128:256] = slab[:, 3]
-
-
-def faces_kernel(parts, state, ylo, yhi, first, second, ghosts):
-    gx, gy, gz = [lax.axis_index(axis) for axis in ("gx", "gy", "gz")]
-    lane = lax.broadcasted_iota(jnp.int32, (1, 256), 1)
-
-    def rows(across, up, top):
+    grid[:, 10:12, 0:8, 0:128] = xhi
+    grid[:, 1:11, 8:10, 0:128] = yhi[...]
+    grid[:, 1:11, 14:16, 0:128] = ylo[...]
+
+    def rows(across, up, far):
         pack = parts[((gy + across) & 7) * 4 + ((gz + (1 if up else 3)) & 3), 8:16]
-        found = jnp.concatenate([pack[top : top + 1], pack[top + 1 : top + 2]], axis=1)
+        found = jnp.concatenate([pack[i : i + 1] for i in range(3 * far, 3 * far + 3)], axis=1)
         return jnp.where(gz == (3 if up else 0), 0.0, found)
 
-    def edge(up, top):
-        y = lane & 7
-        beside = jnp.where(y == 0, rows(1, up, top), 0.0)
-        return jnp.where(y == 7, rows(7, up, top), beside)
-
-    inner = jnp.concatenate(
-        [rows(0, True, 0), rows(0, False, 2), rows(0, True, 4), rows(0, False, 6)], axis=0
-    )
-    inner = exact(inner, lanes(4, (0, 127, 1, 126)), (0,)).reshape(4, 8, 8, 128)
-    edges = jnp.concatenate([edge(True, 0), edge(False, 2)], axis=0)
-    ghosts[:, :, 0:8] = inner
-    ghosts[:, :, 8:16] = exact(edges, lanes(2, (0, 127)), (0,)).reshape(4, 8, 8, 128)
-
-    even = (gx & 1) == 0
-    row = lax.broadcasted_iota(jnp.int32, (1, 8, 128), 1)
-
-    def slab(x, near):
-        beside = jnp.where(
-            row == 0, yhi[:, near, 0:1], jnp.where(row == 7, ylo[:, near, 1:2], 0.0)
-        )
-        return [state[:, x], state[:, x + 1], beside, inner[:, near]]
-
-    for i, (high, low) in enumerate(zip(slab(6, 7), slab(0, 0))):
-        first[:, i] = jnp.where(even, high, low)
-        second[:, i] = jnp.where(even, low, high)
+    y = lax.broadcasted_iota(jnp.int32, (1, 384), 1) & 7
+
+    def edge(up):
+        over = jnp.where(y == 0, rows(1, up, 0), 0.0)
+        return jnp.where(y == 7, rows(7, up, 0), over)
+
+    inner = [rows(0, True, 0), rows(0, False, 0), rows(0, True, 1), rows(0, False, 1)]
+    inner = give_lanes(jnp.concatenate(inner, axis=0), (0, 127, 1, 126))
+    edges = give_lanes(jnp.concatenate([edge(True), edge(False)], axis=0), (0, 127))
+    grid[:, :, 0:8, 128:256] = inner.reshape(4, 12, 8, 128)
+    grid[:, :, 8:16, 128:256] = edges.reshape(4, 12, 8, 128)
 
 
 def final_kernel(
-    parts, cell, dest, elem, weight, state, ylo, yhi, ghosts, first, second, *results
+    parts, cell, dest, elem, weight, state, ylo, yhi, first, second, *results
 ):
     new_state, body_force, grid = results
     match, hot_lane = element_keys(dest[...], elem[...])
-    found = pick(parts[...].reshape(256, 128), hot_lane).reshape(32, 8, ROWS)
+    found = pick(parts[:, 0:8].reshape(256, 128), hot_lane).reshape(32, 8, ROWS)
     pairs = jnp.sum(jnp.where(match, found, 0.0), axis=0)
     column, hot_z = cell_keys(cell[...])
     each = [(pairs[2 * c : 2 * c + 1] + pairs[2 * c + 1 : 2 * c + 2]) * weight[...] for c in range(3)]
@@ -234,7 +251,7 @@
     body_force[...] = body
 
     gz = lax.axis_index("gz")
-    fill(grid, state, ylo, yhi, ghosts, first, second)
+    fill(grid, parts, state, ylo, yhi, first, second)
     level = lax.broadcasted_iota(jnp.int32, (1, 1, 256), 2)
     outside = ((level >= 128) & (level < 192) & (gz == 3)) | ((level >= 192) & (gz == 0))
 
@@ -317,35 +334,35 @@
         pltpu.VMEM((1, 128), jnp.float32),
         pltpu.SemaphoreType.DMA((7,)),
     )
-    side = f32(4, 8, 2, 128)
-    partial, own, yup, ydown = call(
+    slab = f32(4, 2, 8, 128)
+    parts, own, first, second = call(
         sample_kernel,
-        (f32(32, 16, 128), f32(8, 128), side, side),
+        (f32(32, 8, 128), f32(8, 128), slab, slab),
         held,
         7,
         pltpu.HBM,
         60 * 1024 * 1024,
     )(state, cell, dest, elem, weight, element_motion, coef)
-    parts = exchange(partial, PLANE)
+    parts = exchange(parts, PLANE)
+    first = swap(first, "gx", 0)
+    parts, first = lax.optimization_barrier((parts, first))
+
+    totals = call(total_kernel, f32(16, 8, 128), count=2)(parts, own)
+    totals, second = lax.optimization_barrier((totals, second))
+    totals = exchange(totals, "gx")
+    second = swap(second, "gx", 1)
+    side = f32(4, 10, 2, 128)
+    yup, ydown, packs = call(faces_kernel, (side, side, f32(2, 8, 128)), count=3)(
+        state, first, second
+    )
+
+    forces = call(force_kernel, f32(32, 16, 128), count=2)(totals, packs)
+    forces, yup, ydown = lax.optimization_barrier((forces, yup, ydown))
+    forces = exchange(forces, PLANE)
     ylo, yhi = shift(yup, ydown, "gy")
-    parts, ylo, yhi = lax.optimization_barrier((parts, ylo, yhi))
-
-    totals = call(total_kernel, f32(16, 8, 128), count=2)(parts, own)
-    totals = exchange(totals, "gx")
-    slab = f32(4, 4, 8, 128)
-    first, second, ghosts = call(faces_kernel, (slab, slab, f32(4, 8, 16, 128)), count=4)(
-        parts, state, ylo, yhi
-    )
-    first = swap(first, "gx", 0)
-    totals, first = lax.optimization_barrier((totals, first))
-
-    forces = call(force_kernel, f32(32, 8, 128), count=1)(totals)
-    forces, second = lax.optimization_barrier((forces, second))
-    forces = exchange(forces, PLANE)
-    second = swap(second, "gx", 1)
     grid = pltpu.VMEM((4, 12, 16, 256), jnp.float32)
-    return call(final_kernel, (f32(4, 8, 8, 128), f32(3, 8, 8, 128)), (grid,), 11)(
-        forces, cell, dest, elem, weight, state, ylo, yhi, ghosts, first, second
+    return call(final_kernel, (f32(4, 8, 8, 128), f32(3, 8, 8, 128)), (grid,), 10)(
+        forces, cell, dest, elem, weight, state, ylo, yhi, first, second
     )
 
 

time: 64.6 us -> 65.8 us (1.019)
  starting transfers between devices: 37.6 us -> 39 us
    all_to_all x3, starting transfers between devices: 29.4 us -> 30.9 us  [exchange(): return lax.all_to_all(blocks, axes, split_axis=0, concat_axis=0, tiled=True)]
  transfers between devices with their start and end apart: 7 -> 7, of which waited for: 7 -> 7; matrix products, arithmetic and copies ran while one was open for 0% -> 0% of each run, Pallas kernels for 1% -> 0%
where the time goes in v6:
time: 65.8 us; the launch traced here: 65.3 us
  starting transfers between devices  39 us (59%)
  waiting for transfers between devices  19.9 us (30%)
  Pallas kernels  5.74 us (9%)
  between operations  0.73 us (1%)
    all_to_all x3, starting transfers between devices, exchange(): return lax.all_to_all(blocks, axes, split_axis=0, concat_axis=0, tiled=True)  30.9 us
    all_to_all x3, waiting for transfers between devices, exchange(): return lax.all_to_all(blocks, axes, split_axis=0, concat_axis=0, tiled=True)  10.3 us
    ppermute x2, starting transfers between devices, swap(): lax.ppermute(slab, axis, [(i, (i + 1 if i % 2 == odd else i - 1) % count)...  6.41 us
    ppermute x2, waiting for transfers between devices, swap(): lax.ppermute(slab, axis, [(i, (i + 1 if i % 2 == odd else i - 1) % count)...  5.22 us
    ppermute x2, waiting for transfers between devices, shift(): return (lax.ppermute(up, axis, forward), lax.ppermute(down, axis, backward))  4.33 us
    pallas_call x1, Pallas kernels, body(): call(sample_kernel, (f32(32, 8, 128), f32(8, 128), slab, slab), held, 7,...  2.36 us
    pallas_call x1, Pallas kernels, body(): call(final_kernel, (f32(4, 8, 8, 128), f32(3, 8, 8, 128)), (grid,), 10)  1.75 us
    ppermute x2, starting transfers between devices, shift(): return (lax.ppermute(up, axis, forward), lax.ppermute(down, axis, backward))  1.65 us
  transfers between devices with their start and end apart: 7, of which 7 were waited for; matrix products, arithmetic and copies ran while one was open for 0% of the time, Pallas kernels for 0%

profile of v6, /device:TPU:1, one launch (start us, length us, event | category | flops | bytes accessed | tf_op | source)
XLA Modules:
  0.0 65.3 jit_solution(14292176557005389104)
XLA Ops:
  0.6 2.4 %shard_map.86 = (f32[32,8,128]{2,1,0:T(8,128)}, f32[8,128]{1,0:T(8,128)}, f32[4,2,8,128]{3,2,1,0:T(8,128)}, f32[4,2,8,128]{3,2,1,0:T(8,128)}) custom-call(f32[4,8,8,128]{3,2,1,0:T(8,128)} %state.3, s32[1,1024]{1,0:T(1,128)} %bitcast.5, s32[1,1024]{1,0:T(1,128)} %bitcast.7, s32[1,1024]{1,0:T(1,128)} %bitcast.9, f32[1,1024]{1,0:T(1,128)} %bitcast.11, ...), custom_call_target="tpu_custom_call" | custom-call | flops 2000000 | bytes 1000000 | tf_op jit(solution)/shard_map/pallas_call | solution.py:338
  3.0 0.0 copy-start.7
  3.0 0.0 copy-start.5
  3.0 10.4 %all-to-all-start = ((f32[32,8,128]{2,1,0:T(8,128)}), f32[32,8,128]{2,1,0:T(8,128)S(1)}, u32[]{:S(2)}, u32[]{:S(2)}) async-start(f32[32,8,128]{2,1,0:T(8,128)} %get-tuple-element.16), calls=%async_computation | async-start | bytes 262144 | tf_op jit(solution)/shard_map/all_to_all | solution.py:316
  13.5 0.0 copy-done.7
  13.5 1.9 %collective-permute-start = (f32[4,2,8,128]{3,2,1,0:T(8,128)S(1)}, f32[4,2,8,128]{3,2,1,0:T(8,128)S(1)}, u32[]{:S(2)}, u32[]{:S(2)}) collective-permute-start(f32[4,2,8,128]{3,2,1,0:T(8,128)S(1)} %copy-done.7), channel_id=1, source_target_pairs={{0,32},{32,0},{64,96},{96,64},{128,160},{160,128},{192,224},{224,1... | collective-permute-start | bytes 98312 | tf_op jit(solution)/shard_map/ppermute | solution.py:310
  15.4 3.0 %collective-permute-done.first = f32[4,2,8,128]{3,2,1,0:T(8,128)S(1)} collective-permute-done((f32[4,2,8,128]{3,2,1,0:T(8,128)S(1)}, f32[4,2,8,128]{3,2,1,0:T(8,128)S(1)}, u32[]{:S(2)}, u32[]{:S(2)}) %collective-permute-start) | collective-permute-done | bytes 32800 | tf_op jit(solution)/shard_map/ppermute | solution.py:310
  18.4 2.7 %all-to-all-done.parts = f32[32,8,128]{2,1,0:T(8,128)S(1)} async-done(((f32[32,8,128]{2,1,0:T(8,128)}), f32[32,8,128]{2,1,0:T(8,128)S(1)}, u32[]{:S(2)}, u32[]{:S(2)}) %all-to-all-start) | async-done | bytes 131104 | tf_op jit(solution)/shard_map/all_to_all | solution.py:316
  21.1 0.0 copy-done.5
  21.1 0.7 %shard_map.87 = f32[16,8,128]{2,1,0:T(8,128)} custom-call(f32[32,8,128]{2,1,0:T(8,128)S(1)} %all-to-all-done.parts, f32[8,128]{1,0:T(8,128)S(1)} %copy-done.5), custom_call_target="tpu_custom_call" | custom-call | flops 2000000 | bytes 1000000 | tf_op jit(solution)/shard_map/pallas_call | solution.py:350
  21.8 0.0 copy-start.6
  21.8 13.1 %all-to-all-start.1 = ((f32[16,8,128]{2,1,0:T(8,128)}), f32[16,8,128]{2,1,0:T(8,128)S(1)}, u32[]{:S(2)}, u32[]{:S(2)}) async-start(f32[16,8,128]{2,1,0:T(8,128)} %shard_map.87), calls=%async_computation.1 | async-start | bytes 131072 | tf_op jit(solution)/shard_map/all_to_all | solution.py:316
  34.9 0.0 copy-done.6
  34.9 4.5 %collective-permute-start.1 = (f32[4,2,8,128]{3,2,1,0:T(8,128)S(1)}, f32[4,2,8,128]{3,2,1,0:T(8,128)S(1)}, u32[]{:S(2)}, u32[]{:S(2)}) collective-permute-start(f32[4,2,8,128]{3,2,1,0:T(8,128)S(1)} %copy-done.6), channel_id=1, source_target_pairs={{0,480},{32,64},{64,32},{96,128},{128,96},{160,192},{192,160},{224... | collective-permute-start | bytes 98312 | tf_op jit(solution)/shard_map/ppermute | solution.py:310
  39.4 2.2 %collective-permute-done.1.second = f32[4,2,8,128]{3,2,1,0:T(8,128)S(1)} collective-permute-done((f32[4,2,8,128]{3,2,1,0:T(8,128)S(1)}, f32[4,2,8,128]{3,2,1,0:T(8,128)S(1)}, u32[]{:S(2)}, u32[]{:S(2)}) %collective-permute-start.1) | collective-permute-done | bytes 32800 | tf_op jit(solution)/shard_map/ppermute | solution.py:310
  41.6 0.0 copy-done
  41.6 0.2 shard_map.88
  41.9 4.6 %all-to-all-done.1.parts = f32[16,8,128]{2,1,0:T(8,128)S(1)} async-done(((f32[16,8,128]{2,1,0:T(8,128)}), f32[16,8,128]{2,1,0:T(8,128)S(1)}, u32[]{:S(2)}, u32[]{:S(2)}) %all-to-all-start.1) | async-done | bytes 65568 | tf_op jit(solution)/shard_map/all_to_all | solution.py:316
  46.5 0.7 %shard_map.89 = f32[32,16,128]{2,1,0:T(8,128)} custom-call(f32[16,8,128]{2,1,0:T(8,128)S(1)} %all-to-all-done.1.parts, f32[2,8,128]{2,1,0:T(8,128)S(1)} %get-tuple-element.24.packs), custom_call_target="tpu_custom_call" | custom-call | flops 2000000 | bytes 1000000 | tf_op jit(solution)/shard_map/pallas_call | solution.py:359
  47.2 0.0 copy-start.1
  47.2 0.0 copy-start.2
  47.2 7.3 %all-to-all-start.2 = ((f32[32,16,128]{2,1,0:T(8,128)}), f32[32,16,128]{2,1,0:T(8,128)S(1)}, u32[]{:S(2)}, u32[]{:S(2)}) async-start(f32[32,16,128]{2,1,0:T(8,128)} %shard_map.89), calls=%async_computation.2 | async-start | bytes 524288 | tf_op jit(solution)/shard_map/all_to_all | solution.py:316
  54.6 1.6 %collective-permute-start.2 = (f32[4,10,2,128]{3,2,1,0:T(2,128)S(1)}, f32[4,10,2,128]{3,2,1,0:T(2,128)S(1)}, u32[]{:S(2)}, u32[]{:S(2)}) collective-permute-start(f32[4,10,2,128]{3,2,1,0:T(2,128)S(1)} %get-tuple-element.28), channel_id=1, source_target_pairs={{0,4},{4,8},{8,12},{12,16},{16,20},{20,24},{24,28},{28,0},{1,5},{5... | collective-permute-start | bytes 122888 | tf_op jit(solution)/shard_map/ppermute | solution.py:305
  56.2 0.0 collective-permute-start.3
  56.2 2.3 %collective-permute-done.2.ylo = f32[4,10,2,128]{3,2,1,0:T(2,128)S(1)} collective-permute-done((f32[4,10,2,128]{3,2,1,0:T(2,128)S(1)}, f32[4,10,2,128]{3,2,1,0:T(2,128)S(1)}, u32[]{:S(2)}, u32[]{:S(2)}) %collective-permute-start.2) | collective-permute-done | bytes 40992 | tf_op jit(solution)/shard_map/ppermute | solution.py:305
  58.5 2.1 %collective-permute-done.3.yhi = f32[4,10,2,128]{3,2,1,0:T(2,128)S(1)} collective-permute-done((f32[4,10,2,128]{3,2,1,0:T(2,128)S(1)}, f32[4,10,2,128]{3,2,1,0:T(2,128)S(1)}, u32[]{:S(2)}, u32[]{:S(2)}) %collective-permute-start.3) | collective-permute-done | bytes 40992 | tf_op jit(solution)/shard_map/ppermute | solution.py:305
  60.6 3.0 %all-to-all-done.2.parts = f32[32,16,128]{2,1,0:T(8,128)S(1)} async-done(((f32[32,16,128]{2,1,0:T(8,128)}), f32[32,16,128]{2,1,0:T(8,128)S(1)}, u32[]{:S(2)}, u32[]{:S(2)}) %all-to-all-start.2) | async-done | bytes 262176 | tf_op jit(solution)/shard_map/all_to_all | solution.py:316
  63.5 0.0 copy-done.1
  63.5 0.0 copy-done.2
  63.5 0.0 copy-done.3
  63.5 0.0 copy-done.4
  63.5 1.8 %shard_map.90 = (f32[4,8,8,128]{3,2,1,0:T(8,128)}, f32[3,8,8,128]{3,2,1,0:T(8,128)}) custom-call(f32[32,16,128]{2,1,0:T(8,128)S(1)} %all-to-all-done.2.parts, s32[1,1024]{1,0:T(1,128)S(1)} %bitcast.6, s32[1,1024]{1,0:T(1,128)S(1)} %bitcast.8, s32[1,1024]{1,0:T(1,128)S(1)} %bitcast.10, f32[1,1024]{1,0:T(1,128)S(1)} %bitcast.12, f32[4,8,8,128]{3,2,1,0:T(8,128)S(1)} %copy-done, ...), custom_call_target="tpu_custom_call" | custom-call | flops 2000000 | bytes 1000000 | tf_op jit(solution)/shard_map/pallas_call | solution.py:364
  (3 shorter events, 0.0 us)
Async XLA Ops:
  3.0 10.5 %copy-start.7 = (f32[4,2,8,128]{3,2,1,0:T(8,128)S(1)}, f32[4,2,8,128]{3,2,1,0:T(8,128)}, u32[]{:S(2)}) copy-start(f32[4,2,8,128]{3,2,1,0:T(8,128)} %get-tuple-element.17) | copy-start | bytes 98308
  3.0 18.1 %copy-start.5 = (f32[8,128]{1,0:T(8,128)S(1)}, f32[8,128]{1,0:T(8,128)}, u32[]{:S(2)}) copy-start(f32[8,128]{1,0:T(8,128)} %get-tuple-element.19.own) | copy-start | bytes 12292
  3.0 18.1 %all-to-all-start = ((f32[32,8,128]{2,1,0:T(8,128)}), f32[32,8,128]{2,1,0:T(8,128)S(1)}, u32[]{:S(2)}, u32[]{:S(2)}) async-start(f32[32,8,128]{2,1,0:T(8,128)} %get-tuple-element.16), calls=%async_computation | async-start | bytes 262144 | tf_op jit(solution)/shard_map/all_to_all | solution.py:316
  13.5 5.0 %collective-permute-start = (f32[4,2,8,128]{3,2,1,0:T(8,128)S(1)}, f32[4,2,8,128]{3,2,1,0:T(8,128)S(1)}, u32[]{:S(2)}, u32[]{:S(2)}) collective-permute-start(f32[4,2,8,128]{3,2,1,0:T(8,128)S(1)} %copy-done.7), channel_id=1, source_target_pairs={{0,32},{32,0},{64,96},{96,64},{128,160},{160,128},{192,224},{224,1... | collective-permute-start | bytes 98312 | tf_op jit(solution)/shard_map/ppermute | solution.py:310
  21.1 20.5 %copy-start = (f32[4,8,8,128]{3,2,1,0:T(8,128)S(1)}, f32[4,8,8,128]{3,2,1,0:T(8,128)}, u32[]{:S(2)}) copy-start(f32[4,8,8,128]{3,2,1,0:T(8,128)} %state.3) | copy-start | bytes 393220
  21.8 13.1 %copy-start.6 = (f32[4,2,8,128]{3,2,1,0:T(8,128)S(1)}, f32[4,2,8,128]{3,2,1,0:T(8,128)}, u32[]{:S(2)}) copy-start(f32[4,2,8,128]{3,2,1,0:T(8,128)} %get-tuple-element.23) | copy-start | bytes 98308
  21.8 24.7 %all-to-all-start.1 = ((f32[16,8,128]{2,1,0:T(8,128)}), f32[16,8,128]{2,1,0:T(8,128)S(1)}, u32[]{:S(2)}, u32[]{:S(2)}) async-start(f32[16,8,128]{2,1,0:T(8,128)} %shard_map.87), calls=%async_computation.1 | async-start | bytes 131072 | tf_op jit(solution)/shard_map/all_to_all | solution.py:316
  34.9 6.7 %collective-permute-start.1 = (f32[4,2,8,128]{3,2,1,0:T(8,128)S(1)}, f32[4,2,8,128]{3,2,1,0:T(8,128)S(1)}, u32[]{:S(2)}, u32[]{:S(2)}) collective-permute-start(f32[4,2,8,128]{3,2,1,0:T(8,128)S(1)} %copy-done.6), channel_id=1, source_target_pairs={{0,480},{32,64},{64,32},{96,128},{128,96},{160,192},{192,160},{224... | collective-permute-start | bytes 98312 | tf_op jit(solution)/shard_map/ppermute | solution.py:310
  47.2 16.3 %copy-start.1 = (s32[1024]{0:T(1024)S(1)}, s32[1024]{0:T(1024)}, u32[]{:S(2)}) copy-start(s32[1024]{0:T(1024)} %param.8) | copy-start | bytes 12292
  47.2 16.3 %copy-start.2 = (s32[1024,1]{0,1:T(1,128)S(1)}, s32[1024,1]{0,1:T(1,128)}, u32[]{:S(2)}) copy-start(s32[1024,1]{0,1:T(1,128)} %param.9) | copy-start | bytes 12292
  47.2 16.3 %copy-start.3 = (s32[1024]{0:T(1024)S(1)}, s32[1024]{0:T(1024)}, u32[]{:S(2)}) copy-start(s32[1024]{0:T(1024)} %param.11) | copy-start | bytes 12292
  47.2 16.3 %copy-start.4 = (f32[1024]{0:T(1024)S(1)}, f32[1024]{0:T(1024)}, u32[]{:S(2)}) copy-start(f32[1024]{0:T(1024)} %param.10) | copy-start | bytes 12292
  47.2 16.3 %all-to-all-start.2 = ((f32[32,16,128]{2,1,0:T(8,128)}), f32[32,16,128]{2,1,0:T(8,128)S(1)}, u32[]{:S(2)}, u32[]{:S(2)}) async-start(f32[32,16,128]{2,1,0:T(8,128)} %shard_map.89), calls=%async_computation.2 | async-start | bytes 524288 | tf_op jit(solution)/shard_map/all_to_all | solution.py:316
  54.6 3.9 %collective-permute-start.2 = (f32[4,10,2,128]{3,2,1,0:T(2,128)S(1)}, f32[4,10,2,128]{3,2,1,0:T(2,128)S(1)}, u32[]{:S(2)}, u32[]{:S(2)}) collective-permute-start(f32[4,10,2,128]{3,2,1,0:T(2,128)S(1)} %get-tuple-element.28), channel_id=1, source_target_pairs={{0,4},{4,8},{8,12},{12,16},{16,20},{20,24},{24,28},{28,0},{1,5},{5... | collective-permute-start | bytes 122888 | tf_op jit(solution)/shard_map/ppermute | solution.py:305
  56.2 4.3 %collective-permute-start.3 = (f32[4,10,2,128]{3,2,1,0:T(2,128)S(1)}, f32[4,10,2,128]{3,2,1,0:T(2,128)S(1)}, u32[]{:S(2)}, u32[]{:S(2)}) collective-permute-start(f32[4,10,2,128]{3,2,1,0:T(2,128)S(1)} %get-tuple-element.29), channel_id=1, source_target_pairs={{4,0},{8,4},{12,8},{16,12},{20,16},{24,20},{28,24},{0,28},{5,1},{9... | collective-permute-start | bytes 122888 | tf_op jit(solution)/shard_map/ppermute | solution.py:305

commit v7 on v4

--- a/solution.py
+++ b/solution.py
@@ -94,12 +94,28 @@
     return jnp.where(hot, 1.0, 0.0)
 
 
-def exact(left, right, dims):
+def thirds(values):
+    high, rest = halves(values)
+    low = values - high.astype(jnp.float32) - rest.astype(jnp.float32)
+    return high, rest, low.astype(jnp.bfloat16)
+
+
+def take_lanes(places, rows):
+    hot = lanes(8, places).astype(jnp.bfloat16)
+    dims = (((1,), (1,)), ((), ()))
+    parts = [
+        lax.dot_general(hot, part, dims, preferred_element_type=jnp.float32)
+        for part in thirds(rows)
+    ]
+    return parts[0] + parts[1] + parts[2]
+
+
+def give_lanes(rows, places):
+    hot = lanes(len(places), places)
     return lax.dot_general(
-        left,
-        right,
-        ((dims, dims), ((), ())),
-        precision=lax.Precision.HIGHEST,
+        jnp.concatenate(thirds(rows), axis=0),
+        jnp.concatenate([hot, hot, hot], axis=0).astype(jnp.bfloat16),
+        (((0,), (0,)), ((), ())),
         preferred_element_type=jnp.float32,
     )
 
@@ -132,7 +148,7 @@
     own[...] = own_part(motion, coef)
     yup[...] = state[:, :, 6:8]
     ydown[...] = state[:, :, 0:2]
-    ends = exact(lanes(8, (0, 127, 1, 126)), state[...].reshape(256, 128), (1,))
+    ends = take_lanes((0, 127, 1, 126), state[...].reshape(256, 128))
     pack = [ends[i : i + 1, 128 * j : 128 * j + 128] for i in range(4) for j in range(2)]
     out[:, 8:16] = jnp.broadcast_to(jnp.concatenate(pack, axis=0)[None], (32, 8, 128))
     column, hot_z = cell_keys(cell[...])
@@ -175,13 +191,20 @@
     grid[:, 2:10, 14:16, 0:128] = ylo[...]
     grid[:, 2:10, :, 128:256] = ghosts[...]
     even = (lax.axis_index("gx") & 1) == 0
+    row = lax.broadcasted_iota(jnp.int32, (8, 128), 0)
+    column = lax.broadcasted_iota(jnp.int32, (8, 128), 1)
+    outer = (column == 0) | (column == 127)
     for plane, near, slab in (
         (0, 1, jnp.where(even, second[...], first[...])),
         (10, 10, jnp.where(even, first[...], second[...])),
     ):
-        grid[:, plane : plane + 2, 0:8, 0:128] = slab[:, 0:2]
-        grid[:, near, 8:16, 0:128] = slab[:, 2]
-        grid[:, near, 0:8, 128:256] = slab[:, 3]
+        for c in range(4):
+            grid[c, plane, 0:8, 0:128] = slab[2 * c]
+            grid[c, plane + 1, 0:8, 0:128] = slab[2 * c + 1]
+            over, under = slab[8, 2 * c : 2 * c + 1], slab[8, 2 * c + 1 : 2 * c + 2]
+            grid[c, near, 8:16, 0:128] = jnp.where(row == 0, over, jnp.where(row == 7, under, 0.0))
+            ends = slab[9] if c == 0 else pltpu.roll(slab[9], 128 - 2 * c, 1)
+            grid[c, near, 0:8, 128:256] = jnp.where(outer, ends, 0.0)
 
 
 def faces_kernel(parts, state, ylo, yhi, first, second, ghosts):
@@ -201,23 +224,25 @@
     inner = jnp.concatenate(
         [rows(0, True, 0), rows(0, False, 2), rows(0, True, 4), rows(0, False, 6)], axis=0
     )
-    inner = exact(inner, lanes(4, (0, 127, 1, 126)), (0,)).reshape(4, 8, 8, 128)
+    inner = give_lanes(inner, (0, 127, 1, 126)).reshape(4, 8, 8, 128)
     edges = jnp.concatenate([edge(True, 0), edge(False, 2)], axis=0)
     ghosts[:, :, 0:8] = inner
-    ghosts[:, :, 8:16] = exact(edges, lanes(2, (0, 127)), (0,)).reshape(4, 8, 8, 128)
+    ghosts[:, :, 8:16] = give_lanes(edges, (0, 127)).reshape(4, 8, 8, 128)
 
     even = (gx & 1) == 0
-    row = lax.broadcasted_iota(jnp.int32, (1, 8, 128), 1)
+    column = lax.broadcasted_iota(jnp.int32, (8, 128), 1)
+    outer = (column == 0) | (column == 127)
 
     def slab(x, near):
-        beside = jnp.where(
-            row == 0, yhi[:, near, 0:1], jnp.where(row == 7, ylo[:, near, 1:2], 0.0)
-        )
-        return [state[:, x], state[:, x + 1], beside, inner[:, near]]
+        tiles = [state[c, x + i] for c in range(4) for i in range(2)]
+        across = [part[c, near, i : i + 1] for c in range(4) for part, i in ((yhi, 0), (ylo, 1))]
+        ends = [jnp.where(outer, inner[c, near], 0.0) for c in range(4)]
+        ends = [ends[0]] + [pltpu.roll(ends[c], 2 * c, 1) for c in range(1, 4)]
+        return tiles + [jnp.concatenate(across, axis=0), ends[0] + ends[1] + ends[2] + ends[3]]
 
     for i, (high, low) in enumerate(zip(slab(6, 7), slab(0, 0))):
-        first[:, i] = jnp.where(even, high, low)
-        second[:, i] = jnp.where(even, low, high)
+        first[i] = jnp.where(even, high, low)
+        second[i] = jnp.where(even, low, high)
 
 
 def final_kernel(
@@ -332,17 +357,15 @@
 
     totals = call(total_kernel, f32(16, 8, 128), count=2)(parts, own)
     totals = exchange(totals, "gx")
-    slab = f32(4, 4, 8, 128)
+    slab = f32(10, 8, 128)
     first, second, ghosts = call(faces_kernel, (slab, slab, f32(4, 8, 16, 128)), count=4)(
         parts, state, ylo, yhi
     )
-    first = swap(first, "gx", 0)
-    totals, first = lax.optimization_barrier((totals, first))
+    first, second = swap(first, "gx", 0), swap(second, "gx", 1)
+    totals, first, second = lax.optimization_barrier((totals, first, second))
 
     forces = call(force_kernel, f32(32, 8, 128), count=1)(totals)
-    forces, second = lax.optimization_barrier((forces, second))
     forces = exchange(forces, PLANE)
-    second = swap(second, "gx", 1)
     grid = pltpu.VMEM((4, 12, 16, 256), jnp.float32)
     return call(final_kernel, (f32(4, 8, 8, 128), f32(3, 8, 8, 128)), (grid,), 11)(
         forces, cell, dest, elem, weight, state, ylo, yhi, ghosts, first, second

time: 64.6 us -> 63.3 us (0.980)
  blocking collectives: 0 us -> 13 us
  waiting for transfers between devices: 19.6 us -> 11 us
  starting transfers between devices: 37.6 us -> 32.8 us
  Pallas kernels: 6.12 us -> 5.28 us
    all_to_all x0 -> x1, blocking collectives: none -> 13 us  [exchange(): return lax.all_to_all(blocks, axes, split_axis=0, concat_axis=0, tiled=True)]
    all_to_all x3 -> x2, starting transfers between devices: 29.4 us -> 23.6 us  [exchange(): return lax.all_to_all(blocks, axes, split_axis=0, concat_axis=0, tiled=True)]
    all_to_all x3 -> x2, waiting for transfers between devices: 9.78 us -> 4.81 us  [exchange(): return lax.all_to_all(blocks, axes, split_axis=0, concat_axis=0, tiled=True)]
    ppermute x2, waiting for transfers between devices: 5.58 us -> 1.94 us  [swap(): lax.ppermute(slab, axis, [(i, (i + 1 if i % 2 == odd else i - 1) % count)...]
    ppermute x2, starting transfers between devices: 6.49 us -> 7.57 us  [swap(): lax.ppermute(slab, axis, [(i, (i + 1 if i % 2 == odd else i - 1) % count)...]
    pallas_call x1, Pallas kernels: 0.7 us -> 0.04 us  [body(): forces = call(force_kernel, f32(32, 8, 128), count=1)(totals)]
  transfers between devices with their start and end apart: 7 -> 6, of which waited for: 7 -> 5; matrix products, arithmetic and copies ran while one was open for 0% -> 0% of each run, Pallas kernels for 1% -> 0%
where the time goes in v7:
time: 63.3 us; the launch traced here: 62.9 us
  starting transfers between devices  32.8 us (52%)
  blocking collectives  13 us (21%)
  waiting for transfers between devices  11 us (17%)
  Pallas kernels  5.28 us (8%)
  between operations  0.77 us (1%)
    all_to_all x2, starting transfers between devices, exchange(): return lax.all_to_all(blocks, axes, split_axis=0, concat_axis=0, tiled=True)  23.6 us
    all_to_all x1, blocking collectives, exchange(): return lax.all_to_all(blocks, axes, split_axis=0, concat_axis=0, tiled=True)  13 us
    ppermute x2, starting transfers between devices, swap(): lax.ppermute(slab, axis, [(i, (i + 1 if i % 2 == odd else i - 1) % count)...  7.57 us
    all_to_all x2, waiting for transfers between devices, exchange(): return lax.all_to_all(blocks, axes, split_axis=0, concat_axis=0, tiled=True)  4.81 us
    ppermute x2, waiting for transfers between devices, shift(): return (lax.ppermute(up, axis, forward), lax.ppermute(down, axis, backward))  4.22 us
    pallas_call x1, Pallas kernels, body(): call(sample_kernel, (f32(32, 16, 128), f32(8, 128), side, side), held, 7,...  2.4 us
    ppermute x2, waiting for transfers between devices, swap(): lax.ppermute(slab, axis, [(i, (i + 1 if i % 2 == odd else i - 1) % count)...  1.94 us
    pallas_call x1, Pallas kernels, body(): call(final_kernel, (f32(4, 8, 8, 128), f32(3, 8, 8, 128)), (grid,), 11)  1.87 us
  transfers between devices with their start and end apart: 6, of which 5 were waited for; matrix products, arithmetic and copies ran while one was open for 0% of the time, Pallas kernels for 0%

profile of v7, /device:TPU:1, one launch (start us, length us, event | category | flops | bytes accessed | tf_op | source)
XLA Modules:
  0.0 62.9 jit_solution(15067643979041645961)
XLA Ops:
  0.6 2.4 %shard_map.86 = (f32[32,16,128]{2,1,0:T(8,128)}, f32[8,128]{1,0:T(8,128)}, f32[4,8,2,128]{3,2,1,0:T(2,128)}, f32[4,8,2,128]{3,2,1,0:T(2,128)}) custom-call(f32[4,8,8,128]{3,2,1,0:T(8,128)} %state.3, s32[1,1024]{1,0:T(1,128)} %bitcast.5, s32[1,1024]{1,0:T(1,128)} %bitcast.7, s32[1,1024]{1,0:T(1,128)} %bitcast.9, f32[1,1024]{1,0:T(1,128)} %bitcast.11, ...), custom_call_target="tpu_custom_call" | custom-call | flops 2000000 | bytes 1000000 | tf_op jit(solution)/shard_map/pallas_call | solution.py:346
  3.0 0.0 copy-start.7
  3.0 0.0 copy-start.6
  3.1 10.4 %all-to-all-start = ((f32[32,16,128]{2,1,0:T(8,128)}), f32[32,16,128]{2,1,0:T(8,128)S(1)}, u32[]{:S(2)}, u32[]{:S(2)}) async-start(f32[32,16,128]{2,1,0:T(8,128)} %get-tuple-element.15), calls=%async_computation | async-start | bytes 524288 | tf_op jit(solution)/shard_map/all_to_all | solution.py:324
  13.5 0.0 copy-start.5
  13.5 0.0 copy-done.7
  13.5 1.7 %collective-permute-start = (f32[4,8,2,128]{3,2,1,0:T(2,128)S(1)}, f32[4,8,2,128]{3,2,1,0:T(2,128)S(1)}, u32[]{:S(2)}, u32[]{:S(2)}) collective-permute-start(f32[4,8,2,128]{3,2,1,0:T(2,128)S(1)} %copy-done.7), channel_id=1, source_target_pairs={{0,4},{4,8},{8,12},{12,16},{16,20},{20,24},{24,28},{28,0},{1,5},{5... | collective-permute-start | bytes 98312 | tf_op jit(solution)/shard_map/ppermute | solution.py:313
  15.2 0.0 copy-done.6
  15.2 0.0 collective-permute-start.1
  15.2 2.1 %collective-permute-done.ylo = f32[4,8,2,128]{3,2,1,0:T(2,128)S(1)} collective-permute-done((f32[4,8,2,128]{3,2,1,0:T(2,128)S(1)}, f32[4,8,2,128]{3,2,1,0:T(2,128)S(1)}, u32[]{:S(2)}, u32[]{:S(2)}) %collective-permute-start) | collective-permute-done | bytes 32800 | tf_op jit(solution)/shard_map/ppermute | solution.py:313
  17.3 2.1 %collective-permute-done.1.yhi = f32[4,8,2,128]{3,2,1,0:T(2,128)S(1)} collective-permute-done((f32[4,8,2,128]{3,2,1,0:T(2,128)S(1)}, f32[4,8,2,128]{3,2,1,0:T(2,128)S(1)}, u32[]{:S(2)}, u32[]{:S(2)}) %collective-permute-start.1) | collective-permute-done | bytes 32800 | tf_op jit(solution)/shard_map/ppermute | solution.py:313
  19.4 3.1 %all-to-all-done.parts = f32[32,16,128]{2,1,0:T(8,128)S(1)} async-done(((f32[32,16,128]{2,1,0:T(8,128)}), f32[32,16,128]{2,1,0:T(8,128)S(1)}, u32[]{:S(2)}, u32[]{:S(2)}) %all-to-all-start) | async-done | bytes 262176 | tf_op jit(solution)/shard_map/all_to_all | solution.py:324
  22.5 0.0 copy-done.5
  22.5 0.7 %shard_map.87 = f32[16,8,128]{2,1,0:T(8,128)} custom-call(f32[32,16,128]{2,1,0:T(8,128)S(1)} %all-to-all-done.parts, f32[8,128]{1,0:T(8,128)S(1)} %copy-done.5), custom_call_target="tpu_custom_call" | custom-call | flops 2000000 | bytes 1000000 | tf_op jit(solution)/shard_map/pallas_call | solution.py:358
  23.2 13.1 %all-to-all-start.1 = ((f32[16,8,128]{2,1,0:T(8,128)}), f32[16,8,128]{2,1,0:T(8,128)S(1)}, u32[]{:S(2)}, u32[]{:S(2)}) async-start(f32[16,8,128]{2,1,0:T(8,128)} %shard_map.87), calls=%async_computation.1 | async-start | bytes 131072 | tf_op jit(solution)/shard_map/all_to_all | solution.py:324
  36.3 0.0 copy-done
  36.3 0.3 shard_map.88
  36.6 3.3 %collective-permute-start.2 = (f32[10,8,128]{2,1,0:T(8,128)S(1)}, f32[10,8,128]{2,1,0:T(8,128)S(1)}, u32[]{:S(2)}, u32[]{:S(2)}) collective-permute-start(f32[10,8,128]{2,1,0:T(8,128)S(1)} %get-tuple-element.22), channel_id=1, source_target_pairs={{0,32},{32,0},{64,96},{96,64},{128,160},{160,128},{192,224},{224,1... | collective-permute-start | bytes 122888 | tf_op jit(solution)/shard_map/ppermute | solution.py:318
  39.9 4.3 %collective-permute-start.3 = (f32[10,8,128]{2,1,0:T(8,128)S(1)}, f32[10,8,128]{2,1,0:T(8,128)S(1)}, u32[]{:S(2)}, u32[]{:S(2)}) collective-permute-start(f32[10,8,128]{2,1,0:T(8,128)S(1)} %get-tuple-element.23), channel_id=1, source_target_pairs={{0,480},{32,64},{64,32},{96,128},{128,96},{160,192},{192,160},{224... | collective-permute-start | bytes 122888 | tf_op jit(solution)/shard_map/ppermute | solution.py:318
  44.2 0.0 collective-permute-done.2.first
  44.2 1.9 %collective-permute-done.3.second = f32[10,8,128]{2,1,0:T(8,128)S(1)} collective-permute-done((f32[10,8,128]{2,1,0:T(8,128)S(1)}, f32[10,8,128]{2,1,0:T(8,128)S(1)}, u32[]{:S(2)}, u32[]{:S(2)}) %collective-permute-start.3) | collective-permute-done | bytes 40992 | tf_op jit(solution)/shard_map/ppermute | solution.py:318
  46.2 1.7 %all-to-all-done.1.parts = f32[16,8,128]{2,1,0:T(8,128)S(1)} async-done(((f32[16,8,128]{2,1,0:T(8,128)}), f32[16,8,128]{2,1,0:T(8,128)S(1)}, u32[]{:S(2)}, u32[]{:S(2)}) %all-to-all-start.1) | async-done | bytes 65568 | tf_op jit(solution)/shard_map/all_to_all | solution.py:324
  47.9 0.0 copy-start.1
  48.0 0.0 copy-start.2
  48.0 0.0 copy-start.3
  48.0 0.0 copy-start.4
  48.0 13.0 %all_to_all.15.parts = f32[32,8,128]{2,1,0:T(8,128)S(1)} all-to-all(f32[32,8,128]{2,1,0:T(8,128)S(1)} %shard_map.89), channel_id=1, replica_groups=mesh['gx'=16,'gy'=8,'gz'=4] {'gy','gz'}, dimensions={0} | all-to-all | bytes 262144 | tf_op jit(solution)/shard_map/all_to_all | solution.py:324
  61.0 0.0 copy-done.1
  61.0 0.0 copy-done.2
  61.0 0.0 copy-done.3
  61.0 0.0 copy-done.4
  61.0 1.9 %shard_map.90 = (f32[4,8,8,128]{3,2,1,0:T(8,128)}, f32[3,8,8,128]{3,2,1,0:T(8,128)}) custom-call(f32[32,8,128]{2,1,0:T(8,128)S(1)} %all_to_all.15.parts, s32[1,1024]{1,0:T(1,128)S(1)} %bitcast.6, s32[1,1024]{1,0:T(1,128)S(1)} %bitcast.8, s32[1,1024]{1,0:T(1,128)S(1)} %bitcast.10, f32[1,1024]{1,0:T(1,128)S(1)} %bitcast.12, f32[4,8,8,128]{3,2,1,0:T(8,128)S(1)} %copy-done, ...), custom_call_target="tpu_custom_call" | custom-call | flops 2000000 | bytes 1000000 | tf_op jit(solution)/shard_map/pallas_call | solution.py:370
  (2 shorter events, 0.0 us)
Async XLA Ops:
  3.0 10.5 %copy-start.7 = (f32[4,8,2,128]{3,2,1,0:T(2,128)S(1)}, f32[4,8,2,128]{3,2,1,0:T(2,128)}, u32[]{:S(2)}) copy-start(f32[4,8,2,128]{3,2,1,0:T(2,128)} %get-tuple-element.16) | copy-start | bytes 98308
  3.0 12.1 %copy-start.6 = (f32[4,8,2,128]{3,2,1,0:T(2,128)S(1)}, f32[4,8,2,128]{3,2,1,0:T(2,128)}, u32[]{:S(2)}) copy-start(f32[4,8,2,128]{3,2,1,0:T(2,128)} %get-tuple-element.17) | copy-start | bytes 98308
  3.1 19.5 %all-to-all-start = ((f32[32,16,128]{2,1,0:T(8,128)}), f32[32,16,128]{2,1,0:T(8,128)S(1)}, u32[]{:S(2)}, u32[]{:S(2)}) async-start(f32[32,16,128]{2,1,0:T(8,128)} %get-tuple-element.15), calls=%async_computation | async-start | bytes 524288 | tf_op jit(solution)/shard_map/all_to_all | solution.py:324
  13.5 9.0 %copy-start.5 = (f32[8,128]{1,0:T(8,128)S(1)}, f32[8,128]{1,0:T(8,128)}, u32[]{:S(2)}) copy-start(f32[8,128]{1,0:T(8,128)} %get-tuple-element.19.own) | copy-start | bytes 12292
  13.5 3.8 %collective-permute-start = (f32[4,8,2,128]{3,2,1,0:T(2,128)S(1)}, f32[4,8,2,128]{3,2,1,0:T(2,128)S(1)}, u32[]{:S(2)}, u32[]{:S(2)}) collective-permute-start(f32[4,8,2,128]{3,2,1,0:T(2,128)S(1)} %copy-done.7), channel_id=1, source_target_pairs={{0,4},{4,8},{8,12},{12,16},{16,20},{20,24},{24,28},{28,0},{1,5},{5... | collective-permute-start | bytes 98312 | tf_op jit(solution)/shard_map/ppermute | solution.py:313
  15.2 4.2 %collective-permute-start.1 = (f32[4,8,2,128]{3,2,1,0:T(2,128)S(1)}, f32[4,8,2,128]{3,2,1,0:T(2,128)S(1)}, u32[]{:S(2)}, u32[]{:S(2)}) collective-permute-start(f32[4,8,2,128]{3,2,1,0:T(2,128)S(1)} %copy-done.6), channel_id=1, source_target_pairs={{4,0},{8,4},{12,8},{16,12},{20,16},{24,20},{28,24},{0,28},{5,1},{9... | collective-permute-start | bytes 98312 | tf_op jit(solution)/shard_map/ppermute | solution.py:313
  23.2 13.1 %copy-start = (f32[4,8,8,128]{3,2,1,0:T(8,128)S(1)}, f32[4,8,8,128]{3,2,1,0:T(8,128)}, u32[]{:S(2)}) copy-start(f32[4,8,8,128]{3,2,1,0:T(8,128)} %state.3) | copy-start | bytes 393220
  23.2 24.7 %all-to-all-start.1 = ((f32[16,8,128]{2,1,0:T(8,128)}), f32[16,8,128]{2,1,0:T(8,128)S(1)}, u32[]{:S(2)}, u32[]{:S(2)}) async-start(f32[16,8,128]{2,1,0:T(8,128)} %shard_map.87), calls=%async_computation.1 | async-start | bytes 131072 | tf_op jit(solution)/shard_map/all_to_all | solution.py:324
  36.6 7.6 %collective-permute-start.2 = (f32[10,8,128]{2,1,0:T(8,128)S(1)}, f32[10,8,128]{2,1,0:T(8,128)S(1)}, u32[]{:S(2)}, u32[]{:S(2)}) collective-permute-start(f32[10,8,128]{2,1,0:T(8,128)S(1)} %get-tuple-element.22), channel_id=1, source_target_pairs={{0,32},{32,0},{64,96},{96,64},{128,160},{160,128},{192,224},{224,1... | collective-permute-start | bytes 122888 | tf_op jit(solution)/shard_map/ppermute | solution.py:318
  39.9 6.3 %collective-permute-start.3 = (f32[10,8,128]{2,1,0:T(8,128)S(1)}, f32[10,8,128]{2,1,0:T(8,128)S(1)}, u32[]{:S(2)}, u32[]{:S(2)}) collective-permute-start(f32[10,8,128]{2,1,0:T(8,128)S(1)} %get-tuple-element.23), channel_id=1, source_target_pairs={{0,480},{32,64},{64,32},{96,128},{128,96},{160,192},{192,160},{224... | collective-permute-start | bytes 122888 | tf_op jit(solution)/shard_map/ppermute | solution.py:318
  47.9 13.0 %copy-start.1 = (s32[1024]{0:T(1024)S(1)}, s32[1024]{0:T(1024)}, u32[]{:S(2)}) copy-start(s32[1024]{0:T(1024)} %param.8) | copy-start | bytes 12292
  48.0 13.0 %copy-start.2 = (s32[1024,1]{0,1:T(1,128)S(1)}, s32[1024,1]{0,1:T(1,128)}, u32[]{:S(2)}) copy-start(s32[1024,1]{0,1:T(1,128)} %param.9) | copy-start | bytes 12292
  48.0 13.0 %copy-start.3 = (s32[1024]{0:T(1024)S(1)}, s32[1024]{0:T(1024)}, u32[]{:S(2)}) copy-start(s32[1024]{0:T(1024)} %param.11) | copy-start | bytes 12292
  48.0 13.0 %copy-start.4 = (f32[1024]{0:T(1024)S(1)}, f32[1024]{0:T(1024)}, u32[]{:S(2)}) copy-start(f32[1024]{0:T(1024)} %param.10) | copy-start | bytes 12292

commit v8 on v7

--- a/solution.py
+++ b/solution.py
@@ -132,6 +132,7 @@
     own,
     yup,
     ydown,
+    far,
     *scratch,
 ):
     held, sems = scratch[:7], scratch[7]
@@ -149,8 +150,12 @@
     yup[...] = state[:, :, 6:8]
     ydown[...] = state[:, :, 0:2]
     ends = take_lanes((0, 127, 1, 126), state[...].reshape(256, 128))
-    pack = [ends[i : i + 1, 128 * j : 128 * j + 128] for i in range(4) for j in range(2)]
-    out[:, 8:16] = jnp.broadcast_to(jnp.concatenate(pack, axis=0)[None], (32, 8, 128))
+    blank = jnp.zeros((6, 128), jnp.float32)
+    low, high, far_low, far_high = [
+        jnp.concatenate([blank, ends[i : i + 1, 0:128], ends[i : i + 1, 128:256]], axis=0)
+        for i in range(4)
+    ]
+    far[0], far[1] = far_low, far_high
     column, hot_z = cell_keys(cell[...])
     found = pick(state[0:3].reshape(192, 128), hot_z).reshape(3, 64, ROWS)
     sampled = [
@@ -163,15 +168,21 @@
     )
     match, hot_lane = element_keys(dest[...], elem[...])
     spread = jnp.where(match, pattern[None], 0.0).reshape(256, ROWS)
-    out[:, 0:8] = put(spread, hot_lane).reshape(32, 8, 128)
+    sums = put(spread, hot_lane).reshape(32, 8, 128)
+    above = (lax.axis_index("gz") + 1) & 3
+    for level in range(4):
+        near = jnp.where(above == level, high, low)
+        for across in range(level, 32, 4):
+            out[across] = sums[across] + near
 
 
 def total_kernel(parts, own, out):
-    total = jnp.sum(parts[:, 0:8], axis=0) + own[...]
+    row = lax.broadcasted_iota(jnp.int32, (8, 128), 0)
+    total = jnp.where(row < 6, jnp.sum(parts[...], axis=0), 0.0) + own[...]
     out[...] = jnp.broadcast_to(total[None], (16, 8, 128))
 
 
-def force_kernel(parts, out):
+def force_kernel(parts, far, out):
     total = jnp.sum(parts[...], axis=0)
     row = lax.broadcasted_iota(jnp.int32, (8, 128), 0)
 
@@ -182,21 +193,27 @@
     speed = jnp.sqrt(by_parity(jnp.where(row < 6, total * total, 0.0)))
     coef = by_parity(jnp.where(row < 6, 0.0, total))
     force = jnp.where(row < 6, -coef * speed * total, 0.0)
-    out[...] = jnp.broadcast_to(force[None], (32, 8, 128))
-
-
-def fill(grid, state, ylo, yhi, ghosts, first, second):
+    above = (lax.axis_index("gz") + 1) & 3
+    for level in range(4):
+        block = force + jnp.where(above == level, far[1], far[0])
+        for across in range(level, 32, 4):
+            out[across] = block
+
+
+def fill(grid, parts, state, ylo, yhi, ghosts, first, second):
     grid[:, 2:10, 0:8, 0:128] = state[...]
     grid[:, 2:10, 8:10, 0:128] = yhi[...]
     grid[:, 2:10, 14:16, 0:128] = ylo[...]
-    grid[:, 2:10, :, 128:256] = ghosts[...]
-    even = (lax.axis_index("gx") & 1) == 0
+    far = jnp.concatenate([level_of(parts, 0, True), level_of(parts, 0, False)], axis=0)
+    far = give_lanes(far, (1, 126)).reshape(4, 8, 8, 128)
+    grid[:, 2:10, 0:8, 128:256] = ghosts[:, :, 0:8] + far
+    grid[:, 2:10, 8:16, 128:256] = ghosts[:, :, 8:16]
     row = lax.broadcasted_iota(jnp.int32, (8, 128), 0)
     column = lax.broadcasted_iota(jnp.int32, (8, 128), 1)
     outer = (column == 0) | (column == 127)
     for plane, near, slab in (
-        (0, 1, jnp.where(even, second[...], first[...])),
-        (10, 10, jnp.where(even, first[...], second[...])),
+        (0, 1, first[...]),
+        (10, 10, second[...]),
     ):
         for c in range(4):
             grid[c, plane, 0:8, 0:128] = slab[2 * c]
@@ -207,29 +224,27 @@
             grid[c, near, 0:8, 128:256] = jnp.where(outer, ends, 0.0)
 
 
+def level_of(parts, across, up):
+    gy, gz = lax.axis_index("gy"), lax.axis_index("gz")
+    block = parts[((gy + across) & 7) * 4 + ((gz + (1 if up else 3)) & 3)]
+    found = jnp.concatenate([block[6:7], block[7:8]], axis=1)
+    return jnp.where(gz == (3 if up else 0), 0.0, found)
+
+
 def faces_kernel(parts, state, ylo, yhi, first, second, ghosts):
-    gx, gy, gz = [lax.axis_index(axis) for axis in ("gx", "gy", "gz")]
     lane = lax.broadcasted_iota(jnp.int32, (1, 256), 1)
 
-    def rows(across, up, top):
-        pack = parts[((gy + across) & 7) * 4 + ((gz + (1 if up else 3)) & 3), 8:16]
-        found = jnp.concatenate([pack[top : top + 1], pack[top + 1 : top + 2]], axis=1)
-        return jnp.where(gz == (3 if up else 0), 0.0, found)
-
-    def edge(up, top):
+    def edge(up):
         y = lane & 7
-        beside = jnp.where(y == 0, rows(1, up, top), 0.0)
-        return jnp.where(y == 7, rows(7, up, top), beside)
-
-    inner = jnp.concatenate(
-        [rows(0, True, 0), rows(0, False, 2), rows(0, True, 4), rows(0, False, 6)], axis=0
-    )
-    inner = give_lanes(inner, (0, 127, 1, 126)).reshape(4, 8, 8, 128)
-    edges = jnp.concatenate([edge(True, 0), edge(False, 2)], axis=0)
+        beside = jnp.where(y == 0, level_of(parts, 1, up), 0.0)
+        return jnp.where(y == 7, level_of(parts, 7, up), beside)
+
+    inner = jnp.concatenate([level_of(parts, 0, True), level_of(parts, 0, False)], axis=0)
+    inner = give_lanes(inner, (0, 127)).reshape(4, 8, 8, 128)
+    edges = jnp.concatenate([edge(True), edge(False)], axis=0)
     ghosts[:, :, 0:8] = inner
     ghosts[:, :, 8:16] = give_lanes(edges, (0, 127)).reshape(4, 8, 8, 128)
 
-    even = (gx & 1) == 0
     column = lax.broadcasted_iota(jnp.int32, (8, 128), 1)
     outer = (column == 0) | (column == 127)
 
@@ -241,8 +256,8 @@
         return tiles + [jnp.concatenate(across, axis=0), ends[0] + ends[1] + ends[2] + ends[3]]
 
     for i, (high, low) in enumerate(zip(slab(6, 7), slab(0, 0))):
-        first[i] = jnp.where(even, high, low)
-        second[i] = jnp.where(even, low, high)
+        first[i] = high
+        second[i] = low
 
 
 def final_kernel(
@@ -259,7 +274,7 @@
     body_force[...] = body
 
     gz = lax.axis_index("gz")
-    fill(grid, state, ylo, yhi, ghosts, first, second)
+    fill(grid, parts, state, ylo, yhi, ghosts, first, second)
     level = lax.broadcasted_iota(jnp.int32, (1, 1, 256), 2)
     outside = ((level >= 128) & (level < 192) & (gz == 3)) | ((level >= 192) & (gz == 0))
 
@@ -313,13 +328,6 @@
     return lax.ppermute(up, axis, forward), lax.ppermute(down, axis, backward)
 
 
-def swap(slab, axis, odd):
-    count = lax.axis_size(axis)
-    return lax.ppermute(
-        slab, axis, [(i, (i + 1 if i % 2 == odd else i - 1) % count) for i in range(count)]
-    )
-
-
 def exchange(blocks, axes):
     return lax.all_to_all(blocks, axes, split_axis=0, concat_axis=0, tiled=True)
 
@@ -343,9 +351,9 @@
         pltpu.SemaphoreType.DMA((7,)),
     )
     side = f32(4, 8, 2, 128)
-    partial, own, yup, ydown = call(
+    partial, own, yup, ydown, far = call(
         sample_kernel,
-        (f32(32, 16, 128), f32(8, 128), side, side),
+        (f32(32, 8, 128), f32(8, 128), side, side, f32(2, 8, 128)),
         held,
         7,
         pltpu.HBM,
@@ -361,10 +369,10 @@
     first, second, ghosts = call(faces_kernel, (slab, slab, f32(4, 8, 16, 128)), count=4)(
         parts, state, ylo, yhi
     )
-    first, second = swap(first, "gx", 0), swap(second, "gx", 1)
+    first, second = shift(first, second, "gx")
     totals, first, second = lax.optimization_barrier((totals, first, second))
 
-    forces = call(force_kernel, f32(32, 8, 128), count=1)(totals)
+    forces = call(force_kernel, f32(32, 8, 128), count=2)(totals, far)
     forces = exchange(forces, PLANE)
     grid = pltpu.VMEM((4, 12, 16, 256), jnp.float32)
     return call(final_kernel, (f32(4, 8, 8, 128), f32(3, 8, 8, 128)), (grid,), 11)(

time: 63.3 us -> 62.6 us (0.989)
  starting transfers between devices: 32.8 us -> 31.7 us
    ppermute x2 -> x0, starting transfers between devices: 7.57 us -> none  [swap(): lax.ppermute(slab, axis, [(i, (i + 1 if i % 2 == odd else i - 1) % count)...]
    ppermute x2 -> x4, starting transfers between devices: 1.67 us -> 8.16 us  [shift(): return (lax.ppermute(up, axis, forward), lax.ppermute(down, axis, backward))]
    ppermute x2 -> x0, waiting for transfers between devices: 1.94 us -> none  [swap(): lax.ppermute(slab, axis, [(i, (i + 1 if i % 2 == odd else i - 1) % count)...]
    ppermute x2 -> x4, waiting for transfers between devices: 4.22 us -> 5.59 us  [shift(): return (lax.ppermute(up, axis, forward), lax.ppermute(down, axis, backward))]
  transfers between devices with their start and end apart: 6 -> 6, of which waited for: 5 -> 6; matrix products, arithmetic and copies ran while one was open for 0% -> 0% of each run, Pallas kernels for 0% -> 0%
where the time goes in v8:
time: 62.6 us; the launch traced here: 62.1 us
  starting transfers between devices  31.7 us (51%)
  blocking collectives  13.4 us (21%)
  waiting for transfers between devices  10.9 us (17%)
  Pallas kernels  5.27 us (8%)
  between operations  0.78 us (1%)
    all_to_all x2, starting transfers between devices, exchange(): return lax.all_to_all(blocks, axes, split_axis=0, concat_axis=0, tiled=True)  23.6 us
    all_to_all x1, blocking collectives, exchange(): return lax.all_to_all(blocks, axes, split_axis=0, concat_axis=0, tiled=True)  13.4 us
    ppermute x4, starting transfers between devices, shift(): return (lax.ppermute(up, axis, forward), lax.ppermute(down, axis, backward))  8.16 us
    ppermute x4, waiting for transfers between devices, shift(): return (lax.ppermute(up, axis, forward), lax.ppermute(down, axis, backward))  5.59 us
    all_to_all x2, waiting for transfers between devices, exchange(): return lax.all_to_all(blocks, axes, split_axis=0, concat_axis=0, tiled=True)  5.3 us
    pallas_call x1, Pallas kernels, body(): call(sample_kernel, (f32(32, 8, 128), f32(8, 128), side, side, f32(2, 8,...  2.52 us
    pallas_call x1, Pallas kernels, body(): call(final_kernel, (f32(4, 8, 8, 128), f32(3, 8, 8, 128)), (grid,), 11)  1.73 us
  transfers between devices with their start and end apart: 6, of which 6 were waited for; matrix products, arithmetic and copies ran while one was open for 0% of the time, Pallas kernels for 0%

profile of v8, /device:TPU:1, one launch (start us, length us, event | category | flops | bytes accessed | tf_op | source)
XLA Modules:
  0.0 62.1 jit_solution(610312531259622463)
XLA Ops:
  0.6 2.5 %shard_map.86 = (f32[32,8,128]{2,1,0:T(8,128)}, f32[8,128]{1,0:T(8,128)}, f32[4,8,2,128]{3,2,1,0:T(2,128)}, f32[4,8,2,128]{3,2,1,0:T(2,128)}, f32[2,8,128]{2,1,0:T(8,128)}) custom-call(f32[4,8,8,128]{3,2,1,0:T(8,128)} %state.3, s32[1,1024]{1,0:T(1,128)} %bitcast.5, s32[1,1024]{1,0:T(1,128)} %bitcast.7, s32[1,1024]{1,0:T(1,128)} %bitcast.9, ...), custom_call_target="tpu_custom_call" | custom-call | flops 2000000 | bytes 1000000 | tf_op jit(solution)/shard_map/pallas_call | solution.py:354
  3.2 0.0 copy-start.8
  3.2 0.0 copy-start.7
  3.2 10.6 %all-to-all-start = ((f32[32,8,128]{2,1,0:T(8,128)}), f32[32,8,128]{2,1,0:T(8,128)S(1)}, u32[]{:S(2)}, u32[]{:S(2)}) async-start(f32[32,8,128]{2,1,0:T(8,128)} %get-tuple-element.16), calls=%async_computation | async-start | bytes 262144 | tf_op jit(solution)/shard_map/all_to_all | solution.py:332
  13.7 0.0 copy-start.6
  13.8 0.0 copy-done.8
  13.8 1.7 %collective-permute-start = (f32[4,8,2,128]{3,2,1,0:T(2,128)S(1)}, f32[4,8,2,128]{3,2,1,0:T(2,128)S(1)}, u32[]{:S(2)}, u32[]{:S(2)}) collective-permute-start(f32[4,8,2,128]{3,2,1,0:T(2,128)S(1)} %copy-done.8), channel_id=1, source_target_pairs={{0,4},{4,8},{8,12},{12,16},{16,20},{20,24},{24,28},{28,0},{1,5},{5... | collective-permute-start | bytes 98312 | tf_op jit(solution)/shard_map/ppermute | solution.py:328
  15.4 0.0 copy-done.7
  15.4 0.0 collective-permute-start.1
  15.4 1.0 %collective-permute-done.ylo = f32[4,8,2,128]{3,2,1,0:T(2,128)S(1)} collective-permute-done((f32[4,8,2,128]{3,2,1,0:T(2,128)S(1)}, f32[4,8,2,128]{3,2,1,0:T(2,128)S(1)}, u32[]{:S(2)}, u32[]{:S(2)}) %collective-permute-start) | collective-permute-done | bytes 32800 | tf_op jit(solution)/shard_map/ppermute | solution.py:328
  16.5 2.6 %collective-permute-done.1.yhi = f32[4,8,2,128]{3,2,1,0:T(2,128)S(1)} collective-permute-done((f32[4,8,2,128]{3,2,1,0:T(2,128)S(1)}, f32[4,8,2,128]{3,2,1,0:T(2,128)S(1)}, u32[]{:S(2)}, u32[]{:S(2)}) %collective-permute-start.1) | collective-permute-done | bytes 32800 | tf_op jit(solution)/shard_map/ppermute | solution.py:328
  19.1 2.5 %all-to-all-done.parts = f32[32,8,128]{2,1,0:T(8,128)S(1)} async-done(((f32[32,8,128]{2,1,0:T(8,128)}), f32[32,8,128]{2,1,0:T(8,128)S(1)}, u32[]{:S(2)}, u32[]{:S(2)}) %all-to-all-start) | async-done | bytes 131104 | tf_op jit(solution)/shard_map/all_to_all | solution.py:332
  21.6 0.0 copy-done.6
  21.6 0.7 %shard_map.87 = f32[16,8,128]{2,1,0:T(8,128)} custom-call(f32[32,8,128]{2,1,0:T(8,128)S(1)} %all-to-all-done.parts, f32[8,128]{1,0:T(8,128)S(1)} %copy-done.6), custom_call_target="tpu_custom_call" | custom-call | flops 2000000 | bytes 1000000 | tf_op jit(solution)/shard_map/pallas_call | solution.py:366
  22.3 13.0 %all-to-all-start.1 = ((f32[16,8,128]{2,1,0:T(8,128)}), f32[16,8,128]{2,1,0:T(8,128)S(1)}, u32[]{:S(2)}, u32[]{:S(2)}) async-start(f32[16,8,128]{2,1,0:T(8,128)} %shard_map.87), calls=%async_computation.1 | async-start | bytes 131072 | tf_op jit(solution)/shard_map/all_to_all | solution.py:332
  35.3 0.0 copy-done
  35.3 0.0 copy-start.5
  35.3 0.3 shard_map.88
  35.6 3.3 %collective-permute-start.2 = (f32[10,8,128]{2,1,0:T(8,128)S(1)}, f32[10,8,128]{2,1,0:T(8,128)S(1)}, u32[]{:S(2)}, u32[]{:S(2)}) collective-permute-start(f32[10,8,128]{2,1,0:T(8,128)S(1)} %get-tuple-element.23), channel_id=1, source_target_pairs={{0,32},{32,64},{64,96},{96,128},{128,160},{160,192},{192,224},{224... | collective-permute-start | bytes 122888 | tf_op jit(solution)/shard_map/ppermute | solution.py:328
  38.9 3.2 %collective-permute-start.3 = (f32[10,8,128]{2,1,0:T(8,128)S(1)}, f32[10,8,128]{2,1,0:T(8,128)S(1)}, u32[]{:S(2)}, u32[]{:S(2)}) collective-permute-start(f32[10,8,128]{2,1,0:T(8,128)S(1)} %get-tuple-element.24), channel_id=1, source_target_pairs={{32,0},{64,32},{96,64},{128,96},{160,128},{192,160},{224,192},{256... | collective-permute-start | bytes 122888 | tf_op jit(solution)/shard_map/ppermute | solution.py:328
  42.1 0.3 collective-permute-done.2.first
  42.4 1.7 %collective-permute-done.3.second = f32[10,8,128]{2,1,0:T(8,128)S(1)} collective-permute-done((f32[10,8,128]{2,1,0:T(8,128)S(1)}, f32[10,8,128]{2,1,0:T(8,128)S(1)}, u32[]{:S(2)}, u32[]{:S(2)}) %collective-permute-start.3) | collective-permute-done | bytes 40992 | tf_op jit(solution)/shard_map/ppermute | solution.py:328
  44.1 2.8 %all-to-all-done.1.parts = f32[16,8,128]{2,1,0:T(8,128)S(1)} async-done(((f32[16,8,128]{2,1,0:T(8,128)}), f32[16,8,128]{2,1,0:T(8,128)S(1)}, u32[]{:S(2)}, u32[]{:S(2)}) %all-to-all-start.1) | async-done | bytes 65568 | tf_op jit(solution)/shard_map/all_to_all | solution.py:332
  46.8 0.0 copy-done.5
  46.9 0.0 copy-start.1
  46.9 0.0 copy-start.2
  46.9 0.0 copy-start.3
  46.9 0.0 copy-start.4
  46.9 13.4 %all_to_all.15.parts = f32[32,8,128]{2,1,0:T(8,128)S(1)} all-to-all(f32[32,8,128]{2,1,0:T(8,128)S(1)} %shard_map.89), channel_id=1, replica_groups=mesh['gx'=16,'gy'=8,'gz'=4] {'gy','gz'}, dimensions={0} | all-to-all | bytes 262144 | tf_op jit(solution)/shard_map/all_to_all | solution.py:332
  60.4 0.0 copy-done.1
  60.4 0.0 copy-done.2
  60.4 1.7 %shard_map.90 = (f32[4,8,8,128]{3,2,1,0:T(8,128)}, f32[3,8,8,128]{3,2,1,0:T(8,128)}) custom-call(f32[32,8,128]{2,1,0:T(8,128)S(1)} %all_to_all.15.parts, s32[1,1024]{1,0:T(1,128)S(1)} %bitcast.6, s32[1,1024]{1,0:T(1,128)S(1)} %bitcast.8, s32[1,1024]{1,0:T(1,128)S(1)} %bitcast.10, f32[1,1024]{1,0:T(1,128)S(1)} %bitcast.12, f32[4,8,8,128]{3,2,1,0:T(8,128)S(1)} %copy-done, ...), custom_call_target="tpu_custom_call" | custom-call | flops 2000000 | bytes 1000000 | tf_op jit(solution)/shard_map/pallas_call | solution.py:378
  (4 shorter events, 0.0 us)
Async XLA Ops:
  3.2 10.6 %copy-start.8 = (f32[4,8,2,128]{3,2,1,0:T(2,128)S(1)}, f32[4,8,2,128]{3,2,1,0:T(2,128)}, u32[]{:S(2)}) copy-start(f32[4,8,2,128]{3,2,1,0:T(2,128)} %get-tuple-element.17) | copy-start | bytes 98308
  3.2 12.3 %copy-start.7 = (f32[4,8,2,128]{3,2,1,0:T(2,128)S(1)}, f32[4,8,2,128]{3,2,1,0:T(2,128)}, u32[]{:S(2)}) copy-start(f32[4,8,2,128]{3,2,1,0:T(2,128)} %get-tuple-element.18) | copy-start | bytes 98308
  3.2 18.4 %all-to-all-start = ((f32[32,8,128]{2,1,0:T(8,128)}), f32[32,8,128]{2,1,0:T(8,128)S(1)}, u32[]{:S(2)}, u32[]{:S(2)}) async-start(f32[32,8,128]{2,1,0:T(8,128)} %get-tuple-element.16), calls=%async_computation | async-start | bytes 262144 | tf_op jit(solution)/shard_map/all_to_all | solution.py:332
  13.7 7.8 %copy-start.6 = (f32[8,128]{1,0:T(8,128)S(1)}, f32[8,128]{1,0:T(8,128)}, u32[]{:S(2)}) copy-start(f32[8,128]{1,0:T(8,128)} %get-tuple-element.20.own) | copy-start | bytes 12292
  13.8 2.7 %collective-permute-start = (f32[4,8,2,128]{3,2,1,0:T(2,128)S(1)}, f32[4,8,2,128]{3,2,1,0:T(2,128)S(1)}, u32[]{:S(2)}, u32[]{:S(2)}) collective-permute-start(f32[4,8,2,128]{3,2,1,0:T(2,128)S(1)} %copy-done.8), channel_id=1, source_target_pairs={{0,4},{4,8},{8,12},{12,16},{16,20},{20,24},{24,28},{28,0},{1,5},{5... | collective-permute-start | bytes 98312 | tf_op jit(solution)/shard_map/ppermute | solution.py:328
  15.4 3.6 %collective-permute-start.1 = (f32[4,8,2,128]{3,2,1,0:T(2,128)S(1)}, f32[4,8,2,128]{3,2,1,0:T(2,128)S(1)}, u32[]{:S(2)}, u32[]{:S(2)}) collective-permute-start(f32[4,8,2,128]{3,2,1,0:T(2,128)S(1)} %copy-done.7), channel_id=1, source_target_pairs={{4,0},{8,4},{12,8},{16,12},{20,16},{24,20},{28,24},{0,28},{5,1},{9... | collective-permute-start | bytes 98312 | tf_op jit(solution)/shard_map/ppermute | solution.py:328
  21.6 13.7 %copy-start = (f32[4,8,8,128]{3,2,1,0:T(8,128)S(1)}, f32[4,8,8,128]{3,2,1,0:T(8,128)}, u32[]{:S(2)}) copy-start(f32[4,8,8,128]{3,2,1,0:T(8,128)} %state.3) | copy-start | bytes 393220
  22.3 24.6 %all-to-all-start.1 = ((f32[16,8,128]{2,1,0:T(8,128)}), f32[16,8,128]{2,1,0:T(8,128)S(1)}, u32[]{:S(2)}, u32[]{:S(2)}) async-start(f32[16,8,128]{2,1,0:T(8,128)} %shard_map.87), calls=%async_computation.1 | async-start | bytes 131072 | tf_op jit(solution)/shard_map/all_to_all | solution.py:332
  35.3 11.6 %copy-start.5 = (f32[2,8,128]{2,1,0:T(8,128)S(1)}, f32[2,8,128]{2,1,0:T(8,128)}, u32[]{:S(2)}) copy-start(f32[2,8,128]{2,1,0:T(8,128)} %get-tuple-element.26.far) | copy-start | bytes 24580
  35.6 6.8 %collective-permute-start.2 = (f32[10,8,128]{2,1,0:T(8,128)S(1)}, f32[10,8,128]{2,1,0:T(8,128)S(1)}, u32[]{:S(2)}, u32[]{:S(2)}) collective-permute-start(f32[10,8,128]{2,1,0:T(8,128)S(1)} %get-tuple-element.23), channel_id=1, source_target_pairs={{0,32},{32,64},{64,96},{96,128},{128,160},{160,192},{192,224},{224... | collective-permute-start | bytes 122888 | tf_op jit(solution)/shard_map/ppermute | solution.py:328
  38.9 5.2 %collective-permute-start.3 = (f32[10,8,128]{2,1,0:T(8,128)S(1)}, f32[10,8,128]{2,1,0:T(8,128)S(1)}, u32[]{:S(2)}, u32[]{:S(2)}) collective-permute-start(f32[10,8,128]{2,1,0:T(8,128)S(1)} %get-tuple-element.24), channel_id=1, source_target_pairs={{32,0},{64,32},{96,64},{128,96},{160,128},{192,160},{224,192},{256... | collective-permute-start | bytes 122888 | tf_op jit(solution)/shard_map/ppermute | solution.py:328
  46.9 13.5 %copy-start.1 = (s32[1024]{0:T(1024)S(1)}, s32[1024]{0:T(1024)}, u32[]{:S(2)}) copy-start(s32[1024]{0:T(1024)} %param.8) | copy-start | bytes 12292
  46.9 13.5 %copy-start.2 = (s32[1024,1]{0,1:T(1,128)S(1)}, s32[1024,1]{0,1:T(1,128)}, u32[]{:S(2)}) copy-start(s32[1024,1]{0,1:T(1,128)} %param.9) | copy-start | bytes 12292
  46.9 13.5 %copy-start.3 = (s32[1024]{0:T(1024)S(1)}, s32[1024]{0:T(1024)}, u32[]{:S(2)}) copy-start(s32[1024]{0:T(1024)} %param.11) | copy-start | bytes 12292
  46.9 13.5 %copy-start.4 = (f32[1024]{0:T(1024)S(1)}, f32[1024]{0:T(1024)}, u32[]{:S(2)}) copy-start(f32[1024]{0:T(1024)} %param.10) | copy-start | bytes 12292

commit v9 on v8

--- a/solution.py
+++ b/solution.py
@@ -328,8 +328,11 @@
     return lax.ppermute(up, axis, forward), lax.ppermute(down, axis, backward)
 
 
-def exchange(blocks, axes):
-    return lax.all_to_all(blocks, axes, split_axis=0, concat_axis=0, tiled=True)
+def exchange(blocks, axes, order=None):
+    groups = None if order is None else [order]
+    return lax.all_to_all(
+        blocks, axes, split_axis=0, concat_axis=0, tiled=True, axis_index_groups=groups
+    )
 
 
 def body(state, sample_cell, sample_dest, sample_weight, sample_elem, element_motion, element_coef):
@@ -364,7 +367,7 @@
     parts, ylo, yhi = lax.optimization_barrier((parts, ylo, yhi))
 
     totals = call(total_kernel, f32(16, 8, 128), count=2)(parts, own)
-    totals = exchange(totals, "gx")
+    totals = exchange(totals, "gx", [(i + 12) % 16 for i in range(16)])
     slab = f32(10, 8, 128)
     first, second, ghosts = call(faces_kernel, (slab, slab, f32(4, 8, 16, 128)), count=4)(
         parts, state, ylo, yhi

time: 62.6 us -> 59.5 us (0.950)
  waiting for transfers between devices: 10.9 us -> 8.01 us
    all_to_all x2, waiting for transfers between devices: 5.3 us -> 2.52 us  [exchange(): lax.all_to_all(blocks, axes, split_axis=0, concat_axis=0, tiled=True, axi...]
    all_to_all x1, blocking collectives: 13.4 us -> 12.8 us  [exchange(): lax.all_to_all(blocks, axes, split_axis=0, concat_axis=0, tiled=True, axi...]
  transfers between devices with their start and end apart: 6 -> 6, of which waited for: 6 -> 4; matrix products, arithmetic and copies ran while one was open for 0% -> 0% of each run, Pallas kernels for 0% -> 1%
where the time goes in v9:
time: 59.5 us; the launch traced here: 58.8 us
  starting transfers between devices  31.9 us (54%)
  blocking collectives  12.8 us (22%)
  waiting for transfers between devices  8.01 us (13%)
  Pallas kernels  5.27 us (9%)
  between operations  0.77 us (1%)
    all_to_all x2, starting transfers between devices, exchange(): lax.all_to_all(blocks, axes, split_axis=0, concat_axis=0, tiled=True, axi...  23.7 us
    all_to_all x1, blocking collectives, exchange(): lax.all_to_all(blocks, axes, split_axis=0, concat_axis=0, tiled=True, axi...  12.8 us
    ppermute x4, starting transfers between devices, shift(): return (lax.ppermute(up, axis, forward), lax.ppermute(down, axis, backward))  8.16 us
    ppermute x4, waiting for transfers between devices, shift(): return (lax.ppermute(up, axis, forward), lax.ppermute(down, axis, backward))  5.5 us
    pallas_call x1, Pallas kernels, body(): call(sample_kernel, (f32(32, 8, 128), f32(8, 128), side, side, f32(2, 8,...  2.52 us
    all_to_all x2, waiting for transfers between devices, exchange(): lax.all_to_all(blocks, axes, split_axis=0, concat_axis=0, tiled=True, axi...  2.52 us
    pallas_call x1, Pallas kernels, body(): call(final_kernel, (f32(4, 8, 8, 128), f32(3, 8, 8, 128)), (grid,), 11)  1.73 us
  transfers between devices with their start and end apart: 6, of which 4 were waited for; matrix products, arithmetic and copies ran while one was open for 0% of the time, Pallas kernels for 1%

profile of v9, /device:TPU:1, one launch (start us, length us, event | category | flops | bytes accessed | tf_op | source)
XLA Modules:
  0.0 58.8 jit_solution(13580904126626023010)
XLA Ops:
  0.6 2.5 %shard_map.86 = (f32[32,8,128]{2,1,0:T(8,128)}, f32[8,128]{1,0:T(8,128)}, f32[4,8,2,128]{3,2,1,0:T(2,128)}, f32[4,8,2,128]{3,2,1,0:T(2,128)}, f32[2,8,128]{2,1,0:T(8,128)}) custom-call(f32[4,8,8,128]{3,2,1,0:T(8,128)} %state.3, s32[1,1024]{1,0:T(1,128)} %bitcast.5, s32[1,1024]{1,0:T(1,128)} %bitcast.7, s32[1,1024]{1,0:T(1,128)} %bitcast.9, ...), custom_call_target="tpu_custom_call" | custom-call | flops 2000000 | bytes 1000000 | tf_op jit(solution)/shard_map/pallas_call | solution.py:357
  3.2 0.0 copy-start.8
  3.2 0.0 copy-start.7
  3.2 10.6 %all-to-all-start = ((f32[32,8,128]{2,1,0:T(8,128)}), f32[32,8,128]{2,1,0:T(8,128)S(1)}, u32[]{:S(2)}, u32[]{:S(2)}) async-start(f32[32,8,128]{2,1,0:T(8,128)} %get-tuple-element.16), calls=%async_computation | async-start | bytes 262144 | tf_op jit(solution)/shard_map/all_to_all | solution.py:333
  13.7 0.0 copy-start.6
  13.8 0.0 copy-done.8
  13.8 1.7 %collective-permute-start = (f32[4,8,2,128]{3,2,1,0:T(2,128)S(1)}, f32[4,8,2,128]{3,2,1,0:T(2,128)S(1)}, u32[]{:S(2)}, u32[]{:S(2)}) collective-permute-start(f32[4,8,2,128]{3,2,1,0:T(2,128)S(1)} %copy-done.8), channel_id=1, source_target_pairs={{0,4},{4,8},{8,12},{12,16},{16,20},{20,24},{24,28},{28,0},{1,5},{5... | collective-permute-start | bytes 98312 | tf_op jit(solution)/shard_map/ppermute | solution.py:328
  15.4 0.0 copy-done.7
  15.4 0.0 collective-permute-start.1
  15.4 1.0 %collective-permute-done.ylo = f32[4,8,2,128]{3,2,1,0:T(2,128)S(1)} collective-permute-done((f32[4,8,2,128]{3,2,1,0:T(2,128)S(1)}, f32[4,8,2,128]{3,2,1,0:T(2,128)S(1)}, u32[]{:S(2)}, u32[]{:S(2)}) %collective-permute-start) | collective-permute-done | bytes 32800 | tf_op jit(solution)/shard_map/ppermute | solution.py:328
  16.5 2.6 %collective-permute-done.1.yhi = f32[4,8,2,128]{3,2,1,0:T(2,128)S(1)} collective-permute-done((f32[4,8,2,128]{3,2,1,0:T(2,128)S(1)}, f32[4,8,2,128]{3,2,1,0:T(2,128)S(1)}, u32[]{:S(2)}, u32[]{:S(2)}) %collective-permute-start.1) | collective-permute-done | bytes 32800 | tf_op jit(solution)/shard_map/ppermute | solution.py:328
  19.1 2.5 %all-to-all-done.parts = f32[32,8,128]{2,1,0:T(8,128)S(1)} async-done(((f32[32,8,128]{2,1,0:T(8,128)}), f32[32,8,128]{2,1,0:T(8,128)S(1)}, u32[]{:S(2)}, u32[]{:S(2)}) %all-to-all-start) | async-done | bytes 131104 | tf_op jit(solution)/shard_map/all_to_all | solution.py:333
  21.6 0.0 copy-done.6
  21.6 0.7 %shard_map.87 = f32[16,8,128]{2,1,0:T(8,128)} custom-call(f32[32,8,128]{2,1,0:T(8,128)S(1)} %all-to-all-done.parts, f32[8,128]{1,0:T(8,128)S(1)} %copy-done.6), custom_call_target="tpu_custom_call" | custom-call | flops 2000000 | bytes 1000000 | tf_op jit(solution)/shard_map/pallas_call | solution.py:369
  22.3 13.2 %all-to-all-start.1 = ((f32[16,8,128]{2,1,0:T(8,128)}), f32[16,8,128]{2,1,0:T(8,128)S(1)}, u32[]{:S(2)}, u32[]{:S(2)}) async-start(f32[16,8,128]{2,1,0:T(8,128)} %shard_map.87), calls=%async_computation.1 | async-start | bytes 131072 | tf_op jit(solution)/shard_map/all_to_all | solution.py:333
  35.5 0.0 copy-done
  35.5 0.0 copy-start.5
  35.5 0.3 shard_map.88
  35.8 3.1 %collective-permute-start.2 = (f32[10,8,128]{2,1,0:T(8,128)S(1)}, f32[10,8,128]{2,1,0:T(8,128)S(1)}, u32[]{:S(2)}, u32[]{:S(2)}) collective-permute-start(f32[10,8,128]{2,1,0:T(8,128)S(1)} %get-tuple-element.23), channel_id=1, source_target_pairs={{0,32},{32,64},{64,96},{96,128},{128,160},{160,192},{192,224},{224... | collective-permute-start | bytes 122888 | tf_op jit(solution)/shard_map/ppermute | solution.py:328
  38.9 3.4 %collective-permute-start.3 = (f32[10,8,128]{2,1,0:T(8,128)S(1)}, f32[10,8,128]{2,1,0:T(8,128)S(1)}, u32[]{:S(2)}, u32[]{:S(2)}) collective-permute-start(f32[10,8,128]{2,1,0:T(8,128)S(1)} %get-tuple-element.24), channel_id=1, source_target_pairs={{32,0},{64,32},{96,64},{128,96},{160,128},{192,160},{224,192},{256... | collective-permute-start | bytes 122888 | tf_op jit(solution)/shard_map/ppermute | solution.py:328
  42.3 0.0 collective-permute-done.2.first
  42.3 1.9 %collective-permute-done.3.second = f32[10,8,128]{2,1,0:T(8,128)S(1)} collective-permute-done((f32[10,8,128]{2,1,0:T(8,128)S(1)}, f32[10,8,128]{2,1,0:T(8,128)S(1)}, u32[]{:S(2)}, u32[]{:S(2)}) %collective-permute-start.3) | collective-permute-done | bytes 40992 | tf_op jit(solution)/shard_map/ppermute | solution.py:328
  44.2 0.0 all-to-all-done.1.parts
  44.2 0.0 copy-done.5
  44.2 0.0 copy-start.1
  44.2 0.0 copy-start.2
  44.2 0.0 copy-start.3
  44.2 0.0 copy-start.4
  44.3 12.8 %all_to_all.15.parts = f32[32,8,128]{2,1,0:T(8,128)S(1)} all-to-all(f32[32,8,128]{2,1,0:T(8,128)S(1)} %shard_map.89), channel_id=1, replica_groups=mesh['gx'=16,'gy'=8,'gz'=4] {'gy','gz'}, dimensions={0} | all-to-all | bytes 262144 | tf_op jit(solution)/shard_map/all_to_all | solution.py:333
  57.1 0.0 copy-done.1
  57.1 0.0 copy-done.4
  57.1 1.7 %shard_map.90 = (f32[4,8,8,128]{3,2,1,0:T(8,128)}, f32[3,8,8,128]{3,2,1,0:T(8,128)}) custom-call(f32[32,8,128]{2,1,0:T(8,128)S(1)} %all_to_all.15.parts, s32[1,1024]{1,0:T(1,128)S(1)} %bitcast.6, s32[1,1024]{1,0:T(1,128)S(1)} %bitcast.8, s32[1,1024]{1,0:T(1,128)S(1)} %bitcast.10, f32[1,1024]{1,0:T(1,128)S(1)} %bitcast.12, f32[4,8,8,128]{3,2,1,0:T(8,128)S(1)} %copy-done, ...), custom_call_target="tpu_custom_call" | custom-call | flops 2000000 | bytes 1000000 | tf_op jit(solution)/shard_map/pallas_call | solution.py:381
  (4 shorter events, 0.0 us)
Async XLA Ops:
  3.2 10.6 %copy-start.8 = (f32[4,8,2,128]{3,2,1,0:T(2,128)S(1)}, f32[4,8,2,128]{3,2,1,0:T(2,128)}, u32[]{:S(2)}) copy-start(f32[4,8,2,128]{3,2,1,0:T(2,128)} %get-tuple-element.17) | copy-start | bytes 98308
  3.2 12.3 %copy-start.7 = (f32[4,8,2,128]{3,2,1,0:T(2,128)S(1)}, f32[4,8,2,128]{3,2,1,0:T(2,128)}, u32[]{:S(2)}) copy-start(f32[4,8,2,128]{3,2,1,0:T(2,128)} %get-tuple-element.18) | copy-start | bytes 98308
  3.2 18.4 %all-to-all-start = ((f32[32,8,128]{2,1,0:T(8,128)}), f32[32,8,128]{2,1,0:T(8,128)S(1)}, u32[]{:S(2)}, u32[]{:S(2)}) async-start(f32[32,8,128]{2,1,0:T(8,128)} %get-tuple-element.16), calls=%async_computation | async-start | bytes 262144 | tf_op jit(solution)/shard_map/all_to_all | solution.py:333
  13.7 7.8 %copy-start.6 = (f32[8,128]{1,0:T(8,128)S(1)}, f32[8,128]{1,0:T(8,128)}, u32[]{:S(2)}) copy-start(f32[8,128]{1,0:T(8,128)} %get-tuple-element.20.own) | copy-start | bytes 12292
  13.8 2.7 %collective-permute-start = (f32[4,8,2,128]{3,2,1,0:T(2,128)S(1)}, f32[4,8,2,128]{3,2,1,0:T(2,128)S(1)}, u32[]{:S(2)}, u32[]{:S(2)}) collective-permute-start(f32[4,8,2,128]{3,2,1,0:T(2,128)S(1)} %copy-done.8), channel_id=1, source_target_pairs={{0,4},{4,8},{8,12},{12,16},{16,20},{20,24},{24,28},{28,0},{1,5},{5... | collective-permute-start | bytes 98312 | tf_op jit(solution)/shard_map/ppermute | solution.py:328
  15.4 3.6 %collective-permute-start.1 = (f32[4,8,2,128]{3,2,1,0:T(2,128)S(1)}, f32[4,8,2,128]{3,2,1,0:T(2,128)S(1)}, u32[]{:S(2)}, u32[]{:S(2)}) collective-permute-start(f32[4,8,2,128]{3,2,1,0:T(2,128)S(1)} %copy-done.7), channel_id=1, source_target_pairs={{4,0},{8,4},{12,8},{16,12},{20,16},{24,20},{28,24},{0,28},{5,1},{9... | collective-permute-start | bytes 98312 | tf_op jit(solution)/shard_map/ppermute | solution.py:328
  21.6 13.9 %copy-start = (f32[4,8,8,128]{3,2,1,0:T(8,128)S(1)}, f32[4,8,8,128]{3,2,1,0:T(8,128)}, u32[]{:S(2)}) copy-start(f32[4,8,8,128]{3,2,1,0:T(8,128)} %state.3) | copy-start | bytes 393220
  22.3 21.9 %all-to-all-start.1 = ((f32[16,8,128]{2,1,0:T(8,128)}), f32[16,8,128]{2,1,0:T(8,128)S(1)}, u32[]{:S(2)}, u32[]{:S(2)}) async-start(f32[16,8,128]{2,1,0:T(8,128)} %shard_map.87), calls=%async_computation.1 | async-start | bytes 131072 | tf_op jit(solution)/shard_map/all_to_all | solution.py:333
  35.5 8.7 %copy-start.5 = (f32[2,8,128]{2,1,0:T(8,128)S(1)}, f32[2,8,128]{2,1,0:T(8,128)}, u32[]{:S(2)}) copy-start(f32[2,8,128]{2,1,0:T(8,128)} %get-tuple-element.26.far) | copy-start | bytes 24580
  35.8 6.5 %collective-permute-start.2 = (f32[10,8,128]{2,1,0:T(8,128)S(1)}, f32[10,8,128]{2,1,0:T(8,128)S(1)}, u32[]{:S(2)}, u32[]{:S(2)}) collective-permute-start(f32[10,8,128]{2,1,0:T(8,128)S(1)} %get-tuple-element.23), channel_id=1, source_target_pairs={{0,32},{32,64},{64,96},{96,128},{128,160},{160,192},{192,224},{224... | collective-permute-start | bytes 122888 | tf_op jit(solution)/shard_map/ppermute | solution.py:328
  38.9 5.3 %collective-permute-start.3 = (f32[10,8,128]{2,1,0:T(8,128)S(1)}, f32[10,8,128]{2,1,0:T(8,128)S(1)}, u32[]{:S(2)}, u32[]{:S(2)}) collective-permute-start(f32[10,8,128]{2,1,0:T(8,128)S(1)} %get-tuple-element.24), channel_id=1, source_target_pairs={{32,0},{64,32},{96,64},{128,96},{160,128},{192,160},{224,192},{256... | collective-permute-start | bytes 122888 | tf_op jit(solution)/shard_map/ppermute | solution.py:328
  44.2 12.9 %copy-start.1 = (s32[1024]{0:T(1024)S(1)}, s32[1024]{0:T(1024)}, u32[]{:S(2)}) copy-start(s32[1024]{0:T(1024)} %param.8) | copy-start | bytes 12292
  44.2 12.9 %copy-start.2 = (s32[1024,1]{0,1:T(1,128)S(1)}, s32[1024,1]{0,1:T(1,128)}, u32[]{:S(2)}) copy-start(s32[1024,1]{0,1:T(1,128)} %param.9) | copy-start | bytes 12292
  44.2 12.8 %copy-start.3 = (s32[1024]{0:T(1024)S(1)}, s32[1024]{0:T(1024)}, u32[]{:S(2)}) copy-start(s32[1024]{0:T(1024)} %param.11) | copy-start | bytes 12292
  44.2 12.8 %copy-start.4 = (f32[1024]{0:T(1024)S(1)}, f32[1024]{0:T(1024)}, u32[]{:S(2)}) copy-start(f32[1024]{0:T(1024)} %param.10) | copy-start | bytes 12292

commit v10 on v9

--- a/solution.py
+++ b/solution.py
@@ -12,6 +12,7 @@
 
 ROWS = 1024
 PLANE = ("gy", "gz")
+FIRST_TURN, ALONG_TURN, LAST_TURN = 22, 12, 18
 
 
 def call(kernel, outs, scratch=(), count=1, space=pltpu.VMEM, limit=24 * 1024 * 1024):
@@ -59,8 +60,8 @@
     return column, onehot(cell & 127, 128)
 
 
-def element_keys(dest, elem):
-    tile = (elem >> 4) * 4 + (dest & 3)
+def element_keys(dest, elem, turn):
+    tile = ((elem >> 4) * 4 + (dest & 3)) ^ turn
     along = dest >> 2
     number = tile * 2 + (along >> 3)
     shape = (32, 8, ROWS)
@@ -166,14 +167,14 @@
     pattern = jnp.where(
         row == 0, sampled[0], jnp.where(row == 1, sampled[1], jnp.where(row == 2, sampled[2], 0.0))
     )
-    match, hot_lane = element_keys(dest[...], elem[...])
+    match, hot_lane = element_keys(dest[...], elem[...], FIRST_TURN)
     spread = jnp.where(match, pattern[None], 0.0).reshape(256, ROWS)
     sums = put(spread, hot_lane).reshape(32, 8, 128)
     above = (lax.axis_index("gz") + 1) & 3
     for level in range(4):
         near = jnp.where(above == level, high, low)
         for across in range(level, 32, 4):
-            out[across] = sums[across] + near
+            out[across ^ FIRST_TURN] = sums[across ^ FIRST_TURN] + near
 
 
 def total_kernel(parts, own, out):
@@ -197,14 +198,15 @@
     for level in range(4):
         block = force + jnp.where(above == level, far[1], far[0])
         for across in range(level, 32, 4):
-            out[across] = block
+            out[across ^ LAST_TURN] = block
 
 
 def fill(grid, parts, state, ylo, yhi, ghosts, first, second):
     grid[:, 2:10, 0:8, 0:128] = state[...]
     grid[:, 2:10, 8:10, 0:128] = yhi[...]
     grid[:, 2:10, 14:16, 0:128] = ylo[...]
-    far = jnp.concatenate([level_of(parts, 0, True), level_of(parts, 0, False)], axis=0)
+    far = [level_of(parts, 0, up, LAST_TURN) for up in (True, False)]
+    far = jnp.concatenate(far, axis=0)
     far = give_lanes(far, (1, 126)).reshape(4, 8, 8, 128)
     grid[:, 2:10, 0:8, 128:256] = ghosts[:, :, 0:8] + far
     grid[:, 2:10, 8:16, 128:256] = ghosts[:, :, 8:16]
@@ -224,9 +226,9 @@
             grid[c, near, 0:8, 128:256] = jnp.where(outer, ends, 0.0)
 
 
-def level_of(parts, across, up):
+def level_of(parts, across, up, turn):
     gy, gz = lax.axis_index("gy"), lax.axis_index("gz")
-    block = parts[((gy + across) & 7) * 4 + ((gz + (1 if up else 3)) & 3)]
+    block = parts[(((gy + across) & 7) * 4 + ((gz + (1 if up else 3)) & 3)) ^ turn]
     found = jnp.concatenate([block[6:7], block[7:8]], axis=1)
     return jnp.where(gz == (3 if up else 0), 0.0, found)
 
@@ -236,10 +238,11 @@
 
     def edge(up):
         y = lane & 7
-        beside = jnp.where(y == 0, level_of(parts, 1, up), 0.0)
-        return jnp.where(y == 7, level_of(parts, 7, up), beside)
-
-    inner = jnp.concatenate([level_of(parts, 0, True), level_of(parts, 0, False)], axis=0)
+        beside = jnp.where(y == 0, level_of(parts, 1, up, FIRST_TURN), 0.0)
+        return jnp.where(y == 7, level_of(parts, 7, up, FIRST_TURN), beside)
+
+    inner = [level_of(parts, 0, up, FIRST_TURN) for up in (True, False)]
+    inner = jnp.concatenate(inner, axis=0)
     inner = give_lanes(inner, (0, 127)).reshape(4, 8, 8, 128)
     edges = jnp.concatenate([edge(True), edge(False)], axis=0)
     ghosts[:, :, 0:8] = inner
@@ -264,7 +267,7 @@
     parts, cell, dest, elem, weight, state, ylo, yhi, ghosts, first, second, *results
 ):
     new_state, body_force, grid = results
-    match, hot_lane = element_keys(dest[...], elem[...])
+    match, hot_lane = element_keys(dest[...], elem[...], LAST_TURN)
     found = pick(parts[...].reshape(256, 128), hot_lane).reshape(32, 8, ROWS)
     pairs = jnp.sum(jnp.where(match, found, 0.0), axis=0)
     column, hot_z = cell_keys(cell[...])
@@ -328,10 +331,9 @@
     return lax.ppermute(up, axis, forward), lax.ppermute(down, axis, backward)
 
 
-def exchange(blocks, axes, order=None):
-    groups = None if order is None else [order]
+def exchange(blocks, axes, order):
     return lax.all_to_all(
-        blocks, axes, split_axis=0, concat_axis=0, tiled=True, axis_index_groups=groups
+        blocks, axes, split_axis=0, concat_axis=0, tiled=True, axis_index_groups=[order]
     )
 
 
@@ -362,12 +364,12 @@
         pltpu.HBM,
         60 * 1024 * 1024,
     )(state, cell, dest, elem, weight, element_motion, coef)
-    parts = exchange(partial, PLANE)
+    parts = exchange(partial, PLANE, [i ^ FIRST_TURN for i in range(32)])
     ylo, yhi = shift(yup, ydown, "gy")
     parts, ylo, yhi = lax.optimization_barrier((parts, ylo, yhi))
 
     totals = call(total_kernel, f32(16, 8, 128), count=2)(parts, own)
-    totals = exchange(totals, "gx", [(i + 12) % 16 for i in range(16)])
+    totals = exchange(totals, "gx", [(i + ALONG_TURN) % 16 for i in range(16)])
     slab = f32(10, 8, 128)
     first, second, ghosts = call(faces_kernel, (slab, slab, f32(4, 8, 16, 128)), count=4)(
         parts, state, ylo, yhi
@@ -376,7 +378,7 @@
     totals, first, second = lax.optimization_barrier((totals, first, second))
 
     forces = call(force_kernel, f32(32, 8, 128), count=2)(totals, far)
-    forces = exchange(forces, PLANE)
+    forces = exchange(forces, PLANE, [i ^ LAST_TURN for i in range(32)])
     grid = pltpu.VMEM((4, 12, 16, 256), jnp.float32)
     return call(final_kernel, (f32(4, 8, 8, 128), f32(3, 8, 8, 128)), (grid,), 11)(
         forces, cell, dest, elem, weight, state, ylo, yhi, ghosts, first, second

time: 59.5 us -> 56.5 us (0.950)
  waiting for transfers between devices: 8.01 us -> 4.51 us
    all_to_all x2, waiting for transfers between devices: 2.52 us -> 0.01 us  [exchange(): lax.all_to_all(blocks, axes, split_axis=0, concat_axis=0, tiled=True, axi...]
    all_to_all x2, starting transfers between devices: 23.7 us -> 25.1 us  [exchange(): lax.all_to_all(blocks, axes, split_axis=0, concat_axis=0, tiled=True, axi...]
    ppermute x4, starting transfers between devices: 8.16 us -> 7.01 us  [shift(): return (lax.ppermute(up, axis, forward), lax.ppermute(down, axis, backward))]
    ppermute x4, waiting for transfers between devices: 5.5 us -> 4.5 us  [shift(): return (lax.ppermute(up, axis, forward), lax.ppermute(down, axis, backward))]
  transfers between devices with their start and end apart: 6 -> 6, of which waited for: 4 -> 3; matrix products, arithmetic and copies ran while one was open for 0% -> 0% of each run, Pallas kernels for 1% -> 1%
where the time goes in v10:
time: 56.5 us; the launch traced here: 55.8 us
  starting transfers between devices  32.1 us (57%)
  blocking collectives  13.1 us (23%)
  Pallas kernels  5.27 us (9%)
  waiting for transfers between devices  4.51 us (8%)
  between operations  0.77 us (1%)
    all_to_all x2, starting transfers between devices, exchange(): lax.all_to_all(blocks, axes, split_axis=0, concat_axis=0, tiled=True, axi...  25.1 us
    all_to_all x1, blocking collectives, exchange(): lax.all_to_all(blocks, axes, split_axis=0, concat_axis=0, tiled=True, axi...  13.1 us
    ppermute x4, starting transfers between devices, shift(): return (lax.ppermute(up, axis, forward), lax.ppermute(down, axis, backward))  7.01 us
    ppermute x4, waiting for transfers between devices, shift(): return (lax.ppermute(up, axis, forward), lax.ppermute(down, axis, backward))  4.5 us
    pallas_call x1, Pallas kernels, body(): call(sample_kernel, (f32(32, 8, 128), f32(8, 128), side, side, f32(2, 8,...  2.52 us
    pallas_call x1, Pallas kernels, body(): call(final_kernel, (f32(4, 8, 8, 128), f32(3, 8, 8, 128)), (grid,), 11)  1.73 us
  transfers between devices with their start and end apart: 6, of which 3 were waited for; matrix products, arithmetic and copies ran while one was open for 0% of the time, Pallas kernels for 1%

profile of v10, /device:TPU:1, one launch (start us, length us, event | category | flops | bytes accessed | tf_op | source)
XLA Modules:
  0.0 55.8 jit_solution(12070597106075305545)
XLA Ops:
  0.6 2.5 %shard_map.86 = (f32[32,8,128]{2,1,0:T(8,128)}, f32[8,128]{1,0:T(8,128)}, f32[4,8,2,128]{3,2,1,0:T(2,128)}, f32[4,8,2,128]{3,2,1,0:T(2,128)}, f32[2,8,128]{2,1,0:T(8,128)}) custom-call(f32[4,8,8,128]{3,2,1,0:T(8,128)} %state.3, s32[1,1024]{1,0:T(1,128)} %bitcast.5, s32[1,1024]{1,0:T(1,128)} %bitcast.7, s32[1,1024]{1,0:T(1,128)} %bitcast.9, ...), custom_call_target="tpu_custom_call" | custom-call | flops 2000000 | bytes 1000000 | tf_op jit(solution)/shard_map/pallas_call | solution.py:359
  3.2 0.0 copy-start.8
  3.2 0.0 copy-start.7
  3.2 13.7 %all-to-all-start = ((f32[32,8,128]{2,1,0:T(8,128)}), f32[32,8,128]{2,1,0:T(8,128)S(1)}, u32[]{:S(2)}, u32[]{:S(2)}) async-start(f32[32,8,128]{2,1,0:T(8,128)} %get-tuple-element.16), calls=%async_computation | async-start | bytes 262144 | tf_op jit(solution)/shard_map/all_to_all | solution.py:335
  16.9 0.0 copy-start.6
  16.9 0.0 copy-done.8
  16.9 0.1 collective-permute-start
  17.0 0.0 copy-done.7
  17.0 0.5 collective-permute-start.1
  17.5 1.6 %collective-permute-done.ylo = f32[4,8,2,128]{3,2,1,0:T(2,128)S(1)} collective-permute-done((f32[4,8,2,128]{3,2,1,0:T(2,128)S(1)}, f32[4,8,2,128]{3,2,1,0:T(2,128)S(1)}, u32[]{:S(2)}, u32[]{:S(2)}) %collective-permute-start) | collective-permute-done | bytes 32800 | tf_op jit(solution)/shard_map/ppermute | solution.py:331
  19.1 1.3 %collective-permute-done.1.yhi = f32[4,8,2,128]{3,2,1,0:T(2,128)S(1)} collective-permute-done((f32[4,8,2,128]{3,2,1,0:T(2,128)S(1)}, f32[4,8,2,128]{3,2,1,0:T(2,128)S(1)}, u32[]{:S(2)}, u32[]{:S(2)}) %collective-permute-start.1) | collective-permute-done | bytes 32800 | tf_op jit(solution)/shard_map/ppermute | solution.py:331
  20.3 0.0 all-to-all-done.parts
  20.3 0.0 copy-done.6
  20.3 0.7 %shard_map.87 = f32[16,8,128]{2,1,0:T(8,128)} custom-call(f32[32,8,128]{2,1,0:T(8,128)S(1)} %all-to-all-done.parts, f32[8,128]{1,0:T(8,128)S(1)} %copy-done.6), custom_call_target="tpu_custom_call" | custom-call | flops 2000000 | bytes 1000000 | tf_op jit(solution)/shard_map/pallas_call | solution.py:371
  21.0 11.4 %all-to-all-start.1 = ((f32[16,8,128]{2,1,0:T(8,128)}), f32[16,8,128]{2,1,0:T(8,128)S(1)}, u32[]{:S(2)}, u32[]{:S(2)}) async-start(f32[16,8,128]{2,1,0:T(8,128)} %shard_map.87), calls=%async_computation.1 | async-start | bytes 131072 | tf_op jit(solution)/shard_map/all_to_all | solution.py:335
  32.4 0.0 copy-done
  32.4 0.0 copy-start.5
  32.4 0.3 shard_map.88
  32.7 3.1 %collective-permute-start.2 = (f32[10,8,128]{2,1,0:T(8,128)S(1)}, f32[10,8,128]{2,1,0:T(8,128)S(1)}, u32[]{:S(2)}, u32[]{:S(2)}) collective-permute-start(f32[10,8,128]{2,1,0:T(8,128)S(1)} %get-tuple-element.23), channel_id=1, source_target_pairs={{0,32},{32,64},{64,96},{96,128},{128,160},{160,192},{192,224},{224... | collective-permute-start | bytes 122888 | tf_op jit(solution)/shard_map/ppermute | solution.py:331
  35.8 3.4 %collective-permute-start.3 = (f32[10,8,128]{2,1,0:T(8,128)S(1)}, f32[10,8,128]{2,1,0:T(8,128)S(1)}, u32[]{:S(2)}, u32[]{:S(2)}) collective-permute-start(f32[10,8,128]{2,1,0:T(8,128)S(1)} %get-tuple-element.24), channel_id=1, source_target_pairs={{32,0},{64,32},{96,64},{128,96},{160,128},{192,160},{224,192},{256... | collective-permute-start | bytes 122888 | tf_op jit(solution)/shard_map/ppermute | solution.py:331
  39.2 0.0 collective-permute-done.2.first
  39.2 1.6 %collective-permute-done.3.second = f32[10,8,128]{2,1,0:T(8,128)S(1)} collective-permute-done((f32[10,8,128]{2,1,0:T(8,128)S(1)}, f32[10,8,128]{2,1,0:T(8,128)S(1)}, u32[]{:S(2)}, u32[]{:S(2)}) %collective-permute-start.3) | collective-permute-done | bytes 40992 | tf_op jit(solution)/shard_map/ppermute | solution.py:331
  40.8 0.0 all-to-all-done.1.parts
  40.8 0.0 copy-done.5
  40.9 0.0 copy-start.1
  40.9 0.0 copy-start.2
  40.9 0.0 copy-start.3
  40.9 0.0 copy-start.4
  40.9 13.1 %all_to_all.15.parts = f32[32,8,128]{2,1,0:T(8,128)S(1)} all-to-all(f32[32,8,128]{2,1,0:T(8,128)S(1)} %shard_map.89), channel_id=1, replica_groups={{18,19,16,17,22,23,20,21,26,27,24,25,30,31,28,29,2,3,0,1,6,7,4,5,10,11,..., dimensions={0} | all-to-all | bytes 262144 | tf_op jit(solution)/shard_map/all_to_all | solution.py:335
  54.0 0.0 copy-done.1
  54.0 0.0 copy-done.2
  54.1 1.7 %shard_map.90 = (f32[4,8,8,128]{3,2,1,0:T(8,128)}, f32[3,8,8,128]{3,2,1,0:T(8,128)}) custom-call(f32[32,8,128]{2,1,0:T(8,128)S(1)} %all_to_all.15.parts, s32[1,1024]{1,0:T(1,128)S(1)} %bitcast.6, s32[1,1024]{1,0:T(1,128)S(1)} %bitcast.8, s32[1,1024]{1,0:T(1,128)S(1)} %bitcast.10, f32[1,1024]{1,0:T(1,128)S(1)} %bitcast.12, f32[4,8,8,128]{3,2,1,0:T(8,128)S(1)} %copy-done, ...), custom_call_target="tpu_custom_call" | custom-call | flops 2000000 | bytes 1000000 | tf_op jit(solution)/shard_map/pallas_call | solution.py:383
  (4 shorter events, 0.0 us)
Async XLA Ops:
  3.2 13.8 %copy-start.8 = (f32[4,8,2,128]{3,2,1,0:T(2,128)S(1)}, f32[4,8,2,128]{3,2,1,0:T(2,128)}, u32[]{:S(2)}) copy-start(f32[4,8,2,128]{3,2,1,0:T(2,128)} %get-tuple-element.17) | copy-start | bytes 98308
  3.2 13.8 %copy-start.7 = (f32[4,8,2,128]{3,2,1,0:T(2,128)S(1)}, f32[4,8,2,128]{3,2,1,0:T(2,128)}, u32[]{:S(2)}) copy-start(f32[4,8,2,128]{3,2,1,0:T(2,128)} %get-tuple-element.18) | copy-start | bytes 98308
  3.2 17.2 %all-to-all-start = ((f32[32,8,128]{2,1,0:T(8,128)}), f32[32,8,128]{2,1,0:T(8,128)S(1)}, u32[]{:S(2)}, u32[]{:S(2)}) async-start(f32[32,8,128]{2,1,0:T(8,128)} %get-tuple-element.16), calls=%async_computation | async-start | bytes 262144 | tf_op jit(solution)/shard_map/all_to_all | solution.py:335
  16.9 3.4 %copy-start.6 = (f32[8,128]{1,0:T(8,128)S(1)}, f32[8,128]{1,0:T(8,128)}, u32[]{:S(2)}) copy-start(f32[8,128]{1,0:T(8,128)} %get-tuple-element.20.own) | copy-start | bytes 12292
  16.9 2.1 %collective-permute-start = (f32[4,8,2,128]{3,2,1,0:T(2,128)S(1)}, f32[4,8,2,128]{3,2,1,0:T(2,128)S(1)}, u32[]{:S(2)}, u32[]{:S(2)}) collective-permute-start(f32[4,8,2,128]{3,2,1,0:T(2,128)S(1)} %copy-done.8), channel_id=1, source_target_pairs={{0,4},{4,8},{8,12},{12,16},{16,20},{20,24},{24,28},{28,0},{1,5},{5... | collective-permute-start | bytes 98312 | tf_op jit(solution)/shard_map/ppermute | solution.py:331
  17.0 3.3 %collective-permute-start.1 = (f32[4,8,2,128]{3,2,1,0:T(2,128)S(1)}, f32[4,8,2,128]{3,2,1,0:T(2,128)S(1)}, u32[]{:S(2)}, u32[]{:S(2)}) collective-permute-start(f32[4,8,2,128]{3,2,1,0:T(2,128)S(1)} %copy-done.7), channel_id=1, source_target_pairs={{4,0},{8,4},{12,8},{16,12},{20,16},{24,20},{28,24},{0,28},{5,1},{9... | collective-permute-start | bytes 98312 | tf_op jit(solution)/shard_map/ppermute | solution.py:331
  20.3 12.1 %copy-start = (f32[4,8,8,128]{3,2,1,0:T(8,128)S(1)}, f32[4,8,8,128]{3,2,1,0:T(8,128)}, u32[]{:S(2)}) copy-start(f32[4,8,8,128]{3,2,1,0:T(8,128)} %state.3) | copy-start | bytes 393220
  21.0 19.8 %all-to-all-start.1 = ((f32[16,8,128]{2,1,0:T(8,128)}), f32[16,8,128]{2,1,0:T(8,128)S(1)}, u32[]{:S(2)}, u32[]{:S(2)}) async-start(f32[16,8,128]{2,1,0:T(8,128)} %shard_map.87), calls=%async_computation.1 | async-start | bytes 131072 | tf_op jit(solution)/shard_map/all_to_all | solution.py:335
  32.4 8.5 %copy-start.5 = (f32[2,8,128]{2,1,0:T(8,128)S(1)}, f32[2,8,128]{2,1,0:T(8,128)}, u32[]{:S(2)}) copy-start(f32[2,8,128]{2,1,0:T(8,128)} %get-tuple-element.26.far) | copy-start | bytes 24580
  32.7 6.5 %collective-permute-start.2 = (f32[10,8,128]{2,1,0:T(8,128)S(1)}, f32[10,8,128]{2,1,0:T(8,128)S(1)}, u32[]{:S(2)}, u32[]{:S(2)}) collective-permute-start(f32[10,8,128]{2,1,0:T(8,128)S(1)} %get-tuple-element.23), channel_id=1, source_target_pairs={{0,32},{32,64},{64,96},{96,128},{128,160},{160,192},{192,224},{224... | collective-permute-start | bytes 122888 | tf_op jit(solution)/shard_map/ppermute | solution.py:331
  35.8 5.0 %collective-permute-start.3 = (f32[10,8,128]{2,1,0:T(8,128)S(1)}, f32[10,8,128]{2,1,0:T(8,128)S(1)}, u32[]{:S(2)}, u32[]{:S(2)}) collective-permute-start(f32[10,8,128]{2,1,0:T(8,128)S(1)} %get-tuple-element.24), channel_id=1, source_target_pairs={{32,0},{64,32},{96,64},{128,96},{160,128},{192,160},{224,192},{256... | collective-permute-start | bytes 122888 | tf_op jit(solution)/shard_map/ppermute | solution.py:331
  40.9 13.1 %copy-start.1 = (s32[1024]{0:T(1024)S(1)}, s32[1024]{0:T(1024)}, u32[]{:S(2)}) copy-start(s32[1024]{0:T(1024)} %param.8) | copy-start | bytes 12292
  40.9 13.1 %copy-start.2 = (s32[1024,1]{0,1:T(1,128)S(1)}, s32[1024,1]{0,1:T(1,128)}, u32[]{:S(2)}) copy-start(s32[1024,1]{0,1:T(1,128)} %param.9) | copy-start | bytes 12292
  40.9 13.1 %copy-start.3 = (s32[1024]{0:T(1024)S(1)}, s32[1024]{0:T(1024)}, u32[]{:S(2)}) copy-start(s32[1024]{0:T(1024)} %param.11) | copy-start | bytes 12292
  40.9 13.1 %copy-start.4 = (f32[1024]{0:T(1024)S(1)}, f32[1024]{0:T(1024)}, u32[]{:S(2)}) copy-start(f32[1024]{0:T(1024)} %param.10) | copy-start | bytes 12292

commit v11 on v10

--- a/solution.py
+++ b/solution.py
@@ -12,7 +12,7 @@
 
 ROWS = 1024
 PLANE = ("gy", "gz")
-FIRST_TURN, ALONG_TURN, LAST_TURN = 22, 12, 18
+FIRST_TURN, ALONG_TURN, LAST_TURN = 22, 14, 18
 
 
 def call(kernel, outs, scratch=(), count=1, space=pltpu.VMEM, limit=24 * 1024 * 1024):

time: 56.5 us -> 56.5 us (level)
  waiting for transfers between devices: 4.51 us -> 5.11 us
  transfers between devices with their start and end apart: 6 -> 6, of which waited for: 3 -> 4; matrix products, arithmetic and copies ran while one was open for 0% -> 0% of each run, Pallas kernels for 1% -> 1%
where the time goes in v11:
time: 56.5 us; the launch traced here: 56.1 us
  starting transfers between devices  32.1 us (57%)
  blocking collectives  12.8 us (23%)
  Pallas kernels  5.27 us (9%)
  waiting for transfers between devices  5.11 us (9%)
  between operations  0.77 us (1%)
    all_to_all x2, starting transfers between devices, exchange(): lax.all_to_all(blocks, axes, split_axis=0, concat_axis=0, tiled=True, axi...  25.1 us
    all_to_all x1, blocking collectives, exchange(): lax.all_to_all(blocks, axes, split_axis=0, concat_axis=0, tiled=True, axi...  12.8 us
    ppermute x4, starting transfers between devices, shift(): return (lax.ppermute(up, axis, forward), lax.ppermute(down, axis, backward))  7.01 us
    ppermute x4, waiting for transfers between devices, shift(): return (lax.ppermute(up, axis, forward), lax.ppermute(down, axis, backward))  4.56 us
    pallas_call x1, Pallas kernels, body(): call(sample_kernel, (f32(32, 8, 128), f32(8, 128), side, side, f32(2, 8,...  2.52 us
    pallas_call x1, Pallas kernels, body(): call(final_kernel, (f32(4, 8, 8, 128), f32(3, 8, 8, 128)), (grid,), 11)  1.73 us
  transfers between devices with their start and end apart: 6, of which 4 were waited for; matrix products, arithmetic and copies ran while one was open for 0% of the time, Pallas kernels for 1%

profile of v11, /device:TPU:1, one launch (start us, length us, event | category | flops | bytes accessed | tf_op | source)
XLA Modules:
  0.0 56.1 jit_solution(7134577717495843125)
XLA Ops:
  0.6 2.5 %shard_map.86 = (f32[32,8,128]{2,1,0:T(8,128)}, f32[8,128]{1,0:T(8,128)}, f32[4,8,2,128]{3,2,1,0:T(2,128)}, f32[4,8,2,128]{3,2,1,0:T(2,128)}, f32[2,8,128]{2,1,0:T(8,128)}) custom-call(f32[4,8,8,128]{3,2,1,0:T(8,128)} %state.3, s32[1,1024]{1,0:T(1,128)} %bitcast.5, s32[1,1024]{1,0:T(1,128)} %bitcast.7, s32[1,1024]{1,0:T(1,128)} %bitcast.9, ...), custom_call_target="tpu_custom_call" | custom-call | flops 2000000 | bytes 1000000 | tf_op jit(solution)/shard_map/pallas_call | solution.py:359
  3.2 0.0 copy-start.8
  3.2 0.0 copy-start.7
  3.2 13.7 %all-to-all-start = ((f32[32,8,128]{2,1,0:T(8,128)}), f32[32,8,128]{2,1,0:T(8,128)S(1)}, u32[]{:S(2)}, u32[]{:S(2)}) async-start(f32[32,8,128]{2,1,0:T(8,128)} %get-tuple-element.16), calls=%async_computation | async-start | bytes 262144 | tf_op jit(solution)/shard_map/all_to_all | solution.py:335
  16.9 0.0 copy-start.6
  16.9 0.0 copy-done.8
  16.9 0.1 collective-permute-start
  17.0 0.0 copy-done.7
  17.0 0.5 collective-permute-start.1
  17.5 1.6 %collective-permute-done.ylo = f32[4,8,2,128]{3,2,1,0:T(2,128)S(1)} collective-permute-done((f32[4,8,2,128]{3,2,1,0:T(2,128)S(1)}, f32[4,8,2,128]{3,2,1,0:T(2,128)S(1)}, u32[]{:S(2)}, u32[]{:S(2)}) %collective-permute-start) | collective-permute-done | bytes 32800 | tf_op jit(solution)/shard_map/ppermute | solution.py:331
  19.1 1.3 %collective-permute-done.1.yhi = f32[4,8,2,128]{3,2,1,0:T(2,128)S(1)} collective-permute-done((f32[4,8,2,128]{3,2,1,0:T(2,128)S(1)}, f32[4,8,2,128]{3,2,1,0:T(2,128)S(1)}, u32[]{:S(2)}, u32[]{:S(2)}) %collective-permute-start.1) | collective-permute-done | bytes 32800 | tf_op jit(solution)/shard_map/ppermute | solution.py:331
  20.3 0.0 all-to-all-done.parts
  20.3 0.0 copy-done.6
  20.3 0.7 %shard_map.87 = f32[16,8,128]{2,1,0:T(8,128)} custom-call(f32[32,8,128]{2,1,0:T(8,128)S(1)} %all-to-all-done.parts, f32[8,128]{1,0:T(8,128)S(1)} %copy-done.6), custom_call_target="tpu_custom_call" | custom-call | flops 2000000 | bytes 1000000 | tf_op jit(solution)/shard_map/pallas_call | solution.py:371
  21.0 11.4 %all-to-all-start.1 = ((f32[16,8,128]{2,1,0:T(8,128)}), f32[16,8,128]{2,1,0:T(8,128)S(1)}, u32[]{:S(2)}, u32[]{:S(2)}) async-start(f32[16,8,128]{2,1,0:T(8,128)} %shard_map.87), calls=%async_computation.1 | async-start | bytes 131072 | tf_op jit(solution)/shard_map/all_to_all | solution.py:335
  32.4 0.0 copy-done
  32.4 0.0 copy-start.5
  32.4 0.3 shard_map.88
  32.7 3.1 %collective-permute-start.2 = (f32[10,8,128]{2,1,0:T(8,128)S(1)}, f32[10,8,128]{2,1,0:T(8,128)S(1)}, u32[]{:S(2)}, u32[]{:S(2)}) collective-permute-start(f32[10,8,128]{2,1,0:T(8,128)S(1)} %get-tuple-element.23), channel_id=1, source_target_pairs={{0,32},{32,64},{64,96},{96,128},{128,160},{160,192},{192,224},{224... | collective-permute-start | bytes 122888 | tf_op jit(solution)/shard_map/ppermute | solution.py:331
  35.8 3.4 %collective-permute-start.3 = (f32[10,8,128]{2,1,0:T(8,128)S(1)}, f32[10,8,128]{2,1,0:T(8,128)S(1)}, u32[]{:S(2)}, u32[]{:S(2)}) collective-permute-start(f32[10,8,128]{2,1,0:T(8,128)S(1)} %get-tuple-element.24), channel_id=1, source_target_pairs={{32,0},{64,32},{96,64},{128,96},{160,128},{192,160},{224,192},{256... | collective-permute-start | bytes 122888 | tf_op jit(solution)/shard_map/ppermute | solution.py:331
  39.2 0.0 collective-permute-done.2.first
  39.2 1.7 %collective-permute-done.3.second = f32[10,8,128]{2,1,0:T(8,128)S(1)} collective-permute-done((f32[10,8,128]{2,1,0:T(8,128)S(1)}, f32[10,8,128]{2,1,0:T(8,128)S(1)}, u32[]{:S(2)}, u32[]{:S(2)}) %collective-permute-start.3) | collective-permute-done | bytes 40992 | tf_op jit(solution)/shard_map/ppermute | solution.py:331
  40.9 0.5 all-to-all-done.1.parts
  41.4 0.0 copy-done.5
  41.5 0.0 copy-start.1
  41.5 0.0 copy-start.2
  41.5 0.0 copy-start.3
  41.5 0.0 copy-start.4
  41.5 12.8 %all_to_all.15.parts = f32[32,8,128]{2,1,0:T(8,128)S(1)} all-to-all(f32[32,8,128]{2,1,0:T(8,128)S(1)} %shard_map.89), channel_id=1, replica_groups={{18,19,16,17,22,23,20,21,26,27,24,25,30,31,28,29,2,3,0,1,6,7,4,5,10,11,..., dimensions={0} | all-to-all | bytes 262144 | tf_op jit(solution)/shard_map/all_to_all | solution.py:335
  54.3 0.0 copy-done.1
  54.3 0.0 copy-done.2
  54.3 1.7 %shard_map.90 = (f32[4,8,8,128]{3,2,1,0:T(8,128)}, f32[3,8,8,128]{3,2,1,0:T(8,128)}) custom-call(f32[32,8,128]{2,1,0:T(8,128)S(1)} %all_to_all.15.parts, s32[1,1024]{1,0:T(1,128)S(1)} %bitcast.6, s32[1,1024]{1,0:T(1,128)S(1)} %bitcast.8, s32[1,1024]{1,0:T(1,128)S(1)} %bitcast.10, f32[1,1024]{1,0:T(1,128)S(1)} %bitcast.12, f32[4,8,8,128]{3,2,1,0:T(8,128)S(1)} %copy-done, ...), custom_call_target="tpu_custom_call" | custom-call | flops 2000000 | bytes 1000000 | tf_op jit(solution)/shard_map/pallas_call | solution.py:383
  (4 shorter events, 0.0 us)
Async XLA Ops:
  3.2 13.8 %copy-start.8 = (f32[4,8,2,128]{3,2,1,0:T(2,128)S(1)}, f32[4,8,2,128]{3,2,1,0:T(2,128)}, u32[]{:S(2)}) copy-start(f32[4,8,2,128]{3,2,1,0:T(2,128)} %get-tuple-element.17) | copy-start | bytes 98308
  3.2 13.8 %copy-start.7 = (f32[4,8,2,128]{3,2,1,0:T(2,128)S(1)}, f32[4,8,2,128]{3,2,1,0:T(2,128)}, u32[]{:S(2)}) copy-start(f32[4,8,2,128]{3,2,1,0:T(2,128)} %get-tuple-element.18) | copy-start | bytes 98308
  3.2 17.2 %all-to-all-start = ((f32[32,8,128]{2,1,0:T(8,128)}), f32[32,8,128]{2,1,0:T(8,128)S(1)}, u32[]{:S(2)}, u32[]{:S(2)}) async-start(f32[32,8,128]{2,1,0:T(8,128)} %get-tuple-element.16), calls=%async_computation | async-start | bytes 262144 | tf_op jit(solution)/shard_map/all_to_all | solution.py:335
  16.9 3.4 %copy-start.6 = (f32[8,128]{1,0:T(8,128)S(1)}, f32[8,128]{1,0:T(8,128)}, u32[]{:S(2)}) copy-start(f32[8,128]{1,0:T(8,128)} %get-tuple-element.20.own) | copy-start | bytes 12292
  16.9 2.1 %collective-permute-start = (f32[4,8,2,128]{3,2,1,0:T(2,128)S(1)}, f32[4,8,2,128]{3,2,1,0:T(2,128)S(1)}, u32[]{:S(2)}, u32[]{:S(2)}) collective-permute-start(f32[4,8,2,128]{3,2,1,0:T(2,128)S(1)} %copy-done.8), channel_id=1, source_target_pairs={{0,4},{4,8},{8,12},{12,16},{16,20},{20,24},{24,28},{28,0},{1,5},{5... | collective-permute-start | bytes 98312 | tf_op jit(solution)/shard_map/ppermute | solution.py:331
  17.0 3.3 %collective-permute-start.1 = (f32[4,8,2,128]{3,2,1,0:T(2,128)S(1)}, f32[4,8,2,128]{3,2,1,0:T(2,128)S(1)}, u32[]{:S(2)}, u32[]{:S(2)}) collective-permute-start(f32[4,8,2,128]{3,2,1,0:T(2,128)S(1)} %copy-done.7), channel_id=1, source_target_pairs={{4,0},{8,4},{12,8},{16,12},{20,16},{24,20},{28,24},{0,28},{5,1},{9... | collective-permute-start | bytes 98312 | tf_op jit(solution)/shard_map/ppermute | solution.py:331
  20.3 12.1 %copy-start = (f32[4,8,8,128]{3,2,1,0:T(8,128)S(1)}, f32[4,8,8,128]{3,2,1,0:T(8,128)}, u32[]{:S(2)}) copy-start(f32[4,8,8,128]{3,2,1,0:T(8,128)} %state.3) | copy-start | bytes 393220
  21.0 20.4 %all-to-all-start.1 = ((f32[16,8,128]{2,1,0:T(8,128)}), f32[16,8,128]{2,1,0:T(8,128)S(1)}, u32[]{:S(2)}, u32[]{:S(2)}) async-start(f32[16,8,128]{2,1,0:T(8,128)} %shard_map.87), calls=%async_computation.1 | async-start | bytes 131072 | tf_op jit(solution)/shard_map/all_to_all | solution.py:335
  32.4 9.1 %copy-start.5 = (f32[2,8,128]{2,1,0:T(8,128)S(1)}, f32[2,8,128]{2,1,0:T(8,128)}, u32[]{:S(2)}) copy-start(f32[2,8,128]{2,1,0:T(8,128)} %get-tuple-element.26.far) | copy-start | bytes 24580
  32.7 6.5 %collective-permute-start.2 = (f32[10,8,128]{2,1,0:T(8,128)S(1)}, f32[10,8,128]{2,1,0:T(8,128)S(1)}, u32[]{:S(2)}, u32[]{:S(2)}) collective-permute-start(f32[10,8,128]{2,1,0:T(8,128)S(1)} %get-tuple-element.23), channel_id=1, source_target_pairs={{0,32},{32,64},{64,96},{96,128},{128,160},{160,192},{192,224},{224... | collective-permute-start | bytes 122888 | tf_op jit(solution)/shard_map/ppermute | solution.py:331
  35.8 5.1 %collective-permute-start.3 = (f32[10,8,128]{2,1,0:T(8,128)S(1)}, f32[10,8,128]{2,1,0:T(8,128)S(1)}, u32[]{:S(2)}, u32[]{:S(2)}) collective-permute-start(f32[10,8,128]{2,1,0:T(8,128)S(1)} %get-tuple-element.24), channel_id=1, source_target_pairs={{32,0},{64,32},{96,64},{128,96},{160,128},{192,160},{224,192},{256... | collective-permute-start | bytes 122888 | tf_op jit(solution)/shard_map/ppermute | solution.py:331
  41.5 12.8 %copy-start.1 = (s32[1024]{0:T(1024)S(1)}, s32[1024]{0:T(1024)}, u32[]{:S(2)}) copy-start(s32[1024]{0:T(1024)} %param.8) | copy-start | bytes 12292
  41.5 12.8 %copy-start.2 = (s32[1024,1]{0,1:T(1,128)S(1)}, s32[1024,1]{0,1:T(1,128)}, u32[]{:S(2)}) copy-start(s32[1024,1]{0,1:T(1,128)} %param.9) | copy-start | bytes 12292
  41.5 12.8 %copy-start.3 = (s32[1024]{0:T(1024)S(1)}, s32[1024]{0:T(1024)}, u32[]{:S(2)}) copy-start(s32[1024]{0:T(1024)} %param.11) | copy-start | bytes 12292
  41.5 12.8 %copy-start.4 = (f32[1024]{0:T(1024)S(1)}, f32[1024]{0:T(1024)}, u32[]{:S(2)}) copy-start(f32[1024]{0:T(1024)} %param.10) | copy-start | bytes 12292

commit v12 on v11

--- a/solution.py
+++ b/solution.py
@@ -248,13 +248,10 @@
     ghosts[:, :, 0:8] = inner
     ghosts[:, :, 8:16] = give_lanes(edges, (0, 127)).reshape(4, 8, 8, 128)
 
-    column = lax.broadcasted_iota(jnp.int32, (8, 128), 1)
-    outer = (column == 0) | (column == 127)
-
     def slab(x, near):
         tiles = [state[c, x + i] for c in range(4) for i in range(2)]
         across = [part[c, near, i : i + 1] for c in range(4) for part, i in ((yhi, 0), (ylo, 1))]
-        ends = [jnp.where(outer, inner[c, near], 0.0) for c in range(4)]
+        ends = [inner[c, near] for c in range(4)]
         ends = [ends[0]] + [pltpu.roll(ends[c], 2 * c, 1) for c in range(1, 4)]
         return tiles + [jnp.concatenate(across, axis=0), ends[0] + ends[1] + ends[2] + ends[3]]
 

time: 56.5 us -> 56.5 us (level)
  no operation moved by 1% of the time
where the time goes in v12:
time: 56.5 us; the launch traced here: 56.1 us
  starting transfers between devices  32.1 us (57%)
  blocking collectives  12.8 us (23%)
  Pallas kernels  5.27 us (9%)
  waiting for transfers between devices  5.11 us (9%)
  between operations  0.77 us (1%)
    all_to_all x2, starting transfers between devices, exchange(): lax.all_to_all(blocks, axes, split_axis=0, concat_axis=0, tiled=True, axi...  25.1 us
    all_to_all x1, blocking collectives, exchange(): lax.all_to_all(blocks, axes, split_axis=0, concat_axis=0, tiled=True, axi...  12.8 us
    ppermute x4, starting transfers between devices, shift(): return (lax.ppermute(up, axis, forward), lax.ppermute(down, axis, backward))  7.01 us
    ppermute x4, waiting for transfers between devices, shift(): return (lax.ppermute(up, axis, forward), lax.ppermute(down, axis, backward))  4.56 us
    pallas_call x1, Pallas kernels, body(): call(sample_kernel, (f32(32, 8, 128), f32(8, 128), side, side, f32(2, 8,...  2.52 us
    pallas_call x1, Pallas kernels, body(): call(final_kernel, (f32(4, 8, 8, 128), f32(3, 8, 8, 128)), (grid,), 11)  1.73 us
  transfers between devices with their start and end apart: 6, of which 4 were waited for; matrix products, arithmetic and copies ran while one was open for 0% of the time, Pallas kernels for 1%

profile of v12, /device:TPU:1, one launch (start us, length us, event | category | flops | bytes accessed | tf_op | source)
XLA Modules:
  0.0 56.1 jit_solution(5780166574637926889)
XLA Ops:
  0.6 2.5 %shard_map.86 = (f32[32,8,128]{2,1,0:T(8,128)}, f32[8,128]{1,0:T(8,128)}, f32[4,8,2,128]{3,2,1,0:T(2,128)}, f32[4,8,2,128]{3,2,1,0:T(2,128)}, f32[2,8,128]{2,1,0:T(8,128)}) custom-call(f32[4,8,8,128]{3,2,1,0:T(8,128)} %state.3, s32[1,1024]{1,0:T(1,128)} %bitcast.5, s32[1,1024]{1,0:T(1,128)} %bitcast.7, s32[1,1024]{1,0:T(1,128)} %bitcast.9, ...), custom_call_target="tpu_custom_call" | custom-call | flops 2000000 | bytes 1000000 | tf_op jit(solution)/shard_map/pallas_call | solution.py:356
  3.2 0.0 copy-start.8
  3.2 0.0 copy-start.7
  3.2 13.7 %all-to-all-start = ((f32[32,8,128]{2,1,0:T(8,128)}), f32[32,8,128]{2,1,0:T(8,128)S(1)}, u32[]{:S(2)}, u32[]{:S(2)}) async-start(f32[32,8,128]{2,1,0:T(8,128)} %get-tuple-element.16), calls=%async_computation | async-start | bytes 262144 | tf_op jit(solution)/shard_map/all_to_all | solution.py:332
  16.9 0.0 copy-start.6
  16.9 0.0 copy-done.8
  16.9 0.1 collective-permute-start
  17.0 0.0 copy-done.7
  17.0 0.5 collective-permute-start.1
  17.5 1.6 %collective-permute-done.ylo = f32[4,8,2,128]{3,2,1,0:T(2,128)S(1)} collective-permute-done((f32[4,8,2,128]{3,2,1,0:T(2,128)S(1)}, f32[4,8,2,128]{3,2,1,0:T(2,128)S(1)}, u32[]{:S(2)}, u32[]{:S(2)}) %collective-permute-start) | collective-permute-done | bytes 32800 | tf_op jit(solution)/shard_map/ppermute | solution.py:328
  19.1 1.3 %collective-permute-done.1.yhi = f32[4,8,2,128]{3,2,1,0:T(2,128)S(1)} collective-permute-done((f32[4,8,2,128]{3,2,1,0:T(2,128)S(1)}, f32[4,8,2,128]{3,2,1,0:T(2,128)S(1)}, u32[]{:S(2)}, u32[]{:S(2)}) %collective-permute-start.1) | collective-permute-done | bytes 32800 | tf_op jit(solution)/shard_map/ppermute | solution.py:328
  20.3 0.0 all-to-all-done.parts
  20.3 0.0 copy-done.6
  20.3 0.7 %shard_map.87 = f32[16,8,128]{2,1,0:T(8,128)} custom-call(f32[32,8,128]{2,1,0:T(8,128)S(1)} %all-to-all-done.parts, f32[8,128]{1,0:T(8,128)S(1)} %copy-done.6), custom_call_target="tpu_custom_call" | custom-call | flops 2000000 | bytes 1000000 | tf_op jit(solution)/shard_map/pallas_call | solution.py:368
  21.0 11.4 %all-to-all-start.1 = ((f32[16,8,128]{2,1,0:T(8,128)}), f32[16,8,128]{2,1,0:T(8,128)S(1)}, u32[]{:S(2)}, u32[]{:S(2)}) async-start(f32[16,8,128]{2,1,0:T(8,128)} %shard_map.87), calls=%async_computation.1 | async-start | bytes 131072 | tf_op jit(solution)/shard_map/all_to_all | solution.py:332
  32.4 0.0 copy-done
  32.4 0.0 copy-start.5
  32.4 0.3 shard_map.88
  32.7 3.1 %collective-permute-start.2 = (f32[10,8,128]{2,1,0:T(8,128)S(1)}, f32[10,8,128]{2,1,0:T(8,128)S(1)}, u32[]{:S(2)}, u32[]{:S(2)}) collective-permute-start(f32[10,8,128]{2,1,0:T(8,128)S(1)} %get-tuple-element.23), channel_id=1, source_target_pairs={{0,32},{32,64},{64,96},{96,128},{128,160},{160,192},{192,224},{224... | collective-permute-start | bytes 122888 | tf_op jit(solution)/shard_map/ppermute | solution.py:328
  35.8 3.4 %collective-permute-start.3 = (f32[10,8,128]{2,1,0:T(8,128)S(1)}, f32[10,8,128]{2,1,0:T(8,128)S(1)}, u32[]{:S(2)}, u32[]{:S(2)}) collective-permute-start(f32[10,8,128]{2,1,0:T(8,128)S(1)} %get-tuple-element.24), channel_id=1, source_target_pairs={{32,0},{64,32},{96,64},{128,96},{160,128},{192,160},{224,192},{256... | collective-permute-start | bytes 122888 | tf_op jit(solution)/shard_map/ppermute | solution.py:328
  39.2 0.0 collective-permute-done.2.first
  39.2 1.7 %collective-permute-done.3.second = f32[10,8,128]{2,1,0:T(8,128)S(1)} collective-permute-done((f32[10,8,128]{2,1,0:T(8,128)S(1)}, f32[10,8,128]{2,1,0:T(8,128)S(1)}, u32[]{:S(2)}, u32[]{:S(2)}) %collective-permute-start.3) | collective-permute-done | bytes 40992 | tf_op jit(solution)/shard_map/ppermute | solution.py:328
  40.9 0.5 all-to-all-done.1.parts
  41.4 0.0 copy-done.5
  41.5 0.0 copy-start.1
  41.5 0.0 copy-start.2
  41.5 0.0 copy-start.3
  41.5 0.0 copy-start.4
  41.5 12.8 %all_to_all.15.parts = f32[32,8,128]{2,1,0:T(8,128)S(1)} all-to-all(f32[32,8,128]{2,1,0:T(8,128)S(1)} %shard_map.89), channel_id=1, replica_groups={{18,19,16,17,22,23,20,21,26,27,24,25,30,31,28,29,2,3,0,1,6,7,4,5,10,11,..., dimensions={0} | all-to-all | bytes 262144 | tf_op jit(solution)/shard_map/all_to_all | solution.py:332
  54.3 0.0 copy-done.1
  54.3 0.0 copy-done.2
  54.3 1.7 %shard_map.90 = (f32[4,8,8,128]{3,2,1,0:T(8,128)}, f32[3,8,8,128]{3,2,1,0:T(8,128)}) custom-call(f32[32,8,128]{2,1,0:T(8,128)S(1)} %all_to_all.15.parts, s32[1,1024]{1,0:T(1,128)S(1)} %bitcast.6, s32[1,1024]{1,0:T(1,128)S(1)} %bitcast.8, s32[1,1024]{1,0:T(1,128)S(1)} %bitcast.10, f32[1,1024]{1,0:T(1,128)S(1)} %bitcast.12, f32[4,8,8,128]{3,2,1,0:T(8,128)S(1)} %copy-done, ...), custom_call_target="tpu_custom_call" | custom-call | flops 2000000 | bytes 1000000 | tf_op jit(solution)/shard_map/pallas_call | solution.py:380
  (4 shorter events, 0.0 us)
Async XLA Ops:
  3.2 13.8 %copy-start.8 = (f32[4,8,2,128]{3,2,1,0:T(2,128)S(1)}, f32[4,8,2,128]{3,2,1,0:T(2,128)}, u32[]{:S(2)}) copy-start(f32[4,8,2,128]{3,2,1,0:T(2,128)} %get-tuple-element.17) | copy-start | bytes 98308
  3.2 13.8 %copy-start.7 = (f32[4,8,2,128]{3,2,1,0:T(2,128)S(1)}, f32[4,8,2,128]{3,2,1,0:T(2,128)}, u32[]{:S(2)}) copy-start(f32[4,8,2,128]{3,2,1,0:T(2,128)} %get-tuple-element.18) | copy-start | bytes 98308
  3.2 17.2 %all-to-all-start = ((f32[32,8,128]{2,1,0:T(8,128)}), f32[32,8,128]{2,1,0:T(8,128)S(1)}, u32[]{:S(2)}, u32[]{:S(2)}) async-start(f32[32,8,128]{2,1,0:T(8,128)} %get-tuple-element.16), calls=%async_computation | async-start | bytes 262144 | tf_op jit(solution)/shard_map/all_to_all | solution.py:332
  16.9 3.4 %copy-start.6 = (f32[8,128]{1,0:T(8,128)S(1)}, f32[8,128]{1,0:T(8,128)}, u32[]{:S(2)}) copy-start(f32[8,128]{1,0:T(8,128)} %get-tuple-element.20.own) | copy-start | bytes 12292
  16.9 2.1 %collective-permute-start = (f32[4,8,2,128]{3,2,1,0:T(2,128)S(1)}, f32[4,8,2,128]{3,2,1,0:T(2,128)S(1)}, u32[]{:S(2)}, u32[]{:S(2)}) collective-permute-start(f32[4,8,2,128]{3,2,1,0:T(2,128)S(1)} %copy-done.8), channel_id=1, source_target_pairs={{0,4},{4,8},{8,12},{12,16},{16,20},{20,24},{24,28},{28,0},{1,5},{5... | collective-permute-start | bytes 98312 | tf_op jit(solution)/shard_map/ppermute | solution.py:328
  17.0 3.3 %collective-permute-start.1 = (f32[4,8,2,128]{3,2,1,0:T(2,128)S(1)}, f32[4,8,2,128]{3,2,1,0:T(2,128)S(1)}, u32[]{:S(2)}, u32[]{:S(2)}) collective-permute-start(f32[4,8,2,128]{3,2,1,0:T(2,128)S(1)} %copy-done.7), channel_id=1, source_target_pairs={{4,0},{8,4},{12,8},{16,12},{20,16},{24,20},{28,24},{0,28},{5,1},{9... | collective-permute-start | bytes 98312 | tf_op jit(solution)/shard_map/ppermute | solution.py:328
  20.3 12.1 %copy-start = (f32[4,8,8,128]{3,2,1,0:T(8,128)S(1)}, f32[4,8,8,128]{3,2,1,0:T(8,128)}, u32[]{:S(2)}) copy-start(f32[4,8,8,128]{3,2,1,0:T(8,128)} %state.3) | copy-start | bytes 393220
  21.0 20.4 %all-to-all-start.1 = ((f32[16,8,128]{2,1,0:T(8,128)}), f32[16,8,128]{2,1,0:T(8,128)S(1)}, u32[]{:S(2)}, u32[]{:S(2)}) async-start(f32[16,8,128]{2,1,0:T(8,128)} %shard_map.87), calls=%async_computation.1 | async-start | bytes 131072 | tf_op jit(solution)/shard_map/all_to_all | solution.py:332
  32.4 9.1 %copy-start.5 = (f32[2,8,128]{2,1,0:T(8,128)S(1)}, f32[2,8,128]{2,1,0:T(8,128)}, u32[]{:S(2)}) copy-start(f32[2,8,128]{2,1,0:T(8,128)} %get-tuple-element.26.far) | copy-start | bytes 24580
  32.7 6.5 %collective-permute-start.2 = (f32[10,8,128]{2,1,0:T(8,128)S(1)}, f32[10,8,128]{2,1,0:T(8,128)S(1)}, u32[]{:S(2)}, u32[]{:S(2)}) collective-permute-start(f32[10,8,128]{2,1,0:T(8,128)S(1)} %get-tuple-element.23), channel_id=1, source_target_pairs={{0,32},{32,64},{64,96},{96,128},{128,160},{160,192},{192,224},{224... | collective-permute-start | bytes 122888 | tf_op jit(solution)/shard_map/ppermute | solution.py:328
  35.8 5.1 %collective-permute-start.3 = (f32[10,8,128]{2,1,0:T(8,128)S(1)}, f32[10,8,128]{2,1,0:T(8,128)S(1)}, u32[]{:S(2)}, u32[]{:S(2)}) collective-permute-start(f32[10,8,128]{2,1,0:T(8,128)S(1)} %get-tuple-element.24), channel_id=1, source_target_pairs={{32,0},{64,32},{96,64},{128,96},{160,128},{192,160},{224,192},{256... | collective-permute-start | bytes 122888 | tf_op jit(solution)/shard_map/ppermute | solution.py:328
  41.5 12.8 %copy-start.1 = (s32[1024]{0:T(1024)S(1)}, s32[1024]{0:T(1024)}, u32[]{:S(2)}) copy-start(s32[1024]{0:T(1024)} %param.8) | copy-start | bytes 12292
  41.5 12.8 %copy-start.2 = (s32[1024,1]{0,1:T(1,128)S(1)}, s32[1024,1]{0,1:T(1,128)}, u32[]{:S(2)}) copy-start(s32[1024,1]{0,1:T(1,128)} %param.9) | copy-start | bytes 12292
  41.5 12.8 %copy-start.3 = (s32[1024]{0:T(1024)S(1)}, s32[1024]{0:T(1024)}, u32[]{:S(2)}) copy-start(s32[1024]{0:T(1024)} %param.11) | copy-start | bytes 12292
  41.5 12.8 %copy-start.4 = (f32[1024]{0:T(1024)S(1)}, f32[1024]{0:T(1024)}, u32[]{:S(2)}) copy-start(f32[1024]{0:T(1024)} %param.10) | copy-start | bytes 12292
